TPU v7x, 32 devices: a whole 2x2x4 slice. The times are simulated.
32 devices in a mesh: seq: 16 (over z, y, core), row: 2 (over x).
Axes of the slice: x: 2, y: 2, z: 4, core: 2. Of those that a mesh axis runs over, the one named last changes fastest.
Arguments:
- inputs: bfloat16 [2, 32768, 768], P('row', 'seq'), may hold values from -6 to 6
- w_query: bfloat16 [768, 768], replicated, may hold values from -0.21875 to 0.21875
- w_key: bfloat16 [768, 768], replicated, may hold values from -0.21875 to 0.21875
- w_value: bfloat16 [768, 768], replicated, may hold values from -0.21875 to 0.21875
- w_out: bfloat16 [768, 768], replicated, may hold values from -3 to 3
- w_up: bfloat16 [768, 3072], replicated, may hold values from -0.21875 to 0.21875
- w_down: bfloat16 [3072, 768], replicated, may hold values from -0.109375 to 0.109375
- b_query: bfloat16 [768], replicated, may hold values from -3 to 3
- b_key: bfloat16 [768], replicated, may hold values from -3 to 3
- b_value: bfloat16 [768], replicated, may hold values from -3 to 3
- b_out: bfloat16 [768], replicated, may hold values from -3 to 3
- b_up: bfloat16 [3072], replicated, may hold values from -3 to 3
- b_down: bfloat16 [768], replicated, may hold values from -3 to 3
- norm1_gain: bfloat16 [768], replicated, may hold values from 0.5 to 1.5
- norm1_shift: bfloat16 [768], replicated, may hold values from -3 to 3
- norm2_gain: bfloat16 [768], replicated, may hold values from 0.5 to 1.5
- norm2_shift: bfloat16 [768], replicated, may hold values from -3 to 3
- head_feature_directions: bfloat16 [12, 256, 64], replicated, may hold values from -4 to 4
- seq_lengths: int32 [2, 6], P('row'), may hold values from 1024 to 20480, as said below
- seq_starts: int32 [2, 6], P('row'), may hold values from 0 to 30720, as said below
- cotangent: bfloat16 [2, 32768, 768], P('row', 'seq'), may hold values from -6 to 6
Outputs:
- layer_out: float32 [2, 32768, 768], P('row', 'seq')
- input_grad: float32 [2, 32768, 768], P('row', 'seq')
- grad_w_query: float32 [768, 768], replicated
- grad_w_key: float32 [768, 768], replicated
- grad_w_value: float32 [768, 768], replicated
- grad_w_out: float32 [768, 768], replicated
- grad_w_up: float32 [768, 3072], replicated
- grad_w_down: float32 [3072, 768], replicated
- grad_b_query: float32 [768], replicated
- grad_b_key: float32 [768], replicated
- grad_b_value: float32 [768], replicated
- grad_b_out: float32 [768], replicated
- grad_b_up: float32 [3072], replicated
- grad_b_down: float32 [768], replicated
- grad_norm1_gain: float32 [768], replicated
- grad_norm1_shift: float32 [768], replicated
- grad_norm2_gain: float32 [768], replicated
- grad_norm2_shift: float32 [768], replicated
Inputs may be any that keep to these rules, and one draw needn't show every extreme that they name: Each row is split into six buckets laid end to end in an order that differs from row to row. The first bucket holds 20480 token places, the second holds 4096, and each of the last four holds 2048; seq_starts gives each bucket's first place in its row. The sequence of a bucket occupies the first seq_lengths places of that bucket; the rest is padding. The first bucket is always full; every other bucket holds at least its capacity minus 2048 // 2 tokens.
All inputs are finite; a program needn't handle non-finite values.
Results may differ from a plain program's by a relative error of at most 0.04.
Values sent between devices are 32-bit elements; how exact they have to be, the bound alone decides.
No kernel may reach another device: no remote copies, remote signals or barrier semaphores. Data moves between devices by JAX's collectives and lax.ppermute only.
A program may use at most 384 MiB of HBM per device.

v0:
```python
import math

import jax
import jax.numpy as jnp
from jax import lax
from jax.sharding import PartitionSpec as P

EPSILON = 1e-05


def norm_layer(hidden, gain_vec, offset_vec):
    centre = hidden - jnp.mean(hidden, axis=-1, keepdims=True)
    spread = jnp.mean(centre * centre, axis=-1, keepdims=True)
    return centre * lax.rsqrt(spread + EPSILON) * gain_vec + offset_vec


def positive_features(raw_logits, rounded_values, norm_weight, prefactor):
    widened = rounded_values.astype(jnp.float32)
    square = jnp.sum(widened * widened, axis=-1, keepdims=True)
    return jnp.exp(raw_logits - square * norm_weight) * prefactor


def feature_logits(rounded_values, head_feature_directions, feature_scale):
    return feature_scale * jnp.einsum(
        "nlr,lur->nlu", rounded_values, head_feature_directions, preferred_element_type=jnp.float32
    )


def feature_back(
    feat_grad, feat_value, rounded_values, head_feature_directions, feature_scale, norm_weight
):
    logit_grad = feat_grad * feat_value
    through = feature_scale * jnp.einsum(
        "pez,ezi->pei",
        logit_grad.astype(jnp.bfloat16),
        head_feature_directions,
        preferred_element_type=jnp.float32,
    )
    return through - 2.0 * norm_weight * jnp.sum(
        logit_grad, axis=-1, keepdims=True
    ) * rounded_values.astype(jnp.float32)


def pick_bucket(onehot, summed):
    return jnp.sum(onehot.reshape((-1,) + (1,) * (summed.ndim - 1)) * summed, axis=0)


def spread_bucket(onehot, local_part):
    return onehot.reshape((-1,) + (1,) * local_part.ndim) * local_part[None]


def on_device(
    inputs,
    w_query,
    w_key,
    w_value,
    w_out,
    w_up,
    w_down,
    b_query,
    b_key,
    b_value,
    b_out,
    b_up,
    b_down,
    norm1_gain,
    norm1_shift,
    norm2_gain,
    norm2_shift,
    head_feature_directions,
    seq_lengths,
    seq_starts,
    cotangent,
):
    tokens = inputs.shape[1]
    model_width = inputs.shape[2]
    head_count, feature_rows, head_dim = head_feature_directions.shape
    feature_scale = head_dim ** (-0.25)
    norm_weight = 0.5 / math.sqrt(head_dim)
    prefactor = 1.0 / math.sqrt(feature_rows)
    blocks = lax.axis_size("seq")
    position = lax.axis_index("seq")
    group_limit = jnp.array([5 * blocks // 8, blocks // 8] + [blocks // 16] * 4, jnp.int32) * tokens
    openings = seq_starts[0]
    lengths_row = seq_lengths[0]
    block_start = position * tokens
    member = (openings <= block_start) & (block_start < openings + group_limit)
    placement = block_start + jnp.arange(tokens, dtype=jnp.int32)[:, None] - openings[None, :]
    live_token_mask = jnp.sum(
        jnp.where(member[None, :] & (placement < lengths_row[None, :]), 1.0, 0.0), axis=1
    ).astype(jnp.float32)
    onehot = member.astype(jnp.float32)
    tokens_in = inputs[0]

    def project(weight, bias):
        return jnp.dot(tokens_in, weight, preferred_element_type=jnp.float32) + bias.astype(
            jnp.float32
        )

    queries = project(w_query, b_query).astype(jnp.bfloat16).reshape(tokens, head_count, head_dim)
    keys_in = project(w_key, b_key).astype(jnp.bfloat16).reshape(tokens, head_count, head_dim)
    input_values = (
        project(w_value, b_value).astype(jnp.bfloat16).reshape(tokens, head_count, head_dim)
    )
    query_feat = positive_features(
        feature_logits(queries, head_feature_directions, feature_scale),
        queries,
        norm_weight,
        prefactor,
    )
    key_features = positive_features(
        feature_logits(keys_in, head_feature_directions, feature_scale),
        keys_in,
        norm_weight,
        prefactor,
    )
    query_reduced = query_feat.astype(jnp.bfloat16)
    query_wide = query_reduced.astype(jnp.float32)
    key_reduced = (
        key_features.astype(jnp.bfloat16) * live_token_mask.astype(jnp.bfloat16)[:, None, None]
    )
    summary_part = jnp.einsum(
        "uzl,uzy->zly", key_reduced, input_values, preferred_element_type=jnp.float32
    )
    normaliser_part = jnp.sum(key_reduced.astype(jnp.float32), axis=0)
    summed = lax.psum(
        (spread_bucket(onehot, summary_part), spread_bucket(onehot, normaliser_part)), "seq"
    )
    key_value_summary = pick_bucket(onehot, summed[0])
    normaliser = pick_bucket(onehot, summed[1])
    summary_reduced = key_value_summary.astype(jnp.bfloat16)
    attention_numerator = jnp.einsum(
        "pez,ezi->pei", query_reduced, summary_reduced, preferred_element_type=jnp.float32
    )
    denominator = jnp.einsum("thm,hm->th", query_wide, normaliser, precision=lax.Precision.HIGHEST)
    mixture = (
        (attention_numerator / denominator[:, :, None])
        .astype(jnp.bfloat16)
        .reshape(tokens, model_width)
    )
    branch = jnp.dot(mixture, w_out, preferred_element_type=jnp.float32) + b_out.astype(jnp.float32)
    residual = tokens_in.astype(jnp.float32) + branch
    normed1, first_pull = jax.vjp(
        norm_layer, residual, norm1_gain.astype(jnp.float32), norm1_shift.astype(jnp.float32)
    )
    normed_low = normed1.astype(jnp.bfloat16)
    pre_act = jnp.dot(normed_low, w_up, preferred_element_type=jnp.float32) + b_up.astype(
        jnp.float32
    )
    activation, gelu_pull = jax.vjp(jax.nn.gelu, pre_act)
    activation_low = activation.astype(jnp.bfloat16)
    feed_out = jnp.dot(activation_low, w_down, preferred_element_type=jnp.float32) + b_down.astype(
        jnp.float32
    )
    result, second_pull = jax.vjp(
        norm_layer,
        normed1 + feed_out,
        norm2_gain.astype(jnp.float32),
        norm2_shift.astype(jnp.float32),
    )
    seed_grad = cotangent[0].astype(jnp.float32)
    second_grad, gain2_grad, shift2_grad = second_pull(seed_grad)
    feed_grad = second_grad.astype(jnp.bfloat16)
    grad_down = jnp.einsum(
        "tf,td->fd", activation_low, feed_grad, preferred_element_type=jnp.float32
    )
    grad_bdown = jnp.sum(feed_grad.astype(jnp.float32), axis=0)
    active_grad = jnp.einsum("td,fd->tf", feed_grad, w_down, preferred_element_type=jnp.float32)
    pre_grad = gelu_pull(active_grad)[0].astype(jnp.bfloat16)
    grad_up = jnp.einsum("td,tf->df", normed_low, pre_grad, preferred_element_type=jnp.float32)
    grad_bup = jnp.sum(pre_grad.astype(jnp.float32), axis=0)
    normed_grad = second_grad + jnp.einsum(
        "tf,df->td", pre_grad, w_up, preferred_element_type=jnp.float32
    )
    residual_grad, gain1_grad, shift1_grad = first_pull(normed_grad)
    branch_grad = residual_grad.astype(jnp.bfloat16)
    grad_out = jnp.einsum("tk,td->kd", mixture, branch_grad, preferred_element_type=jnp.float32)
    grad_bout = jnp.sum(branch_grad.astype(jnp.float32), axis=0)
    attended_grad = jnp.einsum(
        "td,kd->tk", branch_grad, w_out, preferred_element_type=jnp.float32
    ).reshape(tokens, head_count, head_dim)
    numerator_gradient = (attended_grad / denominator[:, :, None]).astype(jnp.bfloat16)
    denominator_grad = -jnp.sum(attended_grad * attention_numerator, axis=-1) / (
        denominator * denominator
    )
    qfeat_grad = (
        jnp.einsum(
            "nlr,lur->nlu", numerator_gradient, summary_reduced, preferred_element_type=jnp.float32
        )
        + denominator_grad[:, :, None] * normaliser[None]
    )
    summary_grad_part = jnp.einsum(
        "uzl,uzy->zly", query_reduced, numerator_gradient, preferred_element_type=jnp.float32
    )
    normaliser_grad_part = jnp.einsum(
        "thm,th->hm", query_wide, denominator_grad, precision=lax.Precision.HIGHEST
    )
    summed_grad = lax.psum(
        (spread_bucket(onehot, summary_grad_part), spread_bucket(onehot, normaliser_grad_part)),
        "seq",
    )
    summary_grad = pick_bucket(onehot, summed_grad[0])
    normaliser_grad = pick_bucket(onehot, summed_grad[1])
    summary_gradient_reduced = summary_grad.astype(jnp.bfloat16)
    kfeat_grad = (
        jnp.einsum(
            "nlr,lur->nlu",
            input_values,
            summary_gradient_reduced,
            preferred_element_type=jnp.float32,
        )
        + normaliser_grad[None]
    ) * live_token_mask[:, None, None]
    value_grad = (
        jnp.einsum(
            "pez,ezi->pei",
            key_reduced,
            summary_gradient_reduced,
            preferred_element_type=jnp.float32,
        )
        .astype(jnp.bfloat16)
        .reshape(tokens, model_width)
    )
    query_grad = (
        feature_back(
            qfeat_grad, query_feat, queries, head_feature_directions, feature_scale, norm_weight
        )
        .astype(jnp.bfloat16)
        .reshape(tokens, model_width)
    )
    key_grad = (
        feature_back(
            kfeat_grad, key_features, keys_in, head_feature_directions, feature_scale, norm_weight
        )
        .astype(jnp.bfloat16)
        .reshape(tokens, model_width)
    )

    def weight_grad(token_grad):
        return jnp.einsum("td,tk->dk", tokens_in, token_grad, preferred_element_type=jnp.float32)

    def back_through(token_grad, weight):
        return jnp.einsum("tk,dk->td", token_grad, weight, preferred_element_type=jnp.float32)

    input_grad = (
        residual_grad
        + back_through(query_grad, w_query)
        + back_through(key_grad, w_key)
        + back_through(value_grad, w_value)
    )
    grads_list = [
        weight_grad(query_grad),
        weight_grad(key_grad),
        weight_grad(value_grad),
        grad_out,
        grad_up,
        grad_down,
        jnp.sum(query_grad.astype(jnp.float32), axis=0),
        jnp.sum(key_grad.astype(jnp.float32), axis=0),
        jnp.sum(value_grad.astype(jnp.float32), axis=0),
        grad_bout,
        grad_bup,
        grad_bdown,
        gain1_grad,
        shift1_grad,
        gain2_grad,
        shift2_grad,
    ]
    flattened = jnp.concatenate([gradient.reshape(-1) for gradient in grads_list])
    shared = lax.psum_scatter(flattened, ("seq", "row"), scatter_dimension=0, tiled=True)
    combined = lax.all_gather(shared, ("seq", "row"), axis=0, tiled=True)
    pieces = []
    cursor = 0
    for gradient in grads_list:
        pieces.append(combined[cursor : cursor + gradient.size].reshape(gradient.shape))
        cursor = cursor + gradient.size
    return (
        result[None],
        input_grad[None],
        pieces[0],
        pieces[1],
        pieces[2],
        pieces[3],
        pieces[4],
        pieces[5],
        pieces[6],
        pieces[7],
        pieces[8],
        pieces[9],
        pieces[10],
        pieces[11],
        pieces[12],
        pieces[13],
        pieces[14],
        pieces[15],
    )


def solution(mesh):
    return jax.shard_map(
        on_device,
        mesh=mesh,
        in_specs=(
            P("row", "seq", None),
            P(),
            P(),
            P(),
            P(),
            P(),
            P(),
            P(),
            P(),
            P(),
            P(),
            P(),
            P(),
            P(),
            P(),
            P(),
            P(),
            P(),
            P("row", None),
            P("row", None),
            P("row", "seq", None),
        ),
        out_specs=(
            P("row", "seq", None),
            P("row", "seq", None),
            P(),
            P(),
            P(),
            P(),
            P(),
            P(),
            P(),
            P(),
            P(),
            P(),
            P(),
            P(),
            P(),
            P(),
            P(),
            P(),
        ),
        check_vma=False,
    )
```

profile of v0, /device:TPU:0, one launch (start us, length us, event | category | flops | bytes accessed | tf_op | source)
XLA Modules:
  0.0 1565.4 jit_solution(14341729555298297349)
XLA Ops:
  10.8 5.0 add_convert_fusion.2
  19.7 13.1 convert_reduce_fusion.1
  41.2 6.0 add_convert_fusion
  47.2 4.7 copy.85
  51.9 4.6 copy.87
  63.2 14.4 fusion.13
  77.6 84.6 %all-reduce.15.cloned.1.call-done = (f32[6,12,256,64]{2,3,1,0:T(8,128)}, f32[6,12,256]{2,1,0:T(8,128)}) async-done(((f32[6,12,256,64]{2,3,1,0:T(8,128)}, f32[6,12,256]{2,1,0:T(8,128)}), (f32[6,12,256,64]{2,3,1,0:T(8,128)}, f32[6,12,256]{2,1,0:T(8,128)})) %all-reduce.15.cloned.1.call-update) | async-done | bytes 4792336 | tf_op jit(solution)/shard_map/psum | solution.py:126
  163.3 13.1 fusion.64
  177.1 12.5 fusion.31
  189.6 5.0 fusion.79
  198.6 27.2 %multiply_convert_fusion = (bf16[2048,3072]{1,0:T(8,128)(2,1)}, f32[2048,3072]{1,0:T(8,128)}) fusion(f32[3072]{0:T(1024)S(1)} %convert_element_type.162, bf16[768,3072]{1,0:T(8,128)(2,1)} %param.27, f32[2048,768]{0,1:T(8,128)} %copy-done.6, f32[768]{0:T(1024)S(1)} %convert_element_type.160, f32[768]{0:T(1024)S(1)} %convert_element_type.159, ...), kind=kOutput, calls=%fused_computation.19 | convolution fusion | flops 9734455296 | bytes 48793600 | tf_op jit(solution)/shard_map/dot_general | solution.py:147
  225.9 18.0 %fusion.80 = (f32[2048]{0:T(1024)S(1)}, f32[2048,768]{0,1:T(8,128)}) fusion(f32[768]{0:T(1024)S(1)} %convert_element_type.164, bf16[2048,3072]{1,0:T(8,128)(2,1)} %get-tuple-element.136, bf16[3072,768]{1,0:T(8,128)(2,1)} %param.28, f32[768]{0:T(1024)S(1)} %convert_element_type.160, f32[768]{0:T(1024)S(1)} %convert_element_type.159, f32[2048]{0:T(1024)S(1)} %fusion.66, ...), kind=kOutput, calls=%fused_computation.153 | convolution fusion | flops 9674684416 | bytes 29918208 | tf_op jit(solution)/shard_map/dot_general | solution.py:152
  243.9 4.8 fusion.23
  254.3 6.1 convert_reduce_fusion.3
  260.4 34.1 %convert_reduce_fusion = (f32[3072]{0:T(1024)}, bf16[2048,3072]{1,0:T(8,128)(2,1)}) fusion(f32[2048,3072]{1,0:T(8,128)} %get-tuple-element.137, f32[3072]{0:T(1024)S(1)} %convert_element_type.162, bf16[2048,768]{0,1:T(8,128)(2,1)} %get-tuple-element.102, bf16[3072,768]{1,0:T(8,128)(2,1)} %param.28), kind=kOutput, calls=%fused_computation.18 | convolution fusion | flops 9808376832 | bytes 45637632 | tf_op jit(solution)/shard_map/td,fd->tf/dot_general | solution.py:168
  294.5 20.7 %multiply_reduce_fusion = (f32[768]{0:T(1024)}, f32[2048]{0:T(1024)S(1)}, f32[768]{0:T(1024)}, f32[2048,768]{0,1:T(8,128)}) fusion(f32[2048,768]{0,1:T(8,128)} %copy-done.6, f32[2048]{0:T(1024)S(1)} %fusion.66, f32[2048]{0:T(1024)S(1)} %broadcast_multiply_fusion.9, f32[768]{0:T(1024)S(1)} %convert_element_type.159, ...), kind=kOutput, calls=%fused_computation.52 | convolution fusion | flops 9690411008 | bytes 39391232 | tf_op jit(solution)/shard_map/tf,df->td/dot_general | solution.py:172
  315.2 17.1 %convolution_bitcast_fusion = f32[96,24,8,128]{3,2,1,0:T(8,128)} fusion(bf16[2048,3072]{1,0:T(8,128)(2,1)} %get-tuple-element.152, f32[2048,768]{0,1:T(8,128)} %copy-done.6, f32[768]{0:T(1024)S(1)} %convert_element_type.160, f32[768]{0:T(1024)S(1)} %convert_element_type.159, f32[2048]{0:T(1024)S(1)} %fusion.66, f32[2048]{0:T(1024)S(1)} %broadcast_multiply_fusion.9), kind=kOutput, calls=%fused_computation.76 | convolution fusion | flops 9671540736 | bytes 28334080 | tf_op jit(solution)/shard_map/td,tf->df/dot_general | solution.py:170
  332.3 3.9 fusion.73
  337.5 5.2 fusion.86
  346.3 5.1 fusion.68
  351.4 4.4 fusion.32
  355.9 5.1 fusion.61
  364.6 21.4 %fusion.82 = (f32[2048,12]{0,1:T(8,128)S(1)}, bf16[2048,12,256]{2,0,1:T(8,128)(2,1)}) fusion(f32[2048,12]{0,1:T(8,128)S(1)} %copy-done.30, f32[12,2048,256]{2,1,0:T(8,128)} %get-tuple-element.131, f32[12,256]{1,0:T(8,128)S(1)} %copy-done.38, f32[2048,12]{0,1:T(8,128)S(1)} %multiply_divide_fusion, bf16[12,256,64]{1,2,0:T(8,128)(2,1)S(1)} %copy-done.32, ...), kind=kOutput, calls=%fused_computation.155 | convolution fusion | flops 858759168 | bytes 44838912 | tf_op jit(solution)/shard_map/nlr,lur->nlu/dot_general | solution.py:187
  386.1 7.4 convert_reduce_fusion.7
  395.1 4.0 fusion.47
  406.0 6.9 fusion.83
  415.3 9.9 copy.110
  425.2 15.4 fusion.84
  440.6 10.8 reshape.257
  451.5 73.2 %all-reduce.13.cloned.1.call-done = (f32[6,12,256]{2,1,0:T(8,128)}, f32[6,12,256,64]{2,3,1,0:T(8,128)}) async-done(((f32[6,12,256]{2,1,0:T(8,128)}, f32[6,12,256,64]{2,3,1,0:T(8,128)}), (f32[6,12,256]{2,1,0:T(8,128)}, f32[6,12,256,64]{2,3,1,0:T(8,128)})) %all-reduce.13.cloned.1.call-update) | async-done | bytes 4792336 | tf_op jit(solution)/shard_map/psum | solution.py:198
  528.6 10.3 convert_reduce_fusion.5
  538.9 19.2 %fusion.81 = (f32[2048,12]{0,1:T(8,128)S(1)}, bf16[2048,12,256]{2,0,1:T(8,128)(2,1)}) fusion(f32[2048,12]{0,1:T(8,128)S(1)} %copy-done.36, f32[12,2048,256]{2,1,0:T(8,128)} %get-tuple-element.129, f32[2048]{0:T(1024)S(1)} %copy-done.46, f32[12,256]{1,0:T(8,128)S(1)} %multiply_reduce_fusion.6, bf16[12,256,64]{1,2,0:T(8,128)(2,1)S(1)} %multiply_reduce_fusion.4, ...), kind=kOutput, calls=%fused_computation.154 | convolution fusion | flops 855613440 | bytes 41504768 | tf_op jit(solution)/shard_map/nlr,lur->nlu/dot_general | solution.py:206
  558.2 7.2 convert_reduce_fusion.6
  567.0 4.0 fusion.50
  577.3 6.8 fusion.53
  597.2 9.3 constant_dynamic-update-slice_fusion.11
  606.6 3.9 constant_dynamic-update-slice_fusion.10
  622.2 433.5 %all-reduce.11.cloned.1.call-done = f32[7087872]{0:T(1024)} async-done(((f32[7087872]{0:T(1024)}), f32[7087872]{0:T(1024)}) %all-reduce.11.cloned.1.call-update) | async-done | bytes 28351504
  1055.6 9.8 broadcast.172
  1068.4 7.1 copy.97
  1075.6 4.6 fusion.87
  1083.3 4.6 add_bitcast_fusion
  1087.9 6.6 copy.98
  1094.5 406.4 %all-reduce.9.cloned.1.call-done = f32[7087872]{0:T(1024)} async-done(((f32[7087872]{0:T(1024)}), f32[7087872]{0:T(1024)}) %all-reduce.9.cloned.1.call-update) | async-done | bytes 28351504
  1500.9 6.9 fusion.78
  1519.5 14.2 fusion.77
  1533.7 10.9 reshape.258
  1544.6 11.4 slice.108
  (244 shorter events, 109.9 us)
Async XLA Ops:
  7.2 182.4 %copy-start = (bf16[768,768]{1,0:T(8,128)(2,1)S(1)}, bf16[768,768]{1,0:T(8,128)(2,1)}, u32[]{:S(2)}) copy-start(bf16[768,768]{1,0:T(8,128)(2,1)} %param.26) | copy-start | bytes 3538948
  7.2 155.1 %all-reduce.15.cloned.1.call-start = ((), (), s32[]{:S(2)}) async-start(), calls=%async_computation.3 | async-start | bytes 9633792 | tf_op jit(solution)/shard_map/psum | solution.py:126
  8.7 167.8 %copy-start.43 = (f32[6]{0:T(128)}, f32[6]{0:T(128)S(1)}, u32[]{:S(2)}) copy-start(f32[6]{0:T(128)S(1)} %get-tuple-element.109) | copy-start | bytes 76
  19.7 13.1 copy-start.13
  40.9 483.8 %all-reduce.13.cloned.1.call-start = ((), (), s32[]{:S(2)}) async-start(), calls=%async_computation.2 | async-start | bytes 9633792 | tf_op jit(solution)/shard_map/psum | solution.py:198
  47.1 9.4 copy-start.56
  47.1 9.4 copy-start.52
  47.1 9.4 copy-start.57
  47.1 9.5 copy-start.58
  47.1 9.5 copy-start.59
  47.2 9.5 copy-start.60
  47.2 9.5 copy-start.61
  163.2 13.1 copy-start.37
  163.3 13.2 copy-start.12
  176.4 13.1 copy-start.33
  177.1 12.5 copy-start.31
  177.1 12.5 copy-start.22
  315.1 17.1 %copy-start.40 = (f32[2048]{0:T(1024)S(1)}, f32[2048]{0:T(1024)}, u32[]{:S(2)}) copy-start(f32[2048]{0:T(1024)} %copy-done.39) | copy-start | bytes 24580
  315.2 17.2 %copy-start.11 = (f32[2048,768]{0,1:T(8,128)S(1)}, f32[2048,768]{0,1:T(8,128)}, u32[]{:S(2)}) copy-start(f32[2048,768]{0,1:T(8,128)} %get-tuple-element.140) | copy-start | bytes 18874372
  336.2 8.8 slice-start.1
  337.4 8.8 slice-start.2
  337.4 8.8 copy-start.34
  337.5 13.9 slice-start.8
  355.9 8.7 copy-start.30
  355.9 8.7 copy-start.32
  355.9 8.7 copy-start.38
  364.6 21.5 %copy-start.8 = (bf16[2048,768]{0,1:T(8,128)(2,1)S(1)}, bf16[2048,768]{0,1:T(8,128)(2,1)}, u32[]{:S(2)}) copy-start(bf16[2048,768]{0,1:T(8,128)(2,1)} %add_convert_fusion) | copy-start | bytes 9437188
  364.6 21.5 %copy-start.28 = (bf16[12,256,64]{1,2,0:T(8,128)(2,1)S(1)}, bf16[12,256,64]{1,2,0:T(8,128)(2,1)}, u32[]{:S(2)}) copy-start(bf16[12,256,64]{1,2,0:T(8,128)(2,1)} %param.39) | copy-start | bytes 1179652
  386.1 9.0 copy-start.18
  406.0 649.7 %all-reduce.11.cloned.1.call-start = ((), (), s32[]{:S(2)}) async-start(), calls=%async_computation.1 | async-start | bytes 56705024
  415.3 10.0 copy-start.15
  528.6 10.3 copy-start.14
  528.6 10.3 copy-start.36
  528.6 10.3 copy-start.46
  538.9 19.2 %copy-start.21 = (bf16[2048,768]{0,1:T(8,128)(2,1)S(1)}, bf16[2048,768]{0,1:T(8,128)(2,1)}, u32[]{:S(2)}) copy-start(bf16[2048,768]{0,1:T(8,128)(2,1)} %copy-done.20) | copy-start | bytes 9437188
  558.2 8.9 copy-start.19
  597.2 9.3 slice-start.5
  597.2 9.3 slice-start.6
  597.2 9.3 slice-start.7
  606.5 7.9 copy-start.47
  606.5 9.2 copy-start.51
  606.5 9.7 copy-start.50
  606.6 11.0 copy-start.54
  606.6 12.3 copy-start.53
  606.6 13.6 copy-start.49
  606.6 14.9 copy-start.48
  622.1 878.8 %all-reduce.9.cloned.1.call-start = ((), (), s32[]{:S(2)}) async-start(), calls=%async_computation | async-start | bytes 56705024
  1544.5 14.1 copy-start.1
  (34 other events, 140.5 us)
Sparse Core Ops, SparseCore 0:
  41.0 121.2 all-reduce.14
  406.1 118.5 all-reduce.12
  622.2 433.3 all-reduce.10
  1068.5 432.2 all-reduce.8
where the time goes:
time: 1570 us
  waiting for transfers between devices  998 us (64%)
  matrix products  321 us (20%)
  local copies, waits for them, and re-layouts  184 us (12%)
  other arithmetic  47.2 us (3%)
    unnamed x6, waiting for transfers between devices  840 us
    unnamed x178, local copies, waits for them, and re-layouts  96 us
    psum x1, waiting for transfers between devices, on_device(): lax.psum((spread_bucket(onehot, summary_part), spread_bucket(onehot, norm...  84.6 us
    psum x1, waiting for transfers between devices, on_device(): lax.psum((spread_bucket(onehot, summary_grad_part), spread_bucket(onehot,...  73.2 us
    slice x9, local copies, waits for them, and re-layouts, on_device(): combined[cursor:cursor + gradient.size].reshape(gradient.shape)  46.9 us
    dot_general x1, matrix products, on_device(): jnp.einsum('td,fd->tf', feed_grad, w_down, preferred_element_type=jnp.flo...  34.1 us
  transfers between devices with their start and end apart: 4, of which 4 were waited for; matrix products, arithmetic and copies ran while one was open for 7% of the time, Pallas kernels for 0%

commit v1 on v0

--- a/solution.py
+++ b/solution.py
@@ -41,12 +41,96 @@
     ) * rounded_values.astype(jnp.float32)
 
 
-def pick_bucket(onehot, summed):
-    return jnp.sum(onehot.reshape((-1,) + (1,) * (summed.ndim - 1)) * summed, axis=0)
-
-
-def spread_bucket(onehot, local_part):
-    return onehot.reshape((-1,) + (1,) * local_part.ndim) * local_part[None]
+def bits_of(axis):
+    return [(axis, bit) for bit in range(lax.axis_size(axis).bit_length() - 1)]
+
+
+def coordinate(tag):
+    return (lax.axis_index(tag[0]) >> tag[1]) & 1
+
+
+def exchange(sent, tag):
+    pairs = [(i, i ^ (1 << tag[1])) for i in range(lax.axis_size(tag[0]))]
+    return lax.ppermute(sent, tag[0], pairs)
+
+
+def halve_sum(array, tags, order):
+    left = list(tags)
+    for tag in order:
+        where = left.index(tag)
+        mine = coordinate(tag)
+        sent = lax.dynamic_index_in_dim(array, 1 - mine, where, keepdims=False)
+        kept = lax.dynamic_index_in_dim(array, mine, where, keepdims=False)
+        array = kept + exchange(sent, tag)
+        left.pop(where)
+    return array
+
+
+def double_gather(block, order):
+    for tag in reversed(order):
+        other = exchange(block, tag)
+        mine = coordinate(tag) == 0
+        block = jnp.stack([jnp.where(mine, block, other), jnp.where(mine, other, block)])
+    return block
+
+
+def weight_tags():
+    seq, row = bits_of("seq"), bits_of("row")
+    first = seq[:1] + row + seq[1:]
+    second = seq[:2] + row + seq[2:]
+    return first, second
+
+
+def scatter_chunks(chunks):
+    first, second = weight_tags()
+    out = []
+    for number, chunk in enumerate(chunks):
+        order = second if number % 2 else first
+        rows = chunk.shape[0] >> len(first)
+        out.append(halve_sum(chunk.reshape((2,) * len(first) + (rows, chunk.shape[1])), first, order))
+    return out
+
+
+def gather_blocks(block):
+    whole = lax.all_gather(block, ("seq", "row"), axis=0, tiled=False)
+    seq, row = bits_of("seq"), bits_of("row")
+    tags = seq[::-1] + row[::-1]
+    first, _ = weight_tags()
+    whole = whole.reshape((2,) * len(tags) + block.shape)
+    places = [tags.index(tag) for tag in first]
+    rest = list(range(len(tags), len(tags) + block.ndim))
+    return whole.transpose(places + rest).reshape((1 << len(tags),) + block.shape)
+
+
+def sum_devices(array):
+    for tag in weight_tags()[0]:
+        array = array + exchange(array, tag)
+    return array
+
+
+def bucket_sum(onehot, shared, summary_part, normaliser_part):
+    heads, features, width = summary_part.shape
+    tags = bits_of("seq")
+    unit = 8 << len(tags)
+    rows = heads * width + heads
+    padded = -(-rows // unit) * unit
+    part = jnp.concatenate(
+        [
+            summary_part.transpose(0, 2, 1).reshape(heads * width, features),
+            normaliser_part,
+            jnp.zeros((padded - rows, features), jnp.float32),
+        ]
+    )
+    slots = onehot[:shared].reshape(1, shared, 1, 1)
+    blocks = part.reshape(1 << len(tags), 1, padded >> len(tags), features) * slots
+    blocks = blocks.reshape((2,) * len(tags) + blocks.shape[1:])
+    order = tags
+    summed = double_gather(halve_sum(blocks, tags, order), order)
+    summed = jnp.sum(summed.reshape((1 << len(tags),) + summed.shape[len(tags):]) * slots, axis=1)
+    alone = 1.0 - jnp.sum(onehot[:shared])
+    summed = summed.reshape(padded, features) + alone * part
+    summary = summed[: heads * width].reshape(heads, width, features).transpose(0, 2, 1)
+    return summary, summed[heads * width : rows]
 
 
 def on_device(
@@ -80,7 +164,9 @@
     prefactor = 1.0 / math.sqrt(feature_rows)
     blocks = lax.axis_size("seq")
     position = lax.axis_index("seq")
-    group_limit = jnp.array([5 * blocks // 8, blocks // 8] + [blocks // 16] * 4, jnp.int32) * tokens
+    widths = [5 * blocks // 8, blocks // 8] + [blocks // 16] * 4
+    shared = sum(width > 1 for width in widths)
+    group_limit = jnp.array(widths, jnp.int32) * tokens
     openings = seq_starts[0]
     lengths_row = seq_lengths[0]
     block_start = position * tokens
@@ -123,11 +209,7 @@
         "uzl,uzy->zly", key_reduced, input_values, preferred_element_type=jnp.float32
     )
     normaliser_part = jnp.sum(key_reduced.astype(jnp.float32), axis=0)
-    summed = lax.psum(
-        (spread_bucket(onehot, summary_part), spread_bucket(onehot, normaliser_part)), "seq"
-    )
-    key_value_summary = pick_bucket(onehot, summed[0])
-    normaliser = pick_bucket(onehot, summed[1])
+    key_value_summary, normaliser = bucket_sum(onehot, shared, summary_part, normaliser_part)
     summary_reduced = key_value_summary.astype(jnp.bfloat16)
     attention_numerator = jnp.einsum(
         "pez,ezi->pei", query_reduced, summary_reduced, preferred_element_type=jnp.float32
@@ -195,12 +277,9 @@
     normaliser_grad_part = jnp.einsum(
         "thm,th->hm", query_wide, denominator_grad, precision=lax.Precision.HIGHEST
     )
-    summed_grad = lax.psum(
-        (spread_bucket(onehot, summary_grad_part), spread_bucket(onehot, normaliser_grad_part)),
-        "seq",
-    )
-    summary_grad = pick_bucket(onehot, summed_grad[0])
-    normaliser_grad = pick_bucket(onehot, summed_grad[1])
+    summary_grad, normaliser_grad = bucket_sum(
+        onehot, shared, summary_grad_part, normaliser_grad_part
+    )
     summary_gradient_reduced = summary_grad.astype(jnp.bfloat16)
     kfeat_grad = (
         jnp.einsum(
@@ -248,13 +327,25 @@
         + back_through(key_grad, w_key)
         + back_through(value_grad, w_value)
     )
-    grads_list = [
-        weight_grad(query_grad),
-        weight_grad(key_grad),
-        weight_grad(value_grad),
-        grad_out,
-        grad_up,
-        grad_down,
+    ff = grad_up.shape[1]
+
+    def columns(matrix):
+        half = matrix.shape[1] // 2
+        return [matrix[:, :half], matrix[:, half:]]
+
+    down_blocks = scatter_chunks(columns(grad_down))
+    up_blocks = scatter_chunks(columns(grad_up))
+    first_blocks = scatter_chunks([grad_out, weight_grad(query_grad)])
+    last_blocks = scatter_chunks([weight_grad(key_grad), weight_grad(value_grad)])
+    whole_down = gather_blocks(jnp.concatenate(down_blocks, axis=1)).reshape(ff, model_width)
+    whole_up = gather_blocks(jnp.concatenate(up_blocks, axis=1)).reshape(model_width, ff)
+    whole_first = gather_blocks(jnp.stack(first_blocks))
+    whole_last = gather_blocks(jnp.stack(last_blocks))
+
+    def square(whole, which):
+        return whole[:, which].reshape(model_width, model_width)
+
+    small = [
         jnp.sum(query_grad.astype(jnp.float32), axis=0),
         jnp.sum(key_grad.astype(jnp.float32), axis=0),
         jnp.sum(value_grad.astype(jnp.float32), axis=0),
@@ -266,13 +357,18 @@
         gain2_grad,
         shift2_grad,
     ]
-    flattened = jnp.concatenate([gradient.reshape(-1) for gradient in grads_list])
-    shared = lax.psum_scatter(flattened, ("seq", "row"), scatter_dimension=0, tiled=True)
-    combined = lax.all_gather(shared, ("seq", "row"), axis=0, tiled=True)
-    pieces = []
+    small_sum = sum_devices(jnp.concatenate(small).reshape(-1, model_width)).reshape(-1)
+    pieces = [
+        square(whole_first, 1),
+        square(whole_last, 0),
+        square(whole_last, 1),
+        square(whole_first, 0),
+        whole_up,
+        whole_down,
+    ]
     cursor = 0
-    for gradient in grads_list:
-        pieces.append(combined[cursor : cursor + gradient.size].reshape(gradient.shape))
+    for gradient in small:
+        pieces.append(small_sum[cursor : cursor + gradient.size])
         cursor = cursor + gradient.size
     return (
         result[None],

time: 1570 us -> 810 us (0.52)
  waiting for transfers between devices: 998 us -> 271 us
  local copies, waits for them, and re-layouts: 184 us -> 86 us
  starting transfers between devices: 0.38 us -> 65 us
  matrix products: 321 us -> 305 us
    unnamed x6 -> x4, waiting for transfers between devices: 840 us -> 0.07 us
    ppermute x0 -> x61, waiting for transfers between devices: none -> 254 us  [exchange(): return lax.ppermute(sent, tag[0], pairs)]
    psum x2 -> x0, waiting for transfers between devices: 158 us -> none  [the longest x1 84.6 us: on_device(): lax.psum((spread_bucket(onehot, summary_part), spread_bucket(onehot, norm...]
    ppermute x0 -> x61, starting transfers between devices: none -> 64.8 us  [exchange(): return lax.ppermute(sent, tag[0], pairs)]
    unnamed x178 -> x185, local copies, waits for them, and re-layouts: 96 us -> 38.4 us
    reshape x6 -> x1, local copies, waits for them, and re-layouts: 32.1 us -> 0.01 us  [on_device(): jnp.concatenate(small).reshape(-1, model_width)]
    slice x9 -> x11, local copies, waits for them, and re-layouts: 46.9 us -> 16.8 us  [the longest x2 9.17 us: columns(): return [matrix[:, :half], matrix[:, half:]]]
    transpose x0 -> x4, local copies, waits for them, and re-layouts: none -> 22.7 us  [gather_blocks(): whole.transpose(places + rest).reshape((1 << len(tags),) + block.shape)]
  transfers between devices with their start and end apart: 4 -> 65, of which waited for: 4 -> 40; matrix products, arithmetic and copies ran while one was open for 7% -> 28% of each run, Pallas kernels for 0% -> 0%
where the time goes in v1:
time: 810 us; the launch traced here: 806 us
  matrix products  305 us (38%)
  waiting for transfers between devices  271 us (33%)
  local copies, waits for them, and re-layouts  86 us (11%)
  starting transfers between devices  65 us (8%)
  other arithmetic  61.1 us (8%)
  between operations  16.8 us (2%)
    ppermute x61, waiting for transfers between devices, exchange(): return lax.ppermute(sent, tag[0], pairs)  254 us
    ppermute x61, starting transfers between devices, exchange(): return lax.ppermute(sent, tag[0], pairs)  64.8 us
    unnamed x185, local copies, waits for them, and re-layouts  38.4 us
    dot_general x1, matrix products, on_device(): jnp.einsum('td,fd->tf', feed_grad, w_down, preferred_element_type=jnp.flo...  34.2 us
    dot_general x1, matrix products, on_device(): jnp.dot(normed_low, w_up, preferred_element_type=jnp.float32)  27.3 us
    dot_general x2, matrix products, feature_logits(): jnp.einsum('nlr,lur->nlu', rounded_values, head_feature_directions, prefe...  25.1 us
    transpose x4, local copies, waits for them, and re-layouts, gather_blocks(): whole.transpose(places + rest).reshape((1 << len(tags),) + block.shape)  22.7 us
    dot_general x1, matrix products, on_device(): jnp.einsum('tf,df->td', pre_grad, w_up, preferred_element_type=jnp.float32)  20.7 us
  transfers between devices with their start and end apart: 65, of which 40 were waited for; matrix products, arithmetic and copies ran while one was open for 28% of the time, Pallas kernels for 0%

profile of v1, /device:TPU:0, one launch (start us, length us, event | category | flops | bytes accessed | tf_op | source)
XLA Modules:
  0.0 805.6 jit_solution(12044869743303610779)
XLA Ops:
  10.1 5.0 add_convert_fusion.1
  17.6 5.2 add_convert_fusion.2
  22.8 13.0 %convert_reduce_fusion.1 = (f32[12,256]{1,0:T(8,128)S(1)}, bf16[2048,12,256]{2,0,1:T(8,128)(2,1)S(1)}, f32[12,2048,256]{2,1,0:T(8,128)}) fusion(bf16[2048]{0:T(1024)(128)(2,1)S(1)} %convert_element_type.151, f32[2048,12]{0,1:T(8,128)S(1)} %broadcast_multiply_fusion.5, bf16[2048,12,64]{0,2,1:T(8,128)(2,1)S(1)} %bitcast.492, ...), kind=kOutput, calls=%fused_computation.20 | convolution fusion | flops 849343488 | bytes 41402368 | tf_op jit(solution)/shard_map/nlr,lur->nlu/dot_general | solution.py:24
  50.8 10.9 %collective-permute-done.1 = f32[2,2,2,56,256]{4,3,2,1,0:T(8,128)} collective-permute-done((f32[2,2,2,56,256]{4,3,2,1,0:T(8,128)S(1)}, f32[2,2,2,56,256]{4,3,2,1,0:T(8,128)}, u32[]{:S(2)}, u32[]{:S(2)}) %collective-permute-start.1) | collective-permute-done | bytes 458784 | tf_op jit(solution)/shard_map/ppermute | solution.py:54
  64.7 5.3 collective-permute-done.2
  78.5 6.6 add_convert_fusion
  100.2 4.8 copy.98
  107.9 12.1 %fusion.13 = (bf16[2048,12,256]{2,0,1:T(8,128)(2,1)S(1)}, f32[12,2048,256]{2,1,0:T(8,128)}) fusion(f32[2048,12]{0,1:T(8,128)S(1)} %broadcast_multiply_fusion.4, bf16[2048,12,64]{0,2,1:T(8,128)(2,1)S(1)} %bitcast.468, bf16[12,256,64]{1,2,0:T(8,128)(2,1)S(1)} %copy-done.29), kind=kOutput, calls=%fused_computation.22 | convolution fusion | flops 830472192 | bytes 41385984 | tf_op jit(solution)/shard_map/nlr,lur->nlu/dot_general | solution.py:24
  121.8 9.8 %fusion.58 = f32[12,1,2048]{2,1,0:T(1,128)S(1)} fusion(bf16[2048,12,256]{2,0,1:T(8,128)(2,1)S(1)} %get-tuple-element.162, f32[12,256,1]{1,0,2:T(8,128)S(1)} %get-tuple-element.146), kind=kOutput, calls=%fused_computation.236 | convolution fusion | flops 75497472 | bytes 12693504 | tf_op jit(solution)/shard_map/thm,hm->th/dot_general | solution.py:217
  132.2 11.4 %fusion.31 = (bf16[2048,12,64]{0,2,1:T(8,128)(2,1)S(1)}, f32[12,64,2048]{2,1,0:T(8,128)}) fusion(f32[2048,12]{0,1:T(8,128)S(1)} %bitcast.513, bf16[12,64,256]{2,1,0:T(8,128)(2,1)S(1)} %bitcast.509, bf16[2048,12,256]{2,0,1:T(8,128)(2,1)} %copy-done.2), kind=kOutput, calls=%fused_computation.50 | convolution fusion | flops 808452096 | bytes 22511616 | tf_op jit(solution)/shard_map/pez,ezi->pei/dot_general | solution.py:214
  150.8 27.3 %multiply_convert_fusion = (bf16[2048,3072]{1,0:T(8,128)(2,1)}, f32[2048,3072]{1,0:T(8,128)}) fusion(f32[3072]{0:T(1024)S(1)} %convert_element_type.163, bf16[768,3072]{1,0:T(8,128)(2,1)} %param.27, f32[2048,768]{0,1:T(8,128)} %copy-done.7, f32[768]{0:T(1024)S(1)} %convert_element_type.161, f32[768]{0:T(1024)S(1)} %convert_element_type.160, ...), kind=kOutput, calls=%fused_computation.19 | convolution fusion | flops 9734455296 | bytes 48793600 | tf_op jit(solution)/shard_map/dot_general | solution.py:229
  178.1 18.0 %fusion.77 = (f32[2048]{0:T(1024)S(1)}, f32[2048,768]{0,1:T(8,128)}) fusion(f32[768]{0:T(1024)S(1)} %convert_element_type.165, bf16[2048,3072]{1,0:T(8,128)(2,1)} %get-tuple-element.168, bf16[3072,768]{1,0:T(8,128)(2,1)} %param.28, f32[768]{0:T(1024)S(1)} %convert_element_type.161, f32[768]{0:T(1024)S(1)} %convert_element_type.160, f32[2048]{0:T(1024)S(1)} %fusion.60, ...), kind=kOutput, calls=%fused_computation.283 | convolution fusion | flops 9674684416 | bytes 29918208 | tf_op jit(solution)/shard_map/dot_general | solution.py:234
  206.5 6.0 convert_reduce_fusion.3
  212.4 34.2 %convert_reduce_fusion = (f32[3072]{0:T(1024)}, bf16[2048,3072]{1,0:T(8,128)(2,1)}) fusion(f32[2048,3072]{1,0:T(8,128)} %get-tuple-element.169, f32[3072]{0:T(1024)S(1)} %convert_element_type.163, bf16[2048,768]{0,1:T(8,128)(2,1)} %get-tuple-element.125, bf16[3072,768]{1,0:T(8,128)(2,1)} %param.28), kind=kOutput, calls=%fused_computation.18 | convolution fusion | flops 9808376832 | bytes 45637632 | tf_op jit(solution)/shard_map/td,fd->tf/dot_general | solution.py:250
  246.6 20.7 %multiply_reduce_fusion = (f32[768]{0:T(1024)}, f32[2048]{0:T(1024)S(1)}, f32[768]{0:T(1024)}, f32[2048,768]{0,1:T(8,128)}) fusion(f32[2048,768]{0,1:T(8,128)} %copy-done.7, f32[2048]{0:T(1024)S(1)} %fusion.60, f32[2048]{0:T(1024)S(1)} %broadcast_multiply_fusion.7, f32[768]{0:T(1024)S(1)} %convert_element_type.160, ...), kind=kOutput, calls=%fused_computation.52 | convolution fusion | flops 9690411008 | bytes 39391232 | tf_op jit(solution)/shard_map/tf,df->td/dot_general | solution.py:254
  267.3 5.6 fusion.69
  282.1 5.0 fusion.63
  291.8 5.1 fusion.51
  297.9 18.4 %fusion.79 = (f32[2048,12]{0,1:T(8,128)S(1)}, bf16[2048,12,256]{2,0,1:T(8,128)(2,1)}) fusion(f32[2048,12]{0,1:T(8,128)S(1)} %copy-done.33, f32[12,2048,256]{2,1,0:T(8,128)} %get-tuple-element.163, f32[12,256]{1,0:T(8,128)S(1)} %copy-done.51, f32[2048,12]{0,1:T(8,128)S(1)} %multiply_divide_fusion, bf16[12,64,256]{2,1,0:T(8,128)(2,1)S(1)} %bitcast.510, ...), kind=kOutput, calls=%fused_computation.285 | convolution fusion | flops 858759168 | bytes 44838912 | tf_op jit(solution)/shard_map/nlr,lur->nlu/dot_general | solution.py:269
  316.3 8.3 %convert_reduce_fusion.7 = (f32[12,64]{1,0:T(8,128)}, bf16[2048,12,64]{0,2,1:T(8,128)(2,1)S(1)}) fusion(bf16[2048,12,64]{0,2,1:T(8,128)(2,1)S(1)} %bitcast.469, f32[2048,12]{0,1:T(8,128)S(1)} %broadcast_multiply_fusion.3, bf16[12,256,64]{1,2,0:T(8,128)(2,1)S(1)} %copy-done.30, bf16[2048,12,256]{2,0,1:T(8,128)(2,1)} %get-tuple-element.176), kind=kOutput, calls=%fused_computation.57 | convolution fusion | flops 816315648 | bytes 19368960 | tf_op jit(solution)/shard_map/pez,ezi->pei/dot_general | solution.py:33
  333.0 15.4 %fusion.64 = f32[768,3072]{1,0:T(8,128)} fusion(bf16[2048,3072]{1,0:T(8,128)(2,1)} %get-tuple-element.184, f32[2048,768]{0,1:T(8,128)S(1)} %bitcast.456, f32[768]{0:T(1024)S(1)} %copy-done.58, f32[768]{0:T(1024)S(1)} %convert_element_type.160, f32[2048]{0:T(1024)S(1)} %fusion.60, f32[2048]{0:T(1024)S(1)} %broadcast_multiply_fusion.7), kind=kOutput, calls=%fused_computation.273 | convolution fusion | flops 9671540736 | bytes 28334080 | tf_op jit(solution)/shard_map/td,tf->df/dot_general | solution.py:252
  353.8 5.2 collective-permute-done.10
  360.8 5.7 collective-permute-done.11
  368.3 4.8 collective-permute-done.12
  394.8 5.2 collective-permute-done.25
  404.2 8.7 %convert_reduce_fusion.5 = (f32[12,64]{1,0:T(8,128)S(1)}, bf16[12,64,2048]{2,1,0:T(8,128)(2,1)S(1)}) fusion(bf16[12,64,256]{2,1,0:T(8,128)(2,1)S(1)} %bitcast.506, bf16[2048,12,256]{2,0,1:T(8,128)(2,1)} %copy-done.4), kind=kOutput, calls=%fused_computation.55 | convolution fusion | flops 810024192 | bytes 16124928 | tf_op jit(solution)/shard_map/pez,ezi->pei/dot_general | solution.py:294
  417.7 19.0 %fusion.78 = (f32[2048,12]{0,1:T(8,128)S(1)}, bf16[2048,12,256]{2,0,1:T(8,128)(2,1)}) fusion(f32[2048,12]{0,1:T(8,128)S(1)} %copy-done.39, f32[12,2048,256]{2,1,0:T(8,128)} %get-tuple-element.161, f32[2048]{0:T(1024)S(1)} %copy-done.47, f32[12,256]{1,0:T(8,128)S(1)} %slice.144, bf16[12,64,256]{2,1,0:T(8,128)(2,1)S(1)} %bitcast.507, ...), kind=kOutput, calls=%fused_computation.284 | convolution fusion | flops 855613440 | bytes 41504768 | tf_op jit(solution)/shard_map/nlr,lur->nlu/dot_general | solution.py:285
  436.8 7.0 convert_reduce_fusion.6
  461.6 10.2 %collective-permute-done.32 = f32[2,2,2,24,768]{4,3,2,1,0:T(8,128)S(1)} collective-permute-done((f32[2,2,2,24,768]{4,3,2,1,0:T(8,128)S(1)}, f32[2,2,2,24,768]{4,3,2,1,0:T(8,128)S(1)}, u32[]{:S(2)}, u32[]{:S(2)}) %collective-permute-start.32) | collective-permute-done | bytes 589856 | tf_op jit(solution)/shard_map/ppermute | solution.py:54
  503.8 23.3 %collective-permute-done.42 = f32[2,2,2,24,1536]{4,3,2,1,0:T(8,128)S(1)} collective-permute-done((f32[2,2,2,24,1536]{4,3,2,1,0:T(8,128)S(1)}, f32[2,2,2,24,1536]{4,3,2,1,0:T(8,128)S(1)}, u32[]{:S(2)}, u32[]{:S(2)}) %collective-permute-start.42) | collective-permute-done | bytes 1179680 | tf_op jit(solution)/shard_map/ppermute | solution.py:54
  528.6 7.9 collective-permute-done.37
  536.9 13.8 %collective-permute-done.43 = f32[2,2,24,1536]{3,2,1,0:T(8,128)S(1)} collective-permute-done((f32[2,2,24,1536]{3,2,1,0:T(8,128)S(1)}, f32[2,2,24,1536]{3,2,1,0:T(8,128)S(1)}, u32[]{:S(2)}, u32[]{:S(2)}) %collective-permute-start.43) | collective-permute-done | bytes 589856 | tf_op jit(solution)/shard_map/ppermute | solution.py:54
  553.1 14.4 %collective-permute-done.44 = f32[2,24,1536]{2,1,0:T(8,128)S(1)} collective-permute-done((f32[2,24,1536]{2,1,0:T(8,128)S(1)}, f32[2,24,1536]{2,1,0:T(8,128)S(1)}, u32[]{:S(2)}, u32[]{:S(2)}) %collective-permute-start.44) | collective-permute-done | bytes 294944 | tf_op jit(solution)/shard_map/ppermute | solution.py:54
  572.8 6.4 collective-permute-done.45
  581.6 16.4 %fusion.81 = f32[3072,768]{1,0:T(8,128)} fusion(bf16[2048,3072]{1,0:T(8,128)(2,1)} %get-tuple-element.168, bf16[2048,768]{0,1:T(8,128)(2,1)} %get-tuple-element.125), kind=kOutput, calls=%fused_computation.287 | convolution fusion | flops 9663676416 | bytes 25165824 | tf_op jit(solution)/shard_map/tf,td->fd/dot_general | solution.py:246
  612.4 26.9 %collective-permute-done.52 = f32[2,2,2,96,384]{4,3,2,1,0:T(8,128)S(1)} collective-permute-done((f32[2,2,2,96,384]{4,3,2,1,0:T(8,128)S(1)}, f32[2,2,2,96,384]{4,3,2,1,0:T(8,128)S(1)}, u32[]{:S(2)}, u32[]{:S(2)}) %collective-permute-start.52) | collective-permute-done | bytes 1179680 | tf_op jit(solution)/shard_map/ppermute | solution.py:54
  641.1 7.0 collective-permute-done.47
  649.9 22.5 %collective-permute-done.53 = f32[2,2,96,384]{3,2,1,0:T(8,128)S(1)} collective-permute-done((f32[2,2,96,384]{3,2,1,0:T(8,128)S(1)}, f32[2,2,96,384]{3,2,1,0:T(8,128)S(1)}, u32[]{:S(2)}, u32[]{:S(2)}) %collective-permute-start.53) | collective-permute-done | bytes 589856 | tf_op jit(solution)/shard_map/ppermute | solution.py:54
  674.8 15.1 %collective-permute-done.54 = f32[2,96,384]{2,1,0:T(8,128)S(1)} collective-permute-done((f32[2,96,384]{2,1,0:T(8,128)S(1)}, f32[2,96,384]{2,1,0:T(8,128)S(1)}, u32[]{:S(2)}, u32[]{:S(2)}) %collective-permute-start.54) | collective-permute-done | bytes 294944 | tf_op jit(solution)/shard_map/ppermute | solution.py:54
  690.9 8.3 %collective-permute-done.49 = f32[2,96,384]{2,1,0:T(8,128)S(1)} collective-permute-done((f32[2,96,384]{2,1,0:T(8,128)S(1)}, f32[2,96,384]{2,1,0:T(8,128)S(1)}, u32[]{:S(2)}, u32[]{:S(2)}) %collective-permute-start.49) | collective-permute-done | bytes 294944 | tf_op jit(solution)/shard_map/ppermute | solution.py:54
  699.4 9.0 %collective-permute-done.50 = f32[96,384]{1,0:T(8,128)S(1)} collective-permute-done((f32[96,384]{1,0:T(8,128)S(1)}, f32[96,384]{1,0:T(8,128)S(1)}, u32[]{:S(2)}, u32[]{:S(2)}) %collective-permute-start.50) | collective-permute-done | bytes 147488 | tf_op jit(solution)/shard_map/ppermute | solution.py:54
  719.0 6.4 fusion.83
  725.5 6.9 copy.110
  739.8 6.5 add_bitcast_fusion
  746.3 6.6 copy.111
  764.9 8.6 %copy.108 = f32[2,2,2,2,2,24,3072]{6,5,4,3,2,1,0:T(8,128)} copy(f32[2,2,2,2,2,24,3072]{6,5,1,0,2,3,4:T(8,128)} %bitcast.472) | data formatting | bytes 18874368 | tf_op jit(solution)/shard_map/transpose | solution.py:102
  773.6 16.7 %all-gather.15.cloned.1.call-done = f32[3072,768]{1,0:T(8,128)} async-done(((f32[96,768]{1,0:T(8,128)}), f32[3072,768]{1,0:T(8,128)}) %all-gather.15.cloned.1.call-update) | async-done | bytes 9437200 | tf_op jit(solution)/shard_map/all_gather | solution.py:95
  790.3 8.5 %copy.109 = f32[2,2,2,2,2,96,768]{6,5,4,3,2,1,0:T(8,128)} copy(f32[2,2,2,2,2,96,768]{6,5,1,0,2,3,4:T(8,128)} %bitcast.473) | data formatting | bytes 18874368 | tf_op jit(solution)/shard_map/transpose | solution.py:102
  (496 shorter events, 243.5 us)
Async XLA Ops:
  7.2 747.0 %all-gather.9.cloned.1.call-start = ((), (), s32[]{:S(2)}) async-start(), calls=%async_computation | async-start | bytes 4866048 | tf_op jit(solution)/shard_map/all_gather | solution.py:95
  47.8 13.9 %collective-permute-start.1 = (f32[2,2,2,56,256]{4,3,2,1,0:T(8,128)S(1)}, f32[2,2,2,56,256]{4,3,2,1,0:T(8,128)}, u32[]{:S(2)}, u32[]{:S(2)}) collective-permute-start(f32[2,2,2,56,256]{4,3,2,1,0:T(8,128)S(1)} %dynamic-slice_bitcast_fusion.23), channel_id=1, source_target_pairs={{0,4},{2,6},{4,0},{6,2},{8,12},{10,14},{12,8},{14,10},{16,20},{18,... | collective-permute-start | bytes 1376264 | tf_op jit(solution)/shard_map/ppermute | solution.py:54
  77.3 7.8 collective-permute-start.4
  85.1 8.0 collective-permute-start.5
  93.2 12.6 %collective-permute-start.6 = (f32[2,2,2,56,256]{4,3,2,1,0:T(8,128)S(1)}, f32[2,2,2,56,256]{4,3,2,1,0:T(8,128)}, u32[]{:S(2)}, u32[]{:S(2)}) collective-permute-start(f32[2,2,2,56,256]{4,3,2,1,0:T(8,128)S(1)} %pad_maximum_fusion.2), channel_id=1, source_target_pairs={{0,4},{2,6},{4,0},{6,2},{8,12},{10,14},{12,8},{14,10},{16,20},{18,... | collective-permute-start | bytes 1376264 | tf_op jit(solution)/shard_map/ppermute | solution.py:54
  107.2 12.8 %collective-permute-start.7 = (f32[2,2,2,2,56,256]{5,4,3,2,1,0:T(8,128)S(1)}, f32[2,2,2,2,56,256]{5,4,3,2,1,0:T(8,128)S(1)}, u32[]{:S(2)}, u32[]{:S(2)}) collective-permute-start(f32[2,2,2,2,56,256]{5,4,3,2,1,0:T(8,128)S(1)} %pad_maximum_fusion), channel_id=1, source_target_pairs={{0,2},{2,0},{4,6},{6,4},{8,10},{10,8},{12,14},{14,12},{16,18},{18,... | collective-permute-start | bytes 2752520 | tf_op jit(solution)/shard_map/ppermute | solution.py:54
  297.4 33.7 %collective-permute-start.8 = (f32[2,2,2,2,56,256]{5,4,3,2,1,0:T(8,128)S(1)}, f32[2,2,2,2,56,256]{5,4,3,2,1,0:T(8,128)}, u32[]{:S(2)}, u32[]{:S(2)}) collective-permute-start(f32[2,2,2,2,56,256]{5,4,3,2,1,0:T(8,128)S(1)} %dynamic-slice_bitcast_fusion.12), channel_id=1, source_target_pairs={{0,2},{2,0},{4,6},{6,4},{8,10},{10,8},{12,14},{14,12},{16,18},{18,... | collective-permute-start | bytes 2752520 | tf_op jit(solution)/shard_map/ppermute | solution.py:54
  327.6 20.8 %collective-permute-start.21 = (f32[2,2,2,2,24,768]{5,4,3,2,1,0:T(8,128)S(1)}, f32[2,2,2,2,24,768]{5,4,3,2,1,0:T(8,128)}, u32[]{:S(2)}, u32[]{:S(2)}) collective-permute-start(f32[2,2,2,2,24,768]{5,4,3,2,1,0:T(8,128)S(1)} %dynamic-slice_bitcast_fusion.10), channel_id=1, source_target_pairs={{0,2},{2,0},{4,6},{6,4},{8,10},{10,8},{12,14},{14,12},{16,18},{18,... | collective-permute-start | bytes 3538952 | tf_op jit(solution)/shard_map/ppermute | solution.py:54
  330.6 23.1 %collective-permute-start.16 = (f32[2,2,2,2,24,768]{5,4,3,2,1,0:T(8,128)S(1)}, f32[2,2,2,2,24,768]{5,4,3,2,1,0:T(8,128)S(1)}, u32[]{:S(2)}, u32[]{:S(2)}) collective-permute-start(f32[2,2,2,2,24,768]{5,4,3,2,1,0:T(8,128)S(1)} %dynamic-slice_bitcast_fusion.11), channel_id=1, source_target_pairs={{0,2},{2,0},{4,6},{6,4},{8,10},{10,8},{12,14},{14,12},{16,18},{18,... | collective-permute-start | bytes 3538952 | tf_op jit(solution)/shard_map/ppermute | solution.py:54
  332.4 19.1 %collective-permute-start.9 = (f32[2,2,2,56,256]{4,3,2,1,0:T(8,128)S(1)}, f32[2,2,2,56,256]{4,3,2,1,0:T(8,128)S(1)}, u32[]{:S(2)}, u32[]{:S(2)}) collective-permute-start(f32[2,2,2,56,256]{4,3,2,1,0:T(8,128)S(1)} %dynamic-slice_bitcast_fusion.22), channel_id=1, source_target_pairs={{0,4},{2,6},{4,0},{6,2},{8,12},{10,14},{12,8},{14,10},{16,20},{18,... | collective-permute-start | bytes 1376264 | tf_op jit(solution)/shard_map/ppermute | solution.py:54
  349.9 16.7 %collective-permute-start.22 = (f32[2,2,2,24,768]{4,3,2,1,0:T(8,128)S(1)}, f32[2,2,2,24,768]{4,3,2,1,0:T(8,128)S(1)}, u32[]{:S(2)}, u32[]{:S(2)}) collective-permute-start(f32[2,2,2,24,768]{4,3,2,1,0:T(8,128)S(1)} %dynamic-slice_bitcast_fusion.20), channel_id=1, source_target_pairs={{0,4},{2,6},{4,0},{6,2},{8,12},{10,14},{12,8},{14,10},{16,20},{18,... | collective-permute-start | bytes 1769480 | tf_op jit(solution)/shard_map/ppermute | solution.py:54
  359.2 16.3 %collective-permute-start.17 = (f32[2,2,2,24,768]{4,3,2,1,0:T(8,128)S(1)}, f32[2,2,2,24,768]{4,3,2,1,0:T(8,128)S(1)}, u32[]{:S(2)}, u32[]{:S(2)}) collective-permute-start(f32[2,2,2,24,768]{4,3,2,1,0:T(8,128)S(1)} %dynamic-slice_bitcast_fusion.21), channel_id=1, source_target_pairs={{0,1},{1,0},{2,3},{3,2},{4,5},{5,4},{6,7},{7,6},{8,9},{9,8},{10,11... | collective-permute-start | bytes 1769480 | tf_op jit(solution)/shard_map/ppermute | solution.py:54
  366.7 13.2 %collective-permute-start.23 = (f32[2,2,24,768]{3,2,1,0:T(8,128)S(1)}, f32[2,2,24,768]{3,2,1,0:T(8,128)S(1)}, u32[]{:S(2)}, u32[]{:S(2)}) collective-permute-start(f32[2,2,24,768]{3,2,1,0:T(8,128)S(1)} %dynamic-slice_bitcast_fusion.30), channel_id=1, source_target_pairs={{0,1},{1,0},{2,3},{3,2},{4,5},{5,4},{6,7},{7,6},{8,9},{9,8},{10,11... | collective-permute-start | bytes 884744 | tf_op jit(solution)/shard_map/ppermute | solution.py:54
  375.6 9.9 %collective-permute-start.18 = (f32[2,2,24,768]{3,2,1,0:T(8,128)S(1)}, f32[2,2,24,768]{3,2,1,0:T(8,128)S(1)}, u32[]{:S(2)}, u32[]{:S(2)}) collective-permute-start(f32[2,2,24,768]{3,2,1,0:T(8,128)S(1)} %dynamic-slice_bitcast_fusion.31), channel_id=1, source_target_pairs={{0,4},{2,6},{4,0},{6,2},{8,12},{10,14},{12,8},{14,10},{16,20},{18,... | collective-permute-start | bytes 884744 | tf_op jit(solution)/shard_map/ppermute | solution.py:54
  379.3 12.1 %collective-permute-start.14 = (f32[2,2,2,56,256]{4,3,2,1,0:T(8,128)S(1)}, f32[2,2,2,56,256]{4,3,2,1,0:T(8,128)S(1)}, u32[]{:S(2)}, u32[]{:S(2)}) collective-permute-start(f32[2,2,2,56,256]{4,3,2,1,0:T(8,128)S(1)} %pad_maximum_fusion.3), channel_id=1, source_target_pairs={{0,4},{2,6},{4,0},{6,2},{8,12},{10,14},{12,8},{14,10},{16,20},{18,... | collective-permute-start | bytes 1376264 | tf_op jit(solution)/shard_map/ppermute | solution.py:54
  391.6 10.7 %collective-permute-start.15 = (f32[2,2,2,2,56,256]{5,4,3,2,1,0:T(8,128)S(1)}, f32[2,2,2,2,56,256]{5,4,3,2,1,0:T(8,128)}, u32[]{:S(2)}, u32[]{:S(2)}) collective-permute-start(f32[2,2,2,2,56,256]{5,4,3,2,1,0:T(8,128)S(1)} %pad_maximum_fusion.1), channel_id=1, source_target_pairs={{0,2},{2,0},{4,6},{6,4},{8,10},{10,8},{12,14},{14,12},{16,18},{18,... | collective-permute-start | bytes 2752520 | tf_op jit(solution)/shard_map/ppermute | solution.py:54
  391.7 8.3 %collective-permute-start.25 = (f32[24,768]{1,0:T(8,128)S(1)}, f32[24,768]{1,0:T(8,128)S(1)}, u32[]{:S(2)}, u32[]{:S(2)}) collective-permute-start(f32[24,768]{1,0:T(8,128)S(1)} %dynamic-slice_bitcast_fusion.46), channel_id=1, source_target_pairs={{0,16},{2,18},{4,20},{6,22},{8,24},{10,26},{12,28},{14,30},{16,0},... | collective-permute-start | bytes 221192 | tf_op jit(solution)/shard_map/ppermute | solution.py:54
  393.1 8.4 %collective-permute-start.20 = (f32[24,768]{1,0:T(8,128)S(1)}, f32[24,768]{1,0:T(8,128)S(1)}, u32[]{:S(2)}, u32[]{:S(2)}) collective-permute-start(f32[24,768]{1,0:T(8,128)S(1)} %dynamic-slice_bitcast_fusion.47), channel_id=1, source_target_pairs={{0,16},{2,18},{4,20},{6,22},{8,24},{10,26},{12,28},{14,30},{16,0},... | collective-permute-start | bytes 221192 | tf_op jit(solution)/shard_map/ppermute | solution.py:54
  402.2 357.3 %all-gather.11.cloned.1.call-start = ((), (), s32[]{:S(2)}) async-start(), calls=%async_computation.1 | async-start | bytes 4866048 | tf_op jit(solution)/shard_map/all_gather | solution.py:95
  417.1 36.9 %collective-permute-start.31 = (f32[2,2,2,2,24,768]{5,4,3,2,1,0:T(8,128)}, f32[2,2,2,2,24,768]{5,4,3,2,1,0:T(8,128)}, u32[]{:S(2)}, u32[]{:S(2)}) collective-permute-start(f32[2,2,2,2,24,768]{5,4,3,2,1,0:T(8,128)} %dynamic-slice_bitcast_fusion.8), channel_id=1, source_target_pairs={{0,2},{2,0},{4,6},{6,4},{8,10},{10,8},{12,14},{14,12},{16,18},{18,... | collective-permute-start | bytes 3538952 | tf_op jit(solution)/shard_map/ppermute | solution.py:54
  446.9 10.0 %collective-permute-start.26 = (f32[2,2,2,2,24,768]{5,4,3,2,1,0:T(8,128)S(1)}, f32[2,2,2,2,24,768]{5,4,3,2,1,0:T(8,128)}, u32[]{:S(2)}, u32[]{:S(2)}) collective-permute-start(f32[2,2,2,2,24,768]{5,4,3,2,1,0:T(8,128)S(1)} %dynamic-slice_bitcast_fusion.9), channel_id=1, source_target_pairs={{0,2},{2,0},{4,6},{6,4},{8,10},{10,8},{12,14},{14,12},{16,18},{18,... | collective-permute-start | bytes 3538952 | tf_op jit(solution)/shard_map/ppermute | solution.py:54
  453.6 40.8 %collective-permute-start.41 = (f32[2,2,2,2,24,1536]{5,4,3,2,1,0:T(8,128)}, f32[2,2,2,2,24,1536]{5,4,3,2,1,0:T(8,128)S(1)}, u32[]{:S(2)}, u32[]{:S(2)}) collective-permute-start(f32[2,2,2,2,24,1536]{5,4,3,2,1,0:T(8,128)} %dynamic-slice_bitcast_fusion.2), channel_id=1, source_target_pairs={{0,2},{2,0},{4,6},{6,4},{8,10},{10,8},{12,14},{14,12},{16,18},{18,... | collective-permute-start | bytes 7077896 | tf_op jit(solution)/shard_map/ppermute | solution.py:54
  456.4 15.4 %collective-permute-start.32 = (f32[2,2,2,24,768]{4,3,2,1,0:T(8,128)S(1)}, f32[2,2,2,24,768]{4,3,2,1,0:T(8,128)S(1)}, u32[]{:S(2)}, u32[]{:S(2)}) collective-permute-start(f32[2,2,2,24,768]{4,3,2,1,0:T(8,128)S(1)} %dynamic-slice_bitcast_fusion.18), channel_id=1, source_target_pairs={{0,4},{2,6},{4,0},{6,2},{8,12},{10,14},{12,8},{14,10},{16,20},{18,... | collective-permute-start | bytes 1769480 | tf_op jit(solution)/shard_map/ppermute | solution.py:54
  458.5 15.1 %collective-permute-start.27 = (f32[2,2,2,24,768]{4,3,2,1,0:T(8,128)S(1)}, f32[2,2,2,24,768]{4,3,2,1,0:T(8,128)S(1)}, u32[]{:S(2)}, u32[]{:S(2)}) collective-permute-start(f32[2,2,2,24,768]{4,3,2,1,0:T(8,128)S(1)} %dynamic-slice_bitcast_fusion.19), channel_id=1, source_target_pairs={{0,1},{1,0},{2,3},{3,2},{4,5},{5,4},{6,7},{7,6},{8,9},{9,8},{10,11... | collective-permute-start | bytes 1769480 | tf_op jit(solution)/shard_map/ppermute | solution.py:54
  461.6 37.8 %collective-permute-start.36 = (f32[2,2,2,2,24,1536]{5,4,3,2,1,0:T(8,128)}, f32[2,2,2,2,24,1536]{5,4,3,2,1,0:T(8,128)}, u32[]{:S(2)}, u32[]{:S(2)}) collective-permute-start(f32[2,2,2,2,24,1536]{5,4,3,2,1,0:T(8,128)} %dynamic-slice_bitcast_fusion.3), channel_id=1, source_target_pairs={{0,2},{2,0},{4,6},{6,4},{8,10},{10,8},{12,14},{14,12},{16,18},{18,... | collective-permute-start | bytes 7077896 | tf_op jit(solution)/shard_map/ppermute | solution.py:54
  471.9 8.2 %collective-permute-start.33 = (f32[2,2,24,768]{3,2,1,0:T(8,128)S(1)}, f32[2,2,24,768]{3,2,1,0:T(8,128)S(1)}, u32[]{:S(2)}, u32[]{:S(2)}) collective-permute-start(f32[2,2,24,768]{3,2,1,0:T(8,128)S(1)} %dynamic-slice_bitcast_fusion.28), channel_id=1, source_target_pairs={{0,1},{1,0},{2,3},{3,2},{4,5},{5,4},{6,7},{7,6},{8,9},{9,8},{10,11... | collective-permute-start | bytes 884744 | tf_op jit(solution)/shard_map/ppermute | solution.py:54
  473.7 7.9 collective-permute-start.28
  494.3 270.6 %all-gather.13.cloned.1.call-start = ((), (), s32[]{:S(2)}) async-start(), calls=%async_computation.2 | async-start | bytes 9732096 | tf_op jit(solution)/shard_map/all_gather | solution.py:95
  496.5 30.6 %collective-permute-start.42 = (f32[2,2,2,24,1536]{4,3,2,1,0:T(8,128)S(1)}, f32[2,2,2,24,1536]{4,3,2,1,0:T(8,128)S(1)}, u32[]{:S(2)}, u32[]{:S(2)}) collective-permute-start(f32[2,2,2,24,1536]{4,3,2,1,0:T(8,128)S(1)} %dynamic-slice_bitcast_fusion.6), channel_id=1, source_target_pairs={{0,4},{2,6},{4,0},{6,2},{8,12},{10,14},{12,8},{14,10},{16,20},{18,... | collective-permute-start | bytes 3538952 | tf_op jit(solution)/shard_map/ppermute | solution.py:54
  502.3 34.2 %collective-permute-start.37 = (f32[2,2,2,24,1536]{4,3,2,1,0:T(8,128)S(1)}, f32[2,2,2,24,1536]{4,3,2,1,0:T(8,128)S(1)}, u32[]{:S(2)}, u32[]{:S(2)}) collective-permute-start(f32[2,2,2,24,1536]{4,3,2,1,0:T(8,128)S(1)} %dynamic-slice_bitcast_fusion.7), channel_id=1, source_target_pairs={{0,1},{1,0},{2,3},{3,2},{4,5},{5,4},{6,7},{7,6},{8,9},{9,8},{10,11... | collective-permute-start | bytes 3538952 | tf_op jit(solution)/shard_map/ppermute | solution.py:54
  527.3 23.4 %collective-permute-start.43 = (f32[2,2,24,1536]{3,2,1,0:T(8,128)S(1)}, f32[2,2,24,1536]{3,2,1,0:T(8,128)S(1)}, u32[]{:S(2)}, u32[]{:S(2)}) collective-permute-start(f32[2,2,24,1536]{3,2,1,0:T(8,128)S(1)} %dynamic-slice_bitcast_fusion.16), channel_id=1, source_target_pairs={{0,1},{1,0},{2,3},{3,2},{4,5},{5,4},{6,7},{7,6},{8,9},{9,8},{10,11... | collective-permute-start | bytes 1769480 | tf_op jit(solution)/shard_map/ppermute | solution.py:54
  536.8 15.1 %collective-permute-start.38 = (f32[2,2,24,1536]{3,2,1,0:T(8,128)S(1)}, f32[2,2,24,1536]{3,2,1,0:T(8,128)S(1)}, u32[]{:S(2)}, u32[]{:S(2)}) collective-permute-start(f32[2,2,24,1536]{3,2,1,0:T(8,128)S(1)} %dynamic-slice_bitcast_fusion.17), channel_id=1, source_target_pairs={{0,4},{2,6},{4,0},{6,2},{8,12},{10,14},{12,8},{14,10},{16,20},{18,... | collective-permute-start | bytes 1769480 | tf_op jit(solution)/shard_map/ppermute | solution.py:54
  550.8 16.7 %collective-permute-start.44 = (f32[2,24,1536]{2,1,0:T(8,128)S(1)}, f32[2,24,1536]{2,1,0:T(8,128)S(1)}, u32[]{:S(2)}, u32[]{:S(2)}) collective-permute-start(f32[2,24,1536]{2,1,0:T(8,128)S(1)} %dynamic-slice_bitcast_fusion.26), channel_id=1, source_target_pairs={{0,8},{2,10},{4,12},{6,14},{8,0},{10,2},{12,4},{14,6},{16,24},{18,... | collective-permute-start | bytes 884744 | tf_op jit(solution)/shard_map/ppermute | solution.py:54
  552.0 19.0 %collective-permute-start.39 = (f32[2,24,1536]{2,1,0:T(8,128)S(1)}, f32[2,24,1536]{2,1,0:T(8,128)S(1)}, u32[]{:S(2)}, u32[]{:S(2)}) collective-permute-start(f32[2,24,1536]{2,1,0:T(8,128)S(1)} %dynamic-slice_bitcast_fusion.27), channel_id=1, source_target_pairs={{0,8},{2,10},{4,12},{6,14},{8,0},{10,2},{12,4},{14,6},{16,24},{18,... | collective-permute-start | bytes 884744 | tf_op jit(solution)/shard_map/ppermute | solution.py:54
  567.6 11.6 %collective-permute-start.45 = (f32[24,1536]{1,0:T(8,128)S(1)}, f32[24,1536]{1,0:T(8,128)S(1)}, u32[]{:S(2)}, u32[]{:S(2)}) collective-permute-start(f32[24,1536]{1,0:T(8,128)S(1)} %dynamic-slice_bitcast_fusion.36), channel_id=1, source_target_pairs={{0,16},{2,18},{4,20},{6,22},{8,24},{10,26},{12,28},{14,30},{16,0},... | collective-permute-start | bytes 442376 | tf_op jit(solution)/shard_map/ppermute | solution.py:54
  571.0 9.8 %collective-permute-start.40 = (f32[24,1536]{1,0:T(8,128)S(1)}, f32[24,1536]{1,0:T(8,128)S(1)}, u32[]{:S(2)}, u32[]{:S(2)}) collective-permute-start(f32[24,1536]{1,0:T(8,128)S(1)} %dynamic-slice_bitcast_fusion.37), channel_id=1, source_target_pairs={{0,16},{2,18},{4,20},{6,22},{8,24},{10,26},{12,28},{14,30},{16,0},... | collective-permute-start | bytes 442376 | tf_op jit(solution)/shard_map/ppermute | solution.py:54
  581.6 208.7 %all-gather.15.cloned.1.call-start = ((), (), s32[]{:S(2)}) async-start(), calls=%async_computation.3 | async-start | bytes 9732096 | tf_op jit(solution)/shard_map/all_gather | solution.py:95
  602.9 7.7 collective-permute-start.46
  607.7 31.7 %collective-permute-start.52 = (f32[2,2,2,96,384]{4,3,2,1,0:T(8,128)S(1)}, f32[2,2,2,96,384]{4,3,2,1,0:T(8,128)S(1)}, u32[]{:S(2)}, u32[]{:S(2)}) collective-permute-start(f32[2,2,2,96,384]{4,3,2,1,0:T(8,128)S(1)} %dynamic-slice_bitcast_fusion.4), channel_id=1, source_target_pairs={{0,4},{2,6},{4,0},{6,2},{8,12},{10,14},{12,8},{14,10},{16,20},{18,... | collective-permute-start | bytes 3538952 | tf_op jit(solution)/shard_map/ppermute | solution.py:54
  611.0 37.1 %collective-permute-start.47 = (f32[2,2,2,96,384]{4,3,2,1,0:T(8,128)S(1)}, f32[2,2,2,96,384]{4,3,2,1,0:T(8,128)S(1)}, u32[]{:S(2)}, u32[]{:S(2)}) collective-permute-start(f32[2,2,2,96,384]{4,3,2,1,0:T(8,128)S(1)} %dynamic-slice_bitcast_fusion.5), channel_id=1, source_target_pairs={{0,1},{1,0},{2,3},{3,2},{4,5},{5,4},{6,7},{7,6},{8,9},{9,8},{10,11... | collective-permute-start | bytes 3538952 | tf_op jit(solution)/shard_map/ppermute | solution.py:54
  639.5 32.9 %collective-permute-start.53 = (f32[2,2,96,384]{3,2,1,0:T(8,128)S(1)}, f32[2,2,96,384]{3,2,1,0:T(8,128)S(1)}, u32[]{:S(2)}, u32[]{:S(2)}) collective-permute-start(f32[2,2,96,384]{3,2,1,0:T(8,128)S(1)} %dynamic-slice_bitcast_fusion.14), channel_id=1, source_target_pairs={{0,1},{1,0},{2,3},{3,2},{4,5},{5,4},{6,7},{7,6},{8,9},{9,8},{10,11... | collective-permute-start | bytes 1769480 | tf_op jit(solution)/shard_map/ppermute | solution.py:54
  648.4 25.8 %collective-permute-start.48 = (f32[2,2,96,384]{3,2,1,0:T(8,128)S(1)}, f32[2,2,96,384]{3,2,1,0:T(8,128)S(1)}, u32[]{:S(2)}, u32[]{:S(2)}) collective-permute-start(f32[2,2,96,384]{3,2,1,0:T(8,128)S(1)} %dynamic-slice_bitcast_fusion.15), channel_id=1, source_target_pairs={{0,4},{2,6},{4,0},{6,2},{8,12},{10,14},{12,8},{14,10},{16,20},{18,... | collective-permute-start | bytes 1769480 | tf_op jit(solution)/shard_map/ppermute | solution.py:54
  672.6 17.4 %collective-permute-start.54 = (f32[2,96,384]{2,1,0:T(8,128)S(1)}, f32[2,96,384]{2,1,0:T(8,128)S(1)}, u32[]{:S(2)}, u32[]{:S(2)}) collective-permute-start(f32[2,96,384]{2,1,0:T(8,128)S(1)} %dynamic-slice_bitcast_fusion.24), channel_id=1, source_target_pairs={{0,8},{2,10},{4,12},{6,14},{8,0},{10,2},{12,4},{14,6},{16,24},{18,... | collective-permute-start | bytes 884744 | tf_op jit(solution)/shard_map/ppermute | solution.py:54
  674.2 25.0 %collective-permute-start.49 = (f32[2,96,384]{2,1,0:T(8,128)S(1)}, f32[2,96,384]{2,1,0:T(8,128)S(1)}, u32[]{:S(2)}, u32[]{:S(2)}) collective-permute-start(f32[2,96,384]{2,1,0:T(8,128)S(1)} %dynamic-slice_bitcast_fusion.25), channel_id=1, source_target_pairs={{0,8},{2,10},{4,12},{6,14},{8,0},{10,2},{12,4},{14,6},{16,24},{18,... | collective-permute-start | bytes 884744 | tf_op jit(solution)/shard_map/ppermute | solution.py:54
  690.0 9.4 %collective-permute-start.55 = (f32[96,384]{1,0:T(8,128)S(1)}, f32[96,384]{1,0:T(8,128)S(1)}, u32[]{:S(2)}, u32[]{:S(2)}) collective-permute-start(f32[96,384]{1,0:T(8,128)S(1)} %dynamic-slice_bitcast_fusion.34), channel_id=1, source_target_pairs={{0,16},{2,18},{4,20},{6,22},{8,24},{10,26},{12,28},{14,30},{16,0},... | collective-permute-start | bytes 442376 | tf_op jit(solution)/shard_map/ppermute | solution.py:54
  699.3 9.2 %collective-permute-start.50 = (f32[96,384]{1,0:T(8,128)S(1)}, f32[96,384]{1,0:T(8,128)S(1)}, u32[]{:S(2)}, u32[]{:S(2)}) collective-permute-start(f32[96,384]{1,0:T(8,128)S(1)} %dynamic-slice_bitcast_fusion.35), channel_id=1, source_target_pairs={{0,16},{2,18},{4,20},{6,22},{8,24},{10,26},{12,28},{14,30},{16,0},... | collective-permute-start | bytes 442376 | tf_op jit(solution)/shard_map/ppermute | solution.py:54
  717.5 14.9 %collective-permute-start.58 = (f32[13,768]{1,0:T(8,128)S(1)}, f32[13,768]{1,0:T(8,128)S(1)}, u32[]{:S(2)}, u32[]{:S(2)}) collective-permute-start(f32[13,768]{1,0:T(8,128)S(1)} %add.536), channel_id=1, source_target_pairs={{0,4},{2,6},{4,0},{6,2},{8,12},{10,14},{12,8},{14,10},{16,20},{18,... | collective-permute-start | bytes 119816 | tf_op jit(solution)/shard_map/ppermute | solution.py:54
  737.2 15.7 %collective-permute-start.60 = (f32[13,768]{1,0:T(8,128)S(1)}, f32[13,768]{1,0:T(8,128)S(1)}, u32[]{:S(2)}, u32[]{:S(2)}) collective-permute-start(f32[13,768]{1,0:T(8,128)S(1)} %add.538), channel_id=1, source_target_pairs={{0,16},{2,18},{4,20},{6,22},{8,24},{10,26},{12,28},{14,30},{16,0},... | collective-permute-start | bytes 119816 | tf_op jit(solution)/shard_map/ppermute | solution.py:54
  (103 other events, 1576.0 us)
Sparse Core Ops, SparseCore 0:
  402.4 64.9 all-gather.8
  494.4 72.7 all-gather.10
  581.7 108.0 all-gather.12
  709.4 80.8 all-gather.14

commit v2 on v0

v2 whole, which is shorter than its diff:
```python
import functools
import math
import typing

import jax
import jax.numpy as jnp
from jax import lax
from jax.experimental import pallas as pl
from jax.experimental.pallas import tpu as pltpu
from jax.sharding import PartitionSpec as P

EPSILON = 1e-05
F32, BF16 = jnp.float32, jnp.bfloat16
MIB = 1 << 20
GELU_SCALE = math.sqrt(2.0 / math.pi)
GELU_CUBE = 0.044715


class Consts(typing.NamedTuple):
    scale: float
    norm_ratio: float
    offset: float
    heads: int
    size: int
    feats: int
    lanes: int
    pair_feats: int
    tokens: int
    widths: tuple


def nn(left, right):
    return lax.dot_general(left, right, (((1,), (0,)), ((), ())), preferred_element_type=F32)


def nt(left, right):
    return lax.dot_general(left, right, (((1,), (1,)), ((), ())), preferred_element_type=F32)


def tn(left, right):
    return lax.dot_general(left, right, (((0,), (0,)), ((), ())), preferred_element_type=F32)


def whole(shape):
    zeros = (0,) * len(shape)
    return pl.BlockSpec(shape, lambda *_: zeros, pipeline_mode=pl.Buffered(1))


def rows_of(tile, width):
    return pl.BlockSpec((tile, width), lambda i, *_: (i, 0))


def summed(shape):
    zeros = (0,) * len(shape)
    return pl.BlockSpec(shape, lambda *_: zeros)


def shape_of(shape, dtype):
    return jax.ShapeDtypeStruct(shape, dtype)


ANY = pl.BlockSpec(memory_space=pl.ANY)


def clear(*refs):
    @pl.when(pl.program_id(0) == 0)
    def _():
        for ref in refs:
            ref[...] = jnp.zeros(ref.shape, ref.dtype)


def add_to(ref, value):
    ref[...] += value


def features(values, directions_ref, pair, consts):
    wide = values.astype(F32)
    squares = (wide * wide * consts.norm_ratio).astype(BF16)
    dots = nn(jnp.concatenate([values, squares], axis=1), directions_ref[pair])
    return jnp.exp(dots * consts.scale - consts.offset)


def live_tokens(consts, starts, lengths):
    place = lax.axis_index("seq") * consts.tokens
    count = 0
    for bucket, width in enumerate(consts.widths):
        before = place - starts[bucket]
        inside = (before >= 0) & (before < width * consts.tokens)
        count = count + jnp.where(inside, jnp.clip(lengths[bucket] - before, 0, consts.tokens), 0)
    return count


def key_kernel(consts, starts, lengths, x_ref, wk_ref, wv_ref, par_ref, turns_ref,
               k_ref, v_ref, kf_ref, sum_ref, dirs_ref, vt_ref):
    heads, size, feats, lanes, pair_feats = consts.heads, consts.size, consts.feats, consts.lanes, consts.pair_feats
    group = size + 16
    clear(sum_ref)

    @pl.when(pl.program_id(0) == 0)
    def _():
        dirs_ref[...] = jnp.zeros(dirs_ref.shape, BF16)
        minus = jnp.full((size, feats), -1.0, BF16)
        for head in range(heads):
            pair, e = divmod(head, 2)
            turned = jnp.transpose(turns_ref[head].astype(F32)).astype(BF16)
            dirs_ref[pair, pl.ds(e * size, size), pl.ds(e * feats, feats)] = turned
            dirs_ref[pair, pl.ds(lanes + e * size, size), pl.ds(e * feats, feats)] = minus

    tile = x_ref.shape[0]
    x = x_ref[...]
    k_ref[...] = (nn(x, wk_ref[...]) + par_ref[1:2]).astype(BF16)
    values = nn(x, wv_ref[...]) + par_ref[2:3]
    v_ref[...] = values.astype(BF16)
    place = lax.broadcasted_iota(jnp.int32, (group, tile), 1) + pl.program_id(0) * tile
    live = jnp.where(place < live_tokens(consts, starts, lengths), 1.0, 0.0)
    row = lax.broadcasted_iota(jnp.int32, (group - size, tile), 0)
    ones = jnp.where(row == 0, live[size:], 0.0).astype(BF16)
    turned = jnp.transpose(values)
    for head in range(heads):
        part = turned[head * size : (head + 1) * size] * live[:size]
        vt_ref[pl.ds(head * group, size), :] = part.astype(BF16)
        vt_ref[pl.ds(head * group + size, group - size), :] = ones
    for pair in range(heads // 2):
        feat = features(k_ref[:, pl.ds(pair * lanes, lanes)], dirs_ref, pair, consts).astype(BF16)
        kf_ref[:, pl.ds(pair * pair_feats, pair_feats)] = feat
        for e in range(2):
            head = 2 * pair + e
            part = nn(vt_ref[pl.ds(head * group, group), :], feat[:, e * feats : (e + 1) * feats])
            add_to(sum_ref.at[pl.ds(head * size, size), :], part[:size])
            add_to(sum_ref.at[pl.ds(heads * size + head, 1), :], part[size : size + 1])


def query_kernel(consts, x_ref, wq_ref, par_ref, dirs_ref, *rest):
    q_ref, qf_ref = rest[-2:]
    q_ref[...] = (nn(x_ref[...], wq_ref[...]) + par_ref[0:1]).astype(BF16)
    for pair in range(consts.heads // 2):
        qf_ref[:, pl.ds(pair * consts.pair_feats, consts.pair_feats)] = features(
            q_ref[:, pl.ds(pair * consts.lanes, consts.lanes)], dirs_ref, pair, consts
        ).astype(BF16)


def place_sums(consts, total_ref, sums_ref):
    heads, size, feats, lanes = consts.heads, consts.size, consts.feats, consts.lanes

    @pl.when(pl.program_id(0) == 0)
    def _():
        sums_ref[...] = jnp.zeros(sums_ref.shape, BF16)
        for head in range(heads):
            pair, e = divmod(head, 2)
            cut = pl.ds(e * feats, feats)
            sums_ref[pair, pl.ds(e * size, size), cut] = total_ref[pl.ds(head * size, size), :].astype(BF16)
            if sums_ref.shape[1] > lanes:
                row = total_ref[pl.ds(heads * size + head, 1), :]
                sums_ref[pair, pl.ds(lanes + e * size, size), cut] = jnp.broadcast_to(row, (size, feats)).astype(BF16)


def centred(hidden):
    centre = hidden - jnp.mean(hidden, axis=-1, keepdims=True)
    spread = jnp.mean(centre * centre, axis=-1, keepdims=True)
    rstd = lax.rsqrt(spread + EPSILON)
    return centre * rstd, rstd


def norm_back(grad, unit, rstd):
    return rstd * (
        grad
        - jnp.mean(grad, axis=-1, keepdims=True)
        - unit * jnp.mean(grad * unit, axis=-1, keepdims=True)
    )


def forward_kernel(consts, x_ref, ct_ref, qf_ref, total_ref, wo_ref, wu_ref, wd_ref, par_ref,
                   out_ref, mix_ref, rden_ref, unit_ref, rstd_ref, low_ref, sg_ref, fg_ref, act_ref, slope_ref,
                   small_ref, sums_ref):
    lanes, pair_feats = consts.lanes, consts.pair_feats
    clear(small_ref)
    place_sums(consts, total_ref, sums_ref)
    for pair in range(consts.heads // 2):
        both = nt(qf_ref[:, pl.ds(pair * pair_feats, pair_feats)], sums_ref[pair])
        rden = 1.0 / both[:, lanes:]
        rden_ref[:, pl.ds(pair * lanes, lanes)] = rden
        mix_ref[:, pl.ds(pair * lanes, lanes)] = (both[:, :lanes] * rden).astype(BF16)
    hidden = x_ref[...].astype(F32) + (nn(mix_ref[...], wo_ref[...]) + par_ref[3:4])
    unit, rstd = centred(hidden)
    unit_ref[...] = unit
    rstd_ref[...] = jnp.broadcast_to(rstd, rstd_ref.shape)
    normed = unit * par_ref[5:6] + par_ref[6:7]
    low_ref[...] = normed.astype(BF16)
    chunk = par_ref.shape[1]
    for part in range(wu_ref.shape[1] // chunk):
        cut = pl.ds(part * chunk, chunk)
        pre = nn(low_ref[...], wu_ref[:, cut]) + par_ref[9 + part : 10 + part]
        square = pre * pre
        gate = jnp.tanh(pre * (GELU_SCALE + (GELU_SCALE * GELU_CUBE) * square))
        half = 0.5 + 0.5 * gate
        act = pre * half
        act_ref[:, cut] = act.astype(BF16)
        slope = half + act * (1.0 - gate) * (GELU_SCALE + (3.0 * GELU_SCALE * GELU_CUBE) * square)
        slope_ref[:, cut] = slope.astype(BF16)
    hidden = normed + (nn(act_ref[...], wd_ref[...]) + par_ref[4:5])
    unit, rstd = centred(hidden)
    out_ref[...] = unit * par_ref[7:8] + par_ref[8:9]
    seed = ct_ref[...].astype(F32)
    second = norm_back(seed * par_ref[7:8], unit, rstd)
    sg_ref[...] = second
    feed = second.astype(BF16)
    fg_ref[...] = feed
    parts = [
        jnp.sum(seed * unit, axis=0, keepdims=True),
        jnp.sum(seed, axis=0, keepdims=True),
        jnp.sum(feed.astype(F32), axis=0, keepdims=True),
    ]
    for row, part in enumerate(parts):
        add_to(small_ref.at[pl.ds(row, 1), :], part)


def feed_back_kernel(chunk, fg_ref, slope_ref, sg_ref, unit_ref, rstd_ref, wu_ref, wd_ref, par_ref,
                     pg_ref, rg_ref, bg_ref, small_ref, bup_ref):
    clear(small_ref, bup_ref)
    for part in range(wu_ref.shape[1] // chunk):
        cut = pl.ds(part * chunk, chunk)
        pre_grad = nt(fg_ref[...], wd_ref[cut, :]) * slope_ref[:, cut].astype(F32)
        low = pre_grad.astype(BF16)
        pg_ref[:, cut] = low
        add_to(bup_ref.at[:, cut], jnp.sum(low.astype(F32), axis=0, keepdims=True))
    normed_grad = sg_ref[...] + nt(pg_ref[...], wu_ref[...])
    unit = unit_ref[...]
    residual = norm_back(normed_grad * par_ref[5:6], unit, rstd_ref[:, :1])
    rg_ref[...] = residual
    branch = residual.astype(BF16)
    bg_ref[...] = branch
    parts = [
        jnp.sum(normed_grad * unit, axis=0, keepdims=True),
        jnp.sum(normed_grad, axis=0, keepdims=True),
        jnp.sum(branch.astype(F32), axis=0, keepdims=True),
    ]
    for row, part in enumerate(parts):
        add_to(small_ref.at[pl.ds(row, 1), :], part)


def attention_back_kernel(consts, bg_ref, mix_ref, rden_ref, qf_ref, q_ref, sd_ref, dirs_ref, wo_ref,
                          qg_ref, sum_ref, bq_ref, gt_ref):
    heads, size, feats, lanes, pair_feats = consts.heads, consts.size, consts.feats, consts.lanes, consts.pair_feats
    clear(sum_ref, bq_ref)
    attended = nt(bg_ref[...], wo_ref[...]) * rden_ref[...]
    numerator_grad = attended.astype(BF16)
    density = -attended * mix_ref[...].astype(F32)
    density_grad = density.astype(BF16)
    turned, turned_density = jnp.transpose(attended), jnp.transpose(density)
    for head in range(heads):
        gt_ref[pl.ds(head * lanes, size), :] = turned[head * size : (head + 1) * size].astype(BF16)
        gt_ref[pl.ds(head * lanes + size, size), :] = turned_density[head * size : (head + 1) * size].astype(BF16)
    for pair in range(heads // 2):
        cut = slice(pair * lanes, (pair + 1) * lanes)
        feat = qf_ref[:, pl.ds(pair * pair_feats, pair_feats)]
        grad = nn(jnp.concatenate([numerator_grad[:, cut], density_grad[:, cut]], axis=1), sd_ref[pair])
        logit_grad = (grad * feat.astype(F32)).astype(BF16)
        through = nt(logit_grad, dirs_ref[pair])
        query = q_ref[:, pl.ds(pair * lanes, lanes)].astype(F32)
        low = (consts.scale * through[:, :lanes] + through[:, lanes:] * query * (2.0 * consts.norm_ratio * consts.scale)).astype(BF16)
        qg_ref[:, pl.ds(pair * lanes, lanes)] = low
        add_to(bq_ref.at[:, pl.ds(pair * lanes, lanes)], jnp.sum(low.astype(F32), axis=0, keepdims=True))
        for e in range(2):
            head = 2 * pair + e
            part = nn(gt_ref[pl.ds(head * lanes, lanes), :], feat[:, e * feats : (e + 1) * feats])
            add_to(sum_ref.at[pl.ds(head * size, size), :], part[:size])
            add_to(sum_ref.at[pl.ds(heads * size + head, 1), :], jnp.sum(part[size:], axis=0, keepdims=True))


def key_back_kernel(consts, starts, lengths, v_ref, k_ref, kf_ref, total_ref, dirs_ref,
                    kg_ref, vg_ref, small_ref, sg_ref):
    heads, size, feats, lanes, pair_feats = consts.heads, consts.size, consts.feats, consts.lanes, consts.pair_feats
    clear(small_ref)
    place_sums(consts, total_ref, sg_ref)
    tile = v_ref.shape[0]
    row = lax.broadcasted_iota(jnp.int32, (tile, lanes), 0) + pl.program_id(0) * tile
    live = row < live_tokens(consts, starts, lengths)
    sums = [[], []]
    for pair in range(heads // 2):
        cut = pl.ds(pair * lanes, lanes)
        feat_cut = pl.ds(pair * pair_feats, pair_feats)
        feat = kf_ref[:, feat_cut]
        base = heads * size + 2 * pair
        add = jnp.concatenate([total_ref[pl.ds(base, 1), :], total_ref[pl.ds(base + 1, 1), :]], axis=1)
        grad = nn(v_ref[:, cut], sg_ref[pair]) + add
        logit_grad = (grad * feat.astype(F32)).astype(BF16)
        through = nt(logit_grad, dirs_ref[pair])
        key = k_ref[:, cut].astype(F32)
        low = consts.scale * through[:, :lanes] + through[:, lanes:] * key * (2.0 * consts.norm_ratio * consts.scale)
        low = jnp.where(live, low, 0.0).astype(BF16)
        kg_ref[:, cut] = low
        value = jnp.where(live, nt(feat, sg_ref[pair]), 0.0).astype(BF16)
        vg_ref[:, cut] = value
        sums[0].append(jnp.sum(low.astype(F32), axis=0, keepdims=True))
        sums[1].append(jnp.sum(value.astype(F32), axis=0, keepdims=True))
    for number, part in enumerate(sums):
        add_to(small_ref.at[pl.ds(number, 1), :], jnp.concatenate(part, axis=1))


def input_kernel(first_ref, *refs):
    out_ref = refs[-1]
    total = first_ref[...]
    for grad_ref, weight_ref in zip(refs[:-1:2], refs[1:-1:2]):
        total += nt(grad_ref[...], weight_ref[...])
    out_ref[...] = total


class Order:
    def __init__(self):
        self.token = jnp.zeros((1,), jnp.int32)

    def after(self, number):
        return number + self.token[0]

    def call(self, kernel, grid, ins, outs, in_specs, out_specs, deps=(), scratch=(), prefetch=0,
             exps=0, limit=60, aliases=None):
        single = not isinstance(outs, list)
        outs, out_specs = ([outs], [out_specs]) if single else (outs, out_specs)
        given, extra = len(ins), len(deps)

        def body(*refs):
            refs[given + extra + 1 + len(outs)][0] = refs[given + extra][0]
            kernel(*refs[:given], *refs[given + extra + 1 : given + extra + 1 + len(outs)],
                   *refs[given + extra + 2 + len(outs) :])

        number = pl.BlockSpec(memory_space=pltpu.SMEM)
        *results, self.token = pl.pallas_call(
            body,
            out_shape=[*outs, shape_of((1,), jnp.int32)],
            grid_spec=pltpu.PrefetchScalarGridSpec(
                num_scalar_prefetch=prefetch,
                grid=grid,
                in_specs=[*in_specs, *[ANY] * extra, number],
                out_specs=[*out_specs, number],
                scratch_shapes=scratch,
            ),
            input_output_aliases=aliases or {},
            compiler_params=pltpu.CompilerParams(vmem_limit_bytes=limit * MIB),
            cost_estimate=pl.CostEstimate(flops=1, bytes_accessed=1, transcendentals=0),
        )(*ins, *deps, self.token)
        return results[0] if single else results


def outer_tall_kernel(start, a_ref, b_ref, out_ref):
    out_ref[0] = tn(a_ref[...], b_ref[...])


def outer_tall(order, which, a, b, deps=()):
    (tokens, rows), columns, tile = a.shape, b.shape[1], 256
    count = rows // 4 // tile
    return order.call(
        outer_tall_kernel, (2 * count,), [which.reshape(1), a, b], shape_of((2, rows // 4, columns), F32),
        [pl.BlockSpec((tokens, tile), lambda i, which: (0, which[0] * 2 * count + i)), whole(b.shape)],
        pl.BlockSpec((1, tile, columns), lambda i, which: (i // count, i % count, 0)), prefetch=1, deps=deps,
    )


def turn(a_ref, turned_ref):
    @pl.when(pl.program_id(0) == 0)
    def _():
        turned_ref[...] = jnp.transpose(a_ref[...])


def outer_flat_kernel(a_ref, b_ref, *rest):
    out_ref, turned_ref = rest[-2:]
    turn(a_ref, turned_ref)
    out_ref[...] = nn(turned_ref[...], b_ref[...])


def outer_flat(order, a, b, part, given=(), deps=()):
    (tokens, rows), columns, tile = a.shape, b.shape[1], 512
    count = columns // 2 // tile
    cut = [pl.BlockSpec((n, tile), lambda i: (0, part * count + i)) for n in (tokens, rows)]
    return order.call(
        outer_flat_kernel, (count,), [a, b, *given], shape_of((rows, columns), F32),
        [whole(a.shape), cut[0], *[ANY] * len(given)], cut[1],
        scratch=[pltpu.VMEM((rows, tokens), BF16)], deps=deps, aliases={2 + n: n for n in range(len(given))},
    )


def outer_duo_kernel(which, a0_ref, b0_ref, a1_ref, b1_ref, out_ref, turned0_ref, turned1_ref):
    turn(a0_ref, turned0_ref)
    turn(a1_ref, turned1_ref)
    out_ref[0] = nn(turned0_ref[...], b0_ref[...])
    out_ref[1] = nn(turned1_ref[...], b1_ref[...])


def outer_duo(order, which, a0, b0, a1, b1, deps=()):
    (tokens, rows), columns, tile = a0.shape, b0.shape[1], 256
    left = pl.BlockSpec((tokens, rows // 2), lambda i, which: (0, which[0]), pipeline_mode=pl.Buffered(1))
    right = pl.BlockSpec((tokens, tile), lambda i, which: (0, i))
    return order.call(
        outer_duo_kernel, (columns // tile,), [which.reshape(1), a0, b0, a1, b1],
        shape_of((2, rows // 2, columns), F32), [left, right, left, right],
        pl.BlockSpec((2, rows // 2, tile), lambda i, which: (0, 0, i)),
        scratch=[pltpu.VMEM((rows // 2, tokens), BF16)] * 2, prefetch=1, deps=deps,
    )


def part_sums(order, total, tag, before):
    lead, (rows, columns) = total.shape[:-2], total.shape[-2:]
    parted = total.reshape(*lead, before, 2, rows // (2 * before), columns)
    mine = order.after(coordinate(tag))
    cuts = [lax.dynamic_index_in_dim(parted, n, parted.ndim - 3, keepdims=False) for n in (1 - mine, mine)]
    return [part.reshape(*lead, rows // 2, columns) for part in cuts]


def bits_of(axis):
    return [(axis, bit) for bit in range(lax.axis_size(axis).bit_length() - 1)]


def coordinate(tag):
    return (lax.axis_index(tag[0]) >> tag[1]) & 1


def exchange(sent, tag):
    pairs = [(i, i ^ (1 << tag[1])) for i in range(lax.axis_size(tag[0]))]
    return lax.ppermute(sent, tag[0], pairs)


def halving(order, array, tags, sequence):
    left = list(tags)
    for tag in sequence:
        where = left.index(tag)
        mine = order.after(coordinate(tag))
        sent = lax.dynamic_index_in_dim(array, 1 - mine, where, keepdims=False)
        kept = lax.dynamic_index_in_dim(array, mine, where, keepdims=False)
        received = exchange(sent, tag)
        yield sent
        array = kept + received
        left.pop(where)
    yield array


def doubling(order, block, sequence):
    for tag in reversed(sequence):
        other = exchange(block, tag)
        yield block
        mine = order.after(coordinate(tag)) == 0
        block = jnp.stack([jnp.where(mine, block, other), jnp.where(mine, other, block)])
    yield block


def summing(order, array, sequence):
    for tag in sequence:
        other = exchange(array, tag)
        yield array
        array = array + other + order.after(0).astype(F32)
    yield array


def weight_tags():
    seq, row = bits_of("seq"), bits_of("row")
    first = seq[:1] + row + seq[1:]
    second = seq[:2] + row + seq[2:]
    return first, second


def stacked_from(place):
    first, second = weight_tags()
    return first[place:] == second[place:]


def scatter_pair(order, sent, kept):
    orders = weight_tags()
    left = [list(orders[0]), list(orders[0])]
    sent, kept = [sent], [kept]
    for place in range(len(orders[0])):
        tags = [orders[n][place] for n in range(len(kept))]
        received = [exchange(part, tag) for part, tag in zip(sent, tags)]
        for names, number in zip(left, orders):
            names.remove(number[place])
        yield sent
        totals = [stay + came for stay, came in zip(kept, received)]
        if place + 1 == len(orders[0]):
            yield totals[0] + order.after(0).astype(F32)
            return
        if stacked_from(place + 1):
            totals = totals if len(totals) == 1 else [jnp.stack(totals)]
        elif len(totals) == 1:
            totals = [totals[0][0], totals[0][1]]
        tags = [orders[n][place + 1] for n in range(len(totals))]
        befores = [1 << names.index(tag) for names, tag in zip(left, tags)]
        parts = [part_sums(order, *given) for given in zip(totals, tags, befores)]
        sent, kept = [part[0] for part in parts], [part[1] for part in parts]


def gather_pair(order, block):
    orders = weight_tags()
    held = [block]
    have = [[], []]
    for place in reversed(range(len(orders[0]))):
        if place and not stacked_from(place) and len(held) == 1:
            held = [held[0][0], held[0][1]]
        tags = [orders[n][place] for n in range(len(held))]
        others = [exchange(part, tag) for part, tag in zip(held, tags)]
        yield held
        whole_now = []
        for n, (part, other, tag) in enumerate(zip(held, others, tags)):
            mine = order.after(coordinate(tag)) == 0
            before = 1 << sum(orders[0].index(name) < orders[0].index(tag) for name in have[n])
            lead, (rows, columns) = part.shape[:-2], part.shape[-2:]
            shape = (*lead, before, rows // before, columns)
            part, other = part.reshape(shape), other.reshape(shape)
            both = jnp.stack([jnp.where(mine, part, other), jnp.where(mine, other, part)], axis=len(lead) + 1)
            whole_now.append(both.reshape(*lead, 2 * rows, columns))
        for names, number in zip(have, orders):
            names.append(number[place])
        held = whole_now
    yield held


def gather_blocks(block):
    whole = lax.all_gather(block, ("seq", "row"), axis=0, tiled=False)
    seq, row = bits_of("seq"), bits_of("row")
    tags = seq[::-1] + row[::-1]
    first, _ = weight_tags()
    whole = whole.reshape((2,) * len(tags) + block.shape)
    places = [tags.index(tag) for tag in first]
    rest = list(range(len(tags), len(tags) + block.ndim))
    return whole.transpose(places + rest)


def bucket_sum(order, onehot, shared, part):
    tags = bits_of("seq")
    padded, features = part.shape
    slots = onehot[:shared].reshape(1, shared, 1, 1)
    blocks = part.reshape(1 << len(tags), 1, padded >> len(tags), features) * slots
    blocks = blocks.reshape((2,) * len(tags) + blocks.shape[1:])
    steps = halving(order, blocks, tags, tags)
    for _ in tags:
        yield next(steps)
    steps = doubling(order, next(steps), tags)
    for _ in tags:
        yield next(steps)
    summed = next(steps)
    summed = jnp.sum(summed.reshape((1 << len(tags),) + summed.shape[len(tags) :]) * slots, axis=1)
    alone = 1.0 - jnp.sum(onehot[:shared])
    yield summed.reshape(padded, features) + alone * part


def on_device(
    inputs, w_query, w_key, w_value, w_out, w_up, w_down, b_query, b_key, b_value, b_out, b_up, b_down,
    norm1_gain, norm1_shift, norm2_gain, norm2_shift, head_feature_directions, seq_lengths, seq_starts, cotangent,
):
    tokens, width = inputs.shape[1:]
    ff = w_up.shape[1]
    heads, feats, size = head_feature_directions.shape
    pairs, lanes, pair_feats, all_feats = heads // 2, 2 * size, 2 * feats, heads * feats
    scale = size ** (-0.25)
    blocks = lax.axis_size("seq")
    widths = [5 * blocks // 8, blocks // 8] + [blocks // 16] * 4
    consts = Consts(scale, 0.5 / math.sqrt(size) / scale, 0.5 * math.log(feats), heads, size, feats, lanes, pair_feats,
                    tokens, tuple(widths))
    shared = sum(count > 1 for count in widths)
    block_start = lax.axis_index("seq") * tokens
    starts, lengths = seq_starts.reshape(-1), seq_lengths.reshape(-1)
    limits = jnp.array(widths, jnp.int32) * tokens
    onehot = ((starts <= block_start) & (block_start < starts + limits)).astype(F32)
    core = coordinate(("seq", 0))
    count = 2 * len(bits_of("seq"))
    unit = 8 << len(bits_of("seq"))
    sum_rows = -(-(width + heads) // unit) * unit

    params = jnp.concatenate(
        [b_query, b_key, b_value, b_out, b_down, norm1_gain, norm1_shift, norm2_gain, norm2_shift, b_up]
    ).astype(F32).reshape(-1, width)
    x, ct = inputs[0], cotangent[0]
    order = Order()

    def step(*parts):
        arrays = []
        for part in parts:
            given = next(part)
            arrays.extend(given if isinstance(given, list) else [given])
        return arrays

    def finish(part):
        return list(part)[-1]

    tile = 512
    steps = tokens // tile
    narrow, broad = rows_of(tile, width), rows_of(tile, all_feats)
    square, param_spec = whole((width, width)), whole(params.shape)
    sums_shape, dirs_shape = (sum_rows, feats), (pairs, 2 * lanes, pair_feats)
    dirs_spec, sums_spec, total_spec = whole(dirs_shape), whole(dirs_shape), whole(sums_shape)
    f32_rows, bf16_rows = shape_of((tokens, width), F32), shape_of((tokens, width), BF16)
    feat_rows, ff_rows = shape_of((tokens, all_feats), BF16), shape_of((tokens, ff), BF16)
    keys, values, key_feat, key_sum, dirs = order.call(
        functools.partial(key_kernel, consts), (steps,),
        [starts, lengths, x, w_key, w_value, params, head_feature_directions],
        [bf16_rows, bf16_rows, feat_rows, shape_of(sums_shape, F32), shape_of(dirs_shape, BF16)],
        [narrow, square, square, param_spec, whole(head_feature_directions.shape)],
        [narrow, narrow, broad, summed(sums_shape), summed(dirs_shape)],
        scratch=[pltpu.VMEM((heads * (size + 16), tile), BF16)], prefetch=2,
    )
    total = bucket_sum(order, onehot, shared, key_sum)

    def query_half(first, given, deps):
        cut = [pl.BlockSpec((tile, n), lambda i: (i + first, 0)) for n in (width, all_feats)]
        return order.call(
            functools.partial(query_kernel, consts), (steps // 2,),
            [x, w_query, params, dirs, *given], [bf16_rows, feat_rows],
            [cut[0], square, param_spec, dirs_spec, *[ANY] * len(given)], cut, deps=deps,
            aliases={4 + n: n for n in range(len(given))},
        )

    step(total)
    given = query_half(0, [], step(total))
    for _ in range(count - 4):
        step(total)
    queries, query_feat = query_half(steps // 2, given, step(total))
    total = finish(total)

    tile = 256
    steps = tokens // tile
    narrow, broad, long = rows_of(tile, width), rows_of(tile, all_feats), rows_of(tile, ff)
    thin = rows_of(tile, 128)
    up_spec, down_spec = whole((width, ff)), whole((ff, width))
    (result, mixture, rden, unit, rstd, normed_low, second, feed, active, slope, small_forward, sums) = order.call(
        functools.partial(forward_kernel, consts), (steps,),
        [x, ct, query_feat, total, w_out, w_up, w_down, params],
        [f32_rows, bf16_rows, f32_rows, f32_rows, shape_of((tokens, 128), F32), bf16_rows, f32_rows, bf16_rows,
         ff_rows, ff_rows, shape_of((3, width), F32), shape_of(dirs_shape, BF16)],
        [narrow, narrow, broad, total_spec, square, up_spec, down_spec, param_spec],
        [narrow, narrow, narrow, narrow, thin, narrow, narrow, narrow, long, long, summed((3, width)),
         summed(dirs_shape)],
    )

    everyone = ("seq", "row")
    down = scatter_pair(
        order, outer_tall(order, 1 - core, active, feed), outer_tall(order, core, active, feed)
    )
    step(down)
    pre_grad, residual, branch, small_back, grad_bup = order.call(
        functools.partial(feed_back_kernel, 512), (steps,),
        [feed, slope, second, unit, rstd, w_up, w_down, params],
        [ff_rows, f32_rows, bf16_rows, shape_of((3, width), F32), shape_of((1, ff), F32)],
        [narrow, long, narrow, narrow, thin, up_spec, down_spec, param_spec],
        [long, narrow, narrow, summed((3, width)), summed((1, ff))],
        deps=step(down),
    )
    query_grad, query_sum, grad_bquery = order.call(
        functools.partial(attention_back_kernel, consts), (steps,),
        [branch, mixture, rden, query_feat, queries, sums, dirs, w_out],
        [bf16_rows, shape_of(sums_shape, F32), shape_of((1, width), F32)],
        [narrow, narrow, narrow, broad, narrow, sums_spec, dirs_spec, square],
        [narrow, summed(sums_shape), summed((1, width))],
        scratch=[pltpu.VMEM((heads * lanes, tile), BF16)],
        deps=step(down),
    )
    small = jnp.concatenate([small_forward, small_back, grad_bquery, grad_bup.reshape(-1, width)])
    small = summing(order, small, weight_tags()[0])
    total = bucket_sum(order, onehot, shared, query_sum)
    step(total)
    grad_up = outer_flat(order, normed_low, pre_grad, 0, (), step(total) + step(down) + step(small))
    grad_up = outer_flat(order, normed_low, pre_grad, 1, (grad_up,), step(total) + step(down) + step(small))
    whole_up = lax.psum(grad_up, everyone)
    down = gather_blocks(finish(down))
    first_sent = outer_duo(order, 1 - core, mixture, branch, x, query_grad, step(total) + step(small))
    first_kept = outer_duo(order, core, mixture, branch, x, query_grad, step(total) + step(small))
    first = scatter_pair(order, first_sent, first_kept)
    step(first)
    for _ in range(count - 7):
        step(total)

    tile = 512
    steps = tokens // tile
    narrow, broad = rows_of(tile, width), rows_of(tile, all_feats)
    partial_input = order.call(
        input_kernel, (steps,), [residual, query_grad, w_query], f32_rows, [narrow, narrow, square], narrow,
        deps=step(total) + step(first) + step(small),
    )
    small = finish(small)
    total = finish(total)
    key_grad, value_grad, small_key = order.call(
        functools.partial(key_back_kernel, consts), (steps,),
        [starts, lengths, values, keys, key_feat, total, dirs],
        [bf16_rows, bf16_rows, shape_of((2, width), F32)],
        [narrow, narrow, broad, total_spec, dirs_spec],
        [narrow, narrow, summed((2, width))], prefetch=2,
        scratch=[pltpu.VMEM((pairs, lanes, pair_feats), BF16)],
        deps=step(first),
    )
    late = summing(order, small_key, weight_tags()[0])
    last_sent = outer_duo(order, 1 - core, x, key_grad, x, value_grad, step(first) + step(late))
    last_kept = outer_duo(order, core, x, key_grad, x, value_grad, step(first) + step(late))
    first = gather_pair(order, finish(first))
    last = scatter_pair(order, last_sent, last_kept)
    step(last)
    input_grad = order.call(
        input_kernel, (steps,), [partial_input, key_grad, w_key, value_grad, w_value], f32_rows,
        [narrow, narrow, square, narrow, square], narrow,
        deps=step(first) + step(last) + step(late),
    )
    last = gather_pair(order, finish(last))
    first, last, late = [finish(part) for part in (first, last, late)]
    first, last = [[chunk.reshape(width, width) for chunk in pair] for pair in
                   [pair if len(pair) == 2 else [pair[0][0], pair[0][1]] for pair in (first, last)]]

    bits = down.ndim - 3
    whole_down = jnp.moveaxis(down, bits, 1).reshape(ff, width)
    return (
        result[None], input_grad[None],
        first[1], last[0], last[1], first[0],
        whole_up, whole_down,
        small[6], late[0], late[1], small[5], small[7:].reshape(ff), small[2],
        small[3], small[4], small[0], small[1],
    )


def solution(mesh):
    tokens = P("row", "seq", None)
    bucket = P("row", None)
    return jax.shard_map(
        on_device,
        mesh=mesh,
        in_specs=(tokens,) + (P(),) * 17 + (bucket, bucket, tokens),
        out_specs=(tokens, tokens) + (P(),) * 16,
        check_vma=False,
    )
```

time: 1570 us -> 693 us (0.44)
  waiting for transfers between devices: 998 us -> 204 us
  matrix products: 321 us -> 0 us
  Pallas kernels: 0 us -> 269 us
  local copies, waits for them, and re-layouts: 184 us -> 46.9 us
  starting transfers between devices: 0.38 us -> 64.8 us
  between operations: 15 us -> 42.8 us
    unnamed x6 -> x2, waiting for transfers between devices: 840 us -> 0.03 us
    dot_general x30 -> x0, matrix products: 321 us -> none  [the longest x1 34.1 us: on_device(): jnp.einsum('td,fd->tf', feed_grad, w_down, preferred_element_type=jnp.flo...]
    pallas_call x0 -> x17, Pallas kernels: none -> 269 us  [call(): pl.pallas_call(body, out_shape=[*outs, shape_of((1,), jnp.int32)], grid_s...]
    ppermute x0 -> x63, waiting for transfers between devices: none -> 165 us  [exchange(): return lax.ppermute(sent, tag[0], pairs)]
    psum x2 -> x1, waiting for transfers between devices: 158 us -> 39.3 us  [on_device(): whole_up = lax.psum(grad_up, everyone)]
    unnamed x178 -> x101, local copies, waits for them, and re-layouts: 96 us -> 24.2 us
    ppermute x0 -> x63, starting transfers between devices: none -> 64.8 us  [exchange(): return lax.ppermute(sent, tag[0], pairs)]
    slice x9 -> x6, local copies, waits for them, and re-layouts: 46.9 us -> 1.89 us  [the longest x1 0.65 us: on_device(): small[1]]
  transfers between devices with their start and end apart: 4 -> 65, of which waited for: 4 -> 30; matrix products, arithmetic and copies ran while one was open for 7% -> 9% of each run, Pallas kernels for 0% -> 26%
where the time goes in v2:
time: 693 us; the launch traced here: 683 us
  Pallas kernels  269 us (39%)
  waiting for transfers between devices  204 us (29%)
  starting transfers between devices  64.8 us (9%)
  other arithmetic  54.7 us (8%)
  local copies, waits for them, and re-layouts  46.9 us (7%)
  between operations  42.8 us (6%)
    pallas_call x17, Pallas kernels, call(): pl.pallas_call(body, out_shape=[*outs, shape_of((1,), jnp.int32)], grid_s...  269 us
    ppermute x63, waiting for transfers between devices, exchange(): return lax.ppermute(sent, tag[0], pairs)  165 us
    ppermute x63, starting transfers between devices, exchange(): return lax.ppermute(sent, tag[0], pairs)  64.8 us
    psum x1, waiting for transfers between devices, on_device(): whole_up = lax.psum(grad_up, everyone)  39.3 us
    unnamed x101, local copies, waits for them, and re-layouts  24.2 us
    add x18, other arithmetic, scatter_pair(): totals = [stay + came for stay, came in zip(kept, received)]  22.1 us
  transfers between devices with their start and end apart: 65, of which 30 were waited for; matrix products, arithmetic and copies ran while one was open for 9% of the time, Pallas kernels for 26%

profile of v2, /device:TPU:0, one launch (start us, length us, event | category | flops | bytes accessed | tf_op | source)
XLA Modules:
  0.0 682.6 jit_solution(15661277863077457751)
XLA Ops:
  18.6 20.1 %shard_map.349 = (bf16[2048,768]{1,0:T(8,128)(2,1)}, bf16[2048,768]{1,0:T(8,128)(2,1)}, bf16[2048,3072]{1,0:T(8,128)(2,1)}, f32[896,256]{1,0:T(8,128)}, bf16[6,256,512]{2,1,0:T(8,128)(2,1)}, /*index=5*/s32[1]{0:T(128)}) custom-call(s32[6]{0:T(128)} %bitcast.412, s32[6]{0:T(128)} %bitcast.414, bf16[2048,768]{1,0:T(8,128)(2,1)} %bitcast.330, ...), custom_call_target="tpu_custom_call" | custom-call | flops 1 | bytes 1 | tf_op jit(solution)/shard_map/pallas_call | solution.py:327
  45.1 3.0 collective-permute-start.1
  48.1 8.5 %shard_map.350 = (bf16[2048,768]{1,0:T(8,128)(2,1)}, bf16[2048,3072]{1,0:T(8,128)(2,1)}, s32[1]{0:T(128)}) custom-call(bf16[2048,768]{1,0:T(8,128)(2,1)} %bitcast.331, bf16[768,768]{1,0:T(8,128)(2,1)} %refs_2_.2, f32[13,768]{1,0:T(8,128)} %reshape.549.refs_5_.refs_2_.refs_7_, bf16[6,256,512]{2,1,0:T(8,128)(2,1)} %get-tuple-element.77.refs_3_.refs_6_, ...), custom_call_target="tpu_custom_call" | custom-call | flops 1 | bytes 1 | tf_op jit(solution)/shard_map/pallas_call | solution.py:327
  61.5 4.7 collective-permute-done.2
  66.2 2.6 collective-permute-start.3
  68.8 4.6 collective-permute-done.3
  74.7 4.5 collective-permute-done.4
  79.3 3.3 collective-permute-start.5
  82.5 4.0 collective-permute-done.5
  88.2 8.5 %shard_map.351 = (bf16[2048,768]{1,0:T(8,128)(2,1)}, bf16[2048,3072]{1,0:T(8,128)(2,1)}, s32[1]{0:T(128)}) custom-call(bf16[2048,768]{1,0:T(8,128)(2,1)} %bitcast.332, bf16[768,768]{1,0:T(8,128)(2,1)} %refs_2_.2, f32[13,768]{1,0:T(8,128)} %reshape.549.refs_5_.refs_2_.refs_7_, ...), custom_call_target="tpu_custom_call", output_to_operand_aliasing={{0}: (4, {}), {1}: (5, {})} | custom-call | flops 1 | bytes 1 | tf_op jit(solution)/shard_map/pallas_call | solution.py:327
  102.4 59.3 %shard_map.352 = (f32[2048,768]{1,0:T(8,128)}, bf16[2048,768]{1,0:T(8,128)(2,1)}, f32[2048,768]{1,0:T(8,128)}, f32[2048,768]{1,0:T(8,128)}, f32[2048,128]{1,0:T(...) custom-call(bf16[2048,768]{1,0:T(8,128)(2,1)} %bitcast.333, ...), custom_call_target="tpu_custom_call" | custom-call | flops 1 | bytes 1 | tf_op jit(solution)/shard_map/pallas_call | solution.py:327
  161.7 11.2 %shard_map.353 = (f32[2,768,768]{2,1,0:T(8,128)}, s32[1]{0:T(128)}) custom-call(s32[1]{0:T(128)} %bitcast.27.refs_0_, bf16[2048,3072]{1,0:T(8,128)(2,1)} %get-tuple-element.91.refs_1_, bf16[2048,768]{1,0:T(8,128)(2,1)} %get-tuple-element.86.refs_2_.refs_0_, s32[1]{0:T(128)} %get-tuple-element.92.refs_3_), custom_call_target="tpu_custom_call" | custom-call | flops 1 | bytes 1 | tf_op jit(solution)/shard_map/pallas_call | solution.py:327
  173.0 11.2 %shard_map.354 = (f32[2,768,768]{2,1,0:T(8,128)}, s32[1]{0:T(128)}) custom-call(s32[1]{0:T(128)} %bitcast.26.refs_0_, bf16[2048,3072]{1,0:T(8,128)(2,1)} %get-tuple-element.91.refs_1_, bf16[2048,768]{1,0:T(8,128)(2,1)} %get-tuple-element.86.refs_2_.refs_0_, s32[1]{0:T(128)} %get-tuple-element.93.refs_3_), custom_call_target="tpu_custom_call" | custom-call | flops 1 | bytes 1 | tf_op jit(solution)/shard_map/pallas_call | solution.py:327
  184.9 4.4 add.530
  196.4 32.3 %shard_map.355 = (bf16[2048,3072]{1,0:T(8,128)(2,1)}, f32[2048,768]{1,0:T(8,128)}, bf16[2048,768]{1,0:T(8,128)(2,1)}, f32[3,768]{1,0:T(4,128)}, f32[1,3072]{1,0:T(1,128)}, /*index=5*/s32[1]{0:T(128)}) custom-call(bf16[2048,768]{1,0:T(8,128)(2,1)} %get-tuple-element.86.refs_2_.refs_0_, bf16[2048,3072]{1,0:T(8,128)(2,1)} %get-tuple-element.87.refs_1_, ...), custom_call_target="tpu_custom_call" | custom-call | flops 1 | bytes 1 | tf_op jit(solution)/shard_map/pallas_call | solution.py:327
  236.2 21.4 %shard_map.356 = (bf16[2048,768]{1,0:T(8,128)(2,1)}, f32[896,256]{1,0:T(8,128)}, f32[1,768]{1,0:T(1,128)}, s32[1]{0:T(128)}) custom-call(bf16[2048,768]{1,0:T(8,128)(2,1)} %get-tuple-element.98.refs_0_.refs_2_, bf16[2048,768]{1,0:T(8,128)(2,1)} %get-tuple-element.99.refs_1_, f32[2048,768]{1,0:T(8,128)} %get-tuple-element.100.refs_2_, ...), custom_call_target="tpu_custom_call" | custom-call | flops 1 | bytes 1 | tf_op jit(solution)/shard_map/pallas_call | solution.py:327
  272.8 11.0 %shard_map.357 = (f32[768,3072]{1,0:T(8,128)}, s32[1]{0:T(128)}) custom-call(bf16[2048,768]{1,0:T(8,128)(2,1)} %get-tuple-element.107.refs_0_, bf16[2048,3072]{1,0:T(8,128)(2,1)} %get-tuple-element.108.refs_1_, f32[2,2,2,56,256]{4,3,2,1,0:T(8,128)} %copy-done.21, f32[2,96,768]{2,1,0:T(8,128)} %fusion.6.refs_3_, f32[11,768]{1,0:T(8,128)} %copy-done.34, ...), custom_call_target="tpu_custom_call" | custom-call | flops 1 | bytes 1 | tf_op jit(solution)/shard_map/pallas_call | solution.py:327
  292.5 11.1 %shard_map.358 = (f32[768,3072]{1,0:T(8,128)}, s32[1]{0:T(128)}) custom-call(bf16[2048,768]{1,0:T(8,128)(2,1)} %get-tuple-element.107.refs_0_, bf16[2048,3072]{1,0:T(8,128)(2,1)} %get-tuple-element.108.refs_1_, f32[768,3072]{1,0:T(8,128)} %get-tuple-element.114.refs_2_, ...), custom_call_target="tpu_custom_call", output_to_operand_aliasing={{0}: (2, {})} | custom-call | flops 1 | bytes 1 | tf_op jit(solution)/shard_map/pallas_call | solution.py:327
  309.8 3.8 collective-permute-done.15
  314.3 9.1 %shard_map.359 = (f32[2,384,768]{2,1,0:T(8,128)}, s32[1]{0:T(128)}) custom-call(s32[1]{0:T(128)} %bitcast.27.refs_0_, bf16[2048,768]{1,0:T(8,128)(2,1)} %get-tuple-element.99.refs_1_, bf16[2048,768]{1,0:T(8,128)(2,1)} %get-tuple-element.98.refs_0_.refs_2_, bf16[2048,768]{1,0:T(8,128)(2,1)} %bitcast.334, ...), custom_call_target="tpu_custom_call" | custom-call | flops 1 | bytes 1 | tf_op jit(solution)/shard_map/pallas_call | solution.py:327
  325.6 6.5 collective-permute-done.18
  332.8 8.9 %shard_map.360 = (f32[2,384,768]{2,1,0:T(8,128)}, s32[1]{0:T(128)}) custom-call(s32[1]{0:T(128)} %bitcast.26.refs_0_, bf16[2048,768]{1,0:T(8,128)(2,1)} %get-tuple-element.99.refs_1_, bf16[2048,768]{1,0:T(8,128)(2,1)} %get-tuple-element.98.refs_0_.refs_2_, bf16[2048,768]{1,0:T(8,128)(2,1)} %bitcast.335, ...), custom_call_target="tpu_custom_call" | custom-call | flops 1 | bytes 1 | tf_op jit(solution)/shard_map/pallas_call | solution.py:327
  349.6 6.6 collective-permute-done.22
  364.0 9.5 %shard_map.361 = (f32[2048,768]{1,0:T(8,128)}, s32[1]{0:T(128)}) custom-call(f32[2048,768]{1,0:T(8,128)} %get-tuple-element.97.refs_0_, bf16[2048,768]{1,0:T(8,128)(2,1)} %get-tuple-element.104.refs_4_.refs_1_, bf16[768,768]{1,0:T(8,128)(2,1)} %refs_2_.2, f32[2,2,2,56,256]{4,3,2,1,0:T(8,128)} %copy-done.20, f32[192,768]{1,0:T(8,128)} %copy-done.11, ...), custom_call_target="tpu_custom_call" | custom-call | flops 1 | bytes 1 | tf_op jit(solution)/shard_map/pallas_call | solution.py:327
  374.2 3.2 collective-permute-done.25
  380.3 17.9 %collective-permute-done.28 = f32[192,768]{1,0:T(8,128)} collective-permute-done((f32[192,768]{1,0:T(8,128)S(1)}, f32[192,768]{1,0:T(8,128)}, u32[]{:S(2)}, u32[]{:S(2)}) %collective-permute-start.28) | collective-permute-done | bytes 589856 | tf_op jit(solution)/shard_map/ppermute | solution.py:418
  404.3 4.2 collective-permute-done.30
  414.9 16.9 %shard_map.362 = (bf16[2048,768]{1,0:T(8,128)(2,1)}, bf16[2048,768]{1,0:T(8,128)(2,1)}, f32[2,768]{1,0:T(2,128)}, s32[1]{0:T(128)}) custom-call(s32[6]{0:T(128)} %bitcast.413, s32[6]{0:T(128)} %bitcast.415, bf16[2048,768]{1,0:T(8,128)(2,1)} %get-tuple-element.121.refs_2_, bf16[2048,768]{1,0:T(8,128)(2,1)} %get-tuple-element.122.refs_3_, ...), custom_call_target="tpu_custom_call" | custom-call | flops 1 | bytes 1 | tf_op jit(solution)/shard_map/pallas_call | solution.py:327
  433.2 8.9 %shard_map.363 = (f32[2,384,768]{2,1,0:T(8,128)}, s32[1]{0:T(128)}) custom-call(s32[1]{0:T(128)} %bitcast.27.refs_0_, bf16[2048,768]{1,0:T(8,128)(2,1)} %bitcast.336, bf16[2048,768]{1,0:T(8,128)(2,1)} %get-tuple-element.125.refs_2_.refs_1_, bf16[2048,768]{1,0:T(8,128)(2,1)} %bitcast.337, bf16[2048,768]{1,0:T(8,128)(2,1)} %get-tuple-element.126.refs_4_.refs_3_, ...), custom_call_target="tpu_custom_call" | custom-call | flops 1 | bytes 1 | tf_op jit(solution)/shard_map/pallas_call | solution.py:327
  444.6 3.6 collective-permute-done.59
  452.9 11.2 %collective-permute-done.31 = f32[2,48,768]{2,1,0:T(8,128)S(1)} collective-permute-done((f32[2,48,768]{2,1,0:T(8,128)S(1)}, f32[2,48,768]{2,1,0:T(8,128)S(1)}, u32[]{:S(2)}, u32[]{:S(2)}) %collective-permute-start.31) | collective-permute-done | bytes 294944 | tf_op jit(solution)/shard_map/ppermute | solution.py:418
  464.8 9.4 %shard_map.364 = (f32[2,384,768]{2,1,0:T(8,128)}, s32[1]{0:T(128)}) custom-call(s32[1]{0:T(128)} %bitcast.26.refs_0_, bf16[2048,768]{1,0:T(8,128)(2,1)} %bitcast.338, bf16[2048,768]{1,0:T(8,128)(2,1)} %get-tuple-element.125.refs_2_.refs_1_, bf16[2048,768]{1,0:T(8,128)(2,1)} %bitcast.339, bf16[2048,768]{1,0:T(8,128)(2,1)} %get-tuple-element.126.refs_4_.refs_3_, ...), custom_call_target="tpu_custom_call" | custom-call | flops 1 | bytes 1 | tf_op jit(solution)/shard_map/pallas_call | solution.py:327
  479.6 9.7 %collective-permute-done.32 = f32[2,24,768]{2,1,0:T(8,128)S(1)} collective-permute-done((f32[2,24,768]{2,1,0:T(8,128)S(1)}, f32[2,24,768]{2,1,0:T(8,128)S(1)}, u32[]{:S(2)}, u32[]{:S(2)}) %collective-permute-start.32) | collective-permute-done | bytes 147488 | tf_op jit(solution)/shard_map/ppermute | solution.py:418
  494.1 11.8 %shard_map.365 = (f32[2048,768]{1,0:T(8,128)}, s32[1]{0:T(128)}) custom-call(f32[2048,768]{1,0:T(8,128)} %get-tuple-element.120.refs_0_, bf16[2048,768]{1,0:T(8,128)(2,1)} %get-tuple-element.125.refs_2_.refs_1_, bf16[768,768]{1,0:T(8,128)(2,1)} %refs_2_.3, bf16[2048,768]{1,0:T(8,128)(2,1)} %get-tuple-element.126.refs_4_.refs_3_, bf16[768,768]{1,0:T(8,128)(2,1)} %refs_4_.5, ...), custom_call_target="tpu_custom_call" | custom-call | flops 1 | bytes 1 | tf_op jit(solution)/shard_map/pallas_call | solution.py:327
  511.3 3.6 collective-permute-start.61
  518.0 14.2 %collective-permute-done.41 = f32[192,768]{1,0:T(8,128)} collective-permute-done((f32[192,768]{1,0:T(8,128)S(1)}, f32[192,768]{1,0:T(8,128)}, u32[]{:S(2)}, u32[]{:S(2)}) %collective-permute-start.41) | collective-permute-done | bytes 589856 | tf_op jit(solution)/shard_map/ppermute | solution.py:418
  534.3 3.5 collective-permute-start.62
  537.9 2.3 collective-permute-done.42
  540.3 4.1 collective-permute-start.45
  544.4 7.8 %collective-permute-done.45 = f32[2,48,768]{2,1,0:T(8,128)S(1)} collective-permute-done((f32[2,48,768]{2,1,0:T(8,128)S(1)}, f32[2,48,768]{2,1,0:T(8,128)S(1)}, u32[]{:S(2)}, u32[]{:S(2)}) %collective-permute-start.45) | collective-permute-done | bytes 294944 | tf_op jit(solution)/shard_map/ppermute | solution.py:418
  555.3 7.4 %collective-permute-done.46 = f32[2,24,768]{2,1,0:T(8,128)S(1)} collective-permute-done((f32[2,24,768]{2,1,0:T(8,128)S(1)}, f32[2,24,768]{2,1,0:T(8,128)S(1)}, u32[]{:S(2)}, u32[]{:S(2)}) %collective-permute-start.46) | collective-permute-done | bytes 147488 | tf_op jit(solution)/shard_map/ppermute | solution.py:418
  563.5 6.5 collective-permute-done.47
  571.5 8.2 %collective-permute-done.48 = f32[2,48,768]{2,1,0:T(8,128)S(1)} collective-permute-done((f32[2,48,768]{2,1,0:T(8,128)S(1)}, f32[2,48,768]{2,1,0:T(8,128)S(1)}, u32[]{:S(2)}, u32[]{:S(2)}) %collective-permute-start.48) | collective-permute-done | bytes 294944 | tf_op jit(solution)/shard_map/ppermute | solution.py:418
  581.2 5.4 collective-permute-done.52
  592.1 16.3 %collective-permute-done.53 = f32[192,768]{1,0:T(8,128)S(1)} collective-permute-done((f32[192,768]{1,0:T(8,128)S(1)}, f32[192,768]{1,0:T(8,128)S(1)}, u32[]{:S(2)}, u32[]{:S(2)}) %collective-permute-start.53) | collective-permute-done | bytes 589856 | tf_op jit(solution)/shard_map/ppermute | solution.py:418
  617.7 9.7 %copy.113 = f32[2,2,2,2,2,2,48,768]{7,6,5,4,3,2,1,0:T(8,128)} copy(f32[2,2,2,2,2,2,48,768]{7,6,1,2,0,3,4,5:T(8,128)} %bitcast.340) | data formatting | bytes 18874368 | tf_op jit(solution)/shard_map/transpose;transpose | solution.py:702
  627.4 39.3 %all-reduce.2.cloned.1.call-done = f32[768,3072]{1,0:T(8,128)} async-done(((f32[768,3072]{1,0:T(8,128)}), f32[768,3072]{1,0:T(8,128)}) %all-reduce.2.cloned.1.call-update) | async-done | bytes 9437200 | tf_op jit(solution)/shard_map/psum | solution.py:658
  666.7 8.7 %copy.138 = f32[768,3072]{1,0:T(8,128)} copy(f32[768,3072]{1,0:T(8,128)} %all-reduce.2.cloned.1.call-done) | data formatting | bytes 18874368
  (338 shorter events, 136.5 us)
Async XLA Ops:
  7.2 610.5 %all-gather.3.cloned.1.call-start = ((), (), s32[]{:S(2)}) async-start(), calls=%async_computation.1 | async-start | bytes 9732096 | tf_op jit(solution)/shard_map/all_gather | solution.py:514
  45.1 13.8 %collective-permute-start.1 = (f32[2,2,2,56,256]{4,3,2,1,0:T(8,128)S(1)}, f32[2,2,2,56,256]{4,3,2,1,0:T(8,128)S(1)}, u32[]{:S(2)}, u32[]{:S(2)}) collective-permute-start(f32[2,2,2,56,256]{4,3,2,1,0:T(8,128)S(1)} %dynamic-slice_bitcast_fusion.8.refs_4_), channel_id=1, source_target_pairs={{0,4},{2,6},{4,0},{6,2},{8,12},{10,14},{12,8},{14,10},{16,20},{18,... | collective-permute-start | bytes 1376264 | tf_op jit(solution)/shard_map/ppermute | solution.py:418
  86.6 10.7 %collective-permute-start.6 = (f32[2,2,2,56,256]{4,3,2,1,0:T(8,128)S(1)}, f32[2,2,2,56,256]{4,3,2,1,0:T(8,128)S(1)}, u32[]{:S(2)}, u32[]{:S(2)}) collective-permute-start(f32[2,2,2,56,256]{4,3,2,1,0:T(8,128)S(1)} %pad_maximum_fusion.14.refs_6_), channel_id=1, source_target_pairs={{0,4},{2,6},{4,0},{6,2},{8,12},{10,14},{12,8},{14,10},{16,20},{18,... | collective-permute-start | bytes 1376264 | tf_op jit(solution)/shard_map/ppermute | solution.py:418
  172.9 11.9 %collective-permute-start.8 = (f32[2,768,768]{2,1,0:T(8,128)}, f32[2,768,768]{2,1,0:T(8,128)}, u32[]{:S(2)}, u32[]{:S(2)}) collective-permute-start(f32[2,768,768]{2,1,0:T(8,128)} %get-tuple-element.95), channel_id=1, source_target_pairs={{0,2},{2,0},{4,6},{6,4},{8,10},{10,8},{12,14},{14,12},{16,18},{18,... | collective-permute-start | bytes 14155784 | tf_op jit(solution)/shard_map/ppermute | solution.py:418
  192.1 38.0 %collective-permute-start.9 = (f32[384,768]{1,0:T(8,128)}, f32[384,768]{1,0:T(8,128)}, u32[]{:S(2)}, u32[]{:S(2)}) collective-permute-start(f32[384,768]{1,0:T(8,128)} %dynamic-slice_bitcast_fusion.refs_8_), channel_id=1, source_target_pairs={{0,1},{1,0},{2,3},{3,2},{4,5},{5,4},{6,7},{7,6},{8,9},{9,8},{10,11... | collective-permute-start | bytes 3538952 | tf_op jit(solution)/shard_map/ppermute | solution.py:418
  195.4 36.2 %collective-permute-start.10 = (f32[384,768]{1,0:T(8,128)S(1)}, f32[384,768]{1,0:T(8,128)}, u32[]{:S(2)}, u32[]{:S(2)}) collective-permute-start(f32[384,768]{1,0:T(8,128)S(1)} %bitcast.349), channel_id=1, source_target_pairs={{0,4},{2,6},{4,0},{6,2},{8,12},{10,14},{12,8},{14,10},{16,20},{18,... | collective-permute-start | bytes 3538952 | tf_op jit(solution)/shard_map/ppermute | solution.py:418
  234.6 29.4 %collective-permute-start.14 = (f32[192,768]{1,0:T(8,128)S(1)}, f32[192,768]{1,0:T(8,128)}, u32[]{:S(2)}, u32[]{:S(2)}) collective-permute-start(f32[192,768]{1,0:T(8,128)S(1)} %get-tuple-element.209.refs_9_), channel_id=1, source_target_pairs={{0,1},{1,0},{2,3},{3,2},{4,5},{5,4},{6,7},{7,6},{8,9},{9,8},{10,11... | collective-permute-start | bytes 1769480 | tf_op jit(solution)/shard_map/ppermute | solution.py:418
  235.2 30.1 %collective-permute-start.13 = (f32[192,768]{1,0:T(8,128)S(1)}, f32[192,768]{1,0:T(8,128)}, u32[]{:S(2)}, u32[]{:S(2)}) collective-permute-start(f32[192,768]{1,0:T(8,128)S(1)} %get-tuple-element.210.refs_8_), channel_id=1, source_target_pairs={{0,4},{2,6},{4,0},{6,2},{8,12},{10,14},{12,8},{14,10},{16,20},{18,... | collective-permute-start | bytes 1769480 | tf_op jit(solution)/shard_map/ppermute | solution.py:418
  260.7 8.7 %collective-permute-start.11 = (f32[2,2,2,2,56,256]{5,4,3,2,1,0:T(8,128)}, f32[2,2,2,2,56,256]{5,4,3,2,1,0:T(8,128)}, u32[]{:S(2)}, u32[]{:S(2)}) collective-permute-start(f32[2,2,2,2,56,256]{5,4,3,2,1,0:T(8,128)} %dynamic-slice_bitcast_fusion.1), channel_id=1, source_target_pairs={{0,2},{2,0},{4,6},{6,4},{8,10},{10,8},{12,14},{14,12},{16,18},{18,... | collective-permute-start | bytes 2752520 | tf_op jit(solution)/shard_map/ppermute | solution.py:418
  263.3 21.3 %collective-permute-start.17 = (f32[11,768]{1,0:T(8,128)S(1)}, f32[11,768]{1,0:T(8,128)}, u32[]{:S(2)}, u32[]{:S(2)}) collective-permute-start(f32[11,768]{1,0:T(8,128)S(1)} %pad_maximum_fusion.22.refs_4_), channel_id=1, source_target_pairs={{0,2},{2,0},{4,6},{6,4},{8,10},{10,8},{12,14},{14,12},{16,18},{18,... | collective-permute-start | bytes 101384 | tf_op jit(solution)/shard_map/ppermute | solution.py:418
  267.4 20.0 %collective-permute-start.16 = (f32[2,96,768]{2,1,0:T(8,128)}, f32[2,96,768]{2,1,0:T(8,128)}, u32[]{:S(2)}, u32[]{:S(2)}) collective-permute-start(f32[2,96,768]{2,1,0:T(8,128)} %fusion.6.refs_3_), channel_id=1, source_target_pairs={{0,8},{2,10},{4,12},{6,14},{8,0},{10,2},{12,4},{14,6},{16,24},{18,... | collective-permute-start | bytes 1769480 | tf_op jit(solution)/shard_map/ppermute | solution.py:418
  271.7 18.9 %collective-permute-start.12 = (f32[2,2,2,56,256]{4,3,2,1,0:T(8,128)S(1)}, f32[2,2,2,56,256]{4,3,2,1,0:T(8,128)}, u32[]{:S(2)}, u32[]{:S(2)}) collective-permute-start(f32[2,2,2,56,256]{4,3,2,1,0:T(8,128)S(1)} %dynamic-slice_bitcast_fusion.7.refs_2_), channel_id=1, source_target_pairs={{0,4},{2,6},{4,0},{6,2},{8,12},{10,14},{12,8},{14,10},{16,20},{18,... | collective-permute-start | bytes 1376264 | tf_op jit(solution)/shard_map/ppermute | solution.py:418
  288.6 15.6 %collective-permute-start.58 = (f32[2,48,768]{2,1,0:T(8,128)S(1)}, f32[2,48,768]{2,1,0:T(8,128)S(1)}, u32[]{:S(2)}, u32[]{:S(2)}) collective-permute-start(f32[2,48,768]{2,1,0:T(8,128)S(1)} %dynamic-slice_bitcast_fusion.13.refs_4_), channel_id=1, source_target_pairs={{0,16},{2,18},{4,20},{6,22},{8,24},{10,26},{12,28},{14,30},{16,0},... | collective-permute-start | bytes 884744 | tf_op jit(solution)/shard_map/ppermute | solution.py:418
  305.0 361.7 %all-reduce.2.cloned.1.call-start = ((), (), s32[]{:S(2)}) async-start(), calls=%async_computation | async-start | bytes 18874368 | tf_op jit(solution)/shard_map/psum | solution.py:658
  323.4 34.3 %collective-permute-start.23 = (f32[2,384,768]{2,1,0:T(8,128)}, f32[2,384,768]{2,1,0:T(8,128)S(1)}, u32[]{:S(2)}, u32[]{:S(2)}) collective-permute-start(f32[2,384,768]{2,1,0:T(8,128)} %get-tuple-element.119), channel_id=1, source_target_pairs={{0,2},{2,0},{4,6},{6,4},{8,10},{10,8},{12,14},{14,12},{16,18},{18,... | collective-permute-start | bytes 7077896 | tf_op jit(solution)/shard_map/ppermute | solution.py:418
  323.4 8.6 %collective-permute-start.18 = (f32[2,56,256]{2,1,0:T(8,128)S(1)}, f32[2,56,256]{2,1,0:T(8,128)S(1)}, u32[]{:S(2)}, u32[]{:S(2)}) collective-permute-start(f32[2,56,256]{2,1,0:T(8,128)S(1)} %copy-done.29), channel_id=1, source_target_pairs={{0,16},{2,18},{4,20},{6,22},{8,24},{10,26},{12,28},{14,30},{16,0},... | collective-permute-start | bytes 344072 | tf_op jit(solution)/shard_map/ppermute | solution.py:418
  323.9 8.3 %collective-permute-start.20 = (f32[11,768]{1,0:T(8,128)S(1)}, f32[11,768]{1,0:T(8,128)S(1)}, u32[]{:S(2)}, u32[]{:S(2)}) collective-permute-start(f32[11,768]{1,0:T(8,128)S(1)} %copy-done.33), channel_id=1, source_target_pairs={{0,4},{2,6},{4,0},{6,2},{8,12},{10,14},{12,8},{14,10},{16,20},{18,... | collective-permute-start | bytes 101384 | tf_op jit(solution)/shard_map/ppermute | solution.py:418
  332.1 12.5 %collective-permute-start.21 = (f32[2,56,256]{2,1,0:T(8,128)S(1)}, f32[2,56,256]{2,1,0:T(8,128)S(1)}, u32[]{:S(2)}, u32[]{:S(2)}) collective-permute-start(f32[2,56,256]{2,1,0:T(8,128)S(1)} %bitcast_add_fusion.23.refs_5_), channel_id=1, source_target_pairs={{0,16},{2,18},{4,20},{6,22},{8,24},{10,26},{12,28},{14,30},{16,0},... | collective-permute-start | bytes 344072 | tf_op jit(solution)/shard_map/ppermute | solution.py:418
  345.6 10.6 %collective-permute-start.22 = (f32[2,2,56,256]{3,2,1,0:T(8,128)S(1)}, f32[2,2,56,256]{3,2,1,0:T(8,128)S(1)}, u32[]{:S(2)}, u32[]{:S(2)}) collective-permute-start(f32[2,2,56,256]{3,2,1,0:T(8,128)S(1)} %pad_maximum_fusion.21), channel_id=1, source_target_pairs={{0,8},{2,10},{4,12},{6,14},{8,0},{10,2},{12,4},{14,6},{16,24},{18,... | collective-permute-start | bytes 688136 | tf_op jit(solution)/shard_map/ppermute | solution.py:418
  346.0 15.5 %collective-permute-start.24 = (f32[11,768]{1,0:T(8,128)S(1)}, f32[11,768]{1,0:T(8,128)S(1)}, u32[]{:S(2)}, u32[]{:S(2)}) collective-permute-start(f32[11,768]{1,0:T(8,128)S(1)} %copy-done.32), channel_id=1, source_target_pairs={{0,8},{2,10},{4,12},{6,14},{8,0},{10,2},{12,4},{14,6},{16,24},{18,... | collective-permute-start | bytes 101384 | tf_op jit(solution)/shard_map/ppermute | solution.py:418
  356.3 21.0 %collective-permute-start.25 = (f32[2,2,2,56,256]{4,3,2,1,0:T(8,128)S(1)}, f32[2,2,2,56,256]{4,3,2,1,0:T(8,128)}, u32[]{:S(2)}, u32[]{:S(2)}) collective-permute-start(f32[2,2,2,56,256]{4,3,2,1,0:T(8,128)S(1)} %pad_maximum_fusion.15.refs_3_), channel_id=1, source_target_pairs={{0,4},{2,6},{4,0},{6,2},{8,12},{10,14},{12,8},{14,10},{16,20},{18,... | collective-permute-start | bytes 1376264 | tf_op jit(solution)/shard_map/ppermute | solution.py:418
  360.7 37.4 %collective-permute-start.28 = (f32[192,768]{1,0:T(8,128)S(1)}, f32[192,768]{1,0:T(8,128)}, u32[]{:S(2)}, u32[]{:S(2)}) collective-permute-start(f32[192,768]{1,0:T(8,128)S(1)} %bitcast.378), channel_id=1, source_target_pairs={{0,4},{2,6},{4,0},{6,2},{8,12},{10,14},{12,8},{14,10},{16,20},{18,... | collective-permute-start | bytes 1769480 | tf_op jit(solution)/shard_map/ppermute | solution.py:418
  362.8 38.5 %collective-permute-start.27 = (f32[192,768]{1,0:T(8,128)S(1)}, f32[192,768]{1,0:T(8,128)}, u32[]{:S(2)}, u32[]{:S(2)}) collective-permute-start(f32[192,768]{1,0:T(8,128)S(1)} %dynamic-slice_bitcast_fusion.4.refs_4_), channel_id=1, source_target_pairs={{0,1},{1,0},{2,3},{3,2},{4,5},{5,4},{6,7},{7,6},{8,9},{9,8},{10,11... | collective-permute-start | bytes 1769480 | tf_op jit(solution)/shard_map/ppermute | solution.py:418
  380.3 31.0 %collective-permute-start.26 = (f32[2,2,2,2,56,256]{5,4,3,2,1,0:T(8,128)}, f32[2,2,2,2,56,256]{5,4,3,2,1,0:T(8,128)}, u32[]{:S(2)}, u32[]{:S(2)}) collective-permute-start(f32[2,2,2,2,56,256]{5,4,3,2,1,0:T(8,128)} %pad_maximum_fusion.9), channel_id=1, source_target_pairs={{0,2},{2,0},{4,6},{6,4},{8,10},{10,8},{12,14},{14,12},{16,18},{18,... | collective-permute-start | bytes 2752520 | tf_op jit(solution)/shard_map/ppermute | solution.py:418
  442.1 47.9 %collective-permute-start.34 = (f32[2,384,768]{2,1,0:T(8,128)}, f32[2,384,768]{2,1,0:T(8,128)S(1)}, u32[]{:S(2)}, u32[]{:S(2)}) collective-permute-start(f32[2,384,768]{2,1,0:T(8,128)} %get-tuple-element.132), channel_id=1, source_target_pairs={{0,2},{2,0},{4,6},{6,4},{8,10},{10,8},{12,14},{14,12},{16,18},{18,... | collective-permute-start | bytes 7077896 | tf_op jit(solution)/shard_map/ppermute | solution.py:418
  448.3 15.8 %collective-permute-start.31 = (f32[2,48,768]{2,1,0:T(8,128)S(1)}, f32[2,48,768]{2,1,0:T(8,128)S(1)}, u32[]{:S(2)}, u32[]{:S(2)}) collective-permute-start(f32[2,48,768]{2,1,0:T(8,128)S(1)} %copy-done.23), channel_id=1, source_target_pairs={{0,8},{2,10},{4,12},{6,14},{8,0},{10,2},{12,4},{14,6},{16,24},{18,... | collective-permute-start | bytes 884744 | tf_op jit(solution)/shard_map/ppermute | solution.py:418
  451.7 25.8 %collective-permute-start.35 = (f32[2,768]{1,0:T(2,128)S(1)}, f32[2,768]{1,0:T(2,128)S(1)}, u32[]{:S(2)}, u32[]{:S(2)}) collective-permute-start(f32[2,768]{1,0:T(2,128)S(1)} %add_add_fusion.9.refs_6_), channel_id=1, source_target_pairs={{0,1},{1,0},{2,3},{3,2},{4,5},{5,4},{6,7},{7,6},{8,9},{9,8},{10,11... | collective-permute-start | bytes 18440 | tf_op jit(solution)/shard_map/ppermute | solution.py:418
  476.1 13.1 %collective-permute-start.32 = (f32[2,24,768]{2,1,0:T(8,128)S(1)}, f32[2,24,768]{2,1,0:T(8,128)S(1)}, u32[]{:S(2)}, u32[]{:S(2)}) collective-permute-start(f32[2,24,768]{2,1,0:T(8,128)S(1)} %copy-done.28), channel_id=1, source_target_pairs={{0,16},{2,18},{4,20},{6,22},{8,24},{10,26},{12,28},{14,30},{16,0},... | collective-permute-start | bytes 442376 | tf_op jit(solution)/shard_map/ppermute | solution.py:418
  478.2 33.1 %collective-permute-start.60 = (f32[2,768]{1,0:T(2,128)S(1)}, f32[2,768]{1,0:T(2,128)S(1)}, u32[]{:S(2)}, u32[]{:S(2)}) collective-permute-start(f32[2,768]{1,0:T(2,128)S(1)} %add_add_fusion.8.refs_8_), channel_id=1, source_target_pairs={{0,4},{2,6},{4,0},{6,2},{8,12},{10,14},{12,8},{14,10},{16,20},{18,... | collective-permute-start | bytes 18440 | tf_op jit(solution)/shard_map/ppermute | solution.py:418
  489.9 25.0 %collective-permute-start.36 = (f32[2,24,768]{2,1,0:T(8,128)}, f32[2,24,768]{2,1,0:T(8,128)S(1)}, u32[]{:S(2)}, u32[]{:S(2)}) collective-permute-start(f32[2,24,768]{2,1,0:T(8,128)} %fusion.20.refs_5_), channel_id=1, source_target_pairs={{0,16},{2,18},{4,20},{6,22},{8,24},{10,26},{12,28},{14,30},{16,0},... | collective-permute-start | bytes 442376 | tf_op jit(solution)/shard_map/ppermute | solution.py:418
  492.2 23.9 %collective-permute-start.43 = (f32[192,768]{1,0:T(8,128)S(1)}, f32[192,768]{1,0:T(8,128)}, u32[]{:S(2)}, u32[]{:S(2)}) collective-permute-start(f32[192,768]{1,0:T(8,128)S(1)} %bitcast.376), channel_id=1, source_target_pairs={{0,4},{2,6},{4,0},{6,2},{8,12},{10,14},{12,8},{14,10},{16,20},{18,... | collective-permute-start | bytes 1769480 | tf_op jit(solution)/shard_map/ppermute | solution.py:418
  509.7 22.5 %collective-permute-start.41 = (f32[192,768]{1,0:T(8,128)S(1)}, f32[192,768]{1,0:T(8,128)}, u32[]{:S(2)}, u32[]{:S(2)}) collective-permute-start(f32[192,768]{1,0:T(8,128)S(1)} %copy-done.10), channel_id=1, source_target_pairs={{0,1},{1,0},{2,3},{3,2},{4,5},{5,4},{6,7},{7,6},{8,9},{9,8},{10,11... | collective-permute-start | bytes 1769480 | tf_op jit(solution)/shard_map/ppermute | solution.py:418
  511.3 23.0 %collective-permute-start.61 = (f32[2,768]{1,0:T(2,128)S(1)}, f32[2,768]{1,0:T(2,128)S(1)}, u32[]{:S(2)}, u32[]{:S(2)}) collective-permute-start(f32[2,768]{1,0:T(2,128)S(1)} %add_add_fusion.7), channel_id=1, source_target_pairs={{0,8},{2,10},{4,12},{6,14},{8,0},{10,2},{12,4},{14,6},{16,24},{18,... | collective-permute-start | bytes 18440 | tf_op jit(solution)/shard_map/ppermute | solution.py:418
  515.9 28.4 %collective-permute-start.37 = (f32[2,48,768]{2,1,0:T(8,128)S(1)}, f32[2,48,768]{2,1,0:T(8,128)S(1)}, u32[]{:S(2)}, u32[]{:S(2)}) collective-permute-start(f32[2,48,768]{2,1,0:T(8,128)S(1)} %bitcast.400), channel_id=1, source_target_pairs={{0,8},{2,10},{4,12},{6,14},{8,0},{10,2},{12,4},{14,6},{16,24},{18,... | collective-permute-start | bytes 884744 | tf_op jit(solution)/shard_map/ppermute | solution.py:418
  517.2 20.6 %collective-permute-start.44 = (f32[96,768]{1,0:T(8,128)S(1)}, f32[96,768]{1,0:T(8,128)S(1)}, u32[]{:S(2)}, u32[]{:S(2)}) collective-permute-start(f32[96,768]{1,0:T(8,128)S(1)} %dynamic-slice_bitcast_fusion.9), channel_id=1, source_target_pairs={{0,1},{1,0},{2,3},{3,2},{4,5},{5,4},{6,7},{7,6},{8,9},{9,8},{10,11... | collective-permute-start | bytes 884744 | tf_op jit(solution)/shard_map/ppermute | solution.py:418
  534.3 10.1 %collective-permute-start.62 = (f32[2,768]{1,0:T(2,128)S(1)}, f32[2,768]{1,0:T(2,128)S(1)}, u32[]{:S(2)}, u32[]{:S(2)}) collective-permute-start(f32[2,768]{1,0:T(2,128)S(1)} %add_add_fusion.6), channel_id=1, source_target_pairs={{0,16},{2,18},{4,20},{6,22},{8,24},{10,26},{12,28},{14,30},{16,0},... | collective-permute-start | bytes 18440 | tf_op jit(solution)/shard_map/ppermute | solution.py:418
  540.3 12.0 %collective-permute-start.45 = (f32[2,48,768]{2,1,0:T(8,128)S(1)}, f32[2,48,768]{2,1,0:T(8,128)S(1)}, u32[]{:S(2)}, u32[]{:S(2)}) collective-permute-start(f32[2,48,768]{2,1,0:T(8,128)S(1)} %fusion.10), channel_id=1, source_target_pairs={{0,8},{2,10},{4,12},{6,14},{8,0},{10,2},{12,4},{14,6},{16,24},{18,... | collective-permute-start | bytes 884744 | tf_op jit(solution)/shard_map/ppermute | solution.py:418
  552.3 10.4 %collective-permute-start.46 = (f32[2,24,768]{2,1,0:T(8,128)S(1)}, f32[2,24,768]{2,1,0:T(8,128)S(1)}, u32[]{:S(2)}, u32[]{:S(2)}) collective-permute-start(f32[2,24,768]{2,1,0:T(8,128)S(1)} %dynamic-slice_bitcast_fusion.16), channel_id=1, source_target_pairs={{0,16},{2,18},{4,20},{6,22},{8,24},{10,26},{12,28},{14,30},{16,0},... | collective-permute-start | bytes 442376 | tf_op jit(solution)/shard_map/ppermute | solution.py:418
  552.4 10.4 %collective-permute-start.55 = (f32[96,768]{1,0:T(8,128)S(1)}, f32[96,768]{1,0:T(8,128)S(1)}, u32[]{:S(2)}, u32[]{:S(2)}) collective-permute-start(f32[96,768]{1,0:T(8,128)S(1)} %bitcast.406), channel_id=1, source_target_pairs={{0,4},{2,6},{4,0},{6,2},{8,12},{10,14},{12,8},{14,10},{16,20},{18,... | collective-permute-start | bytes 884744 | tf_op jit(solution)/shard_map/ppermute | solution.py:418
  553.9 16.3 %collective-permute-start.38 = (f32[96,768]{1,0:T(8,128)S(1)}, f32[96,768]{1,0:T(8,128)S(1)}, u32[]{:S(2)}, u32[]{:S(2)}) collective-permute-start(f32[96,768]{1,0:T(8,128)S(1)} %bitcast.404), channel_id=1, source_target_pairs={{0,1},{1,0},{2,3},{3,2},{4,5},{5,4},{6,7},{7,6},{8,9},{9,8},{10,11... | collective-permute-start | bytes 884744 | tf_op jit(solution)/shard_map/ppermute | solution.py:418
  562.9 16.9 %collective-permute-start.56 = (f32[192,768]{1,0:T(8,128)S(1)}, f32[192,768]{1,0:T(8,128)S(1)}, u32[]{:S(2)}, u32[]{:S(2)}) collective-permute-start(f32[192,768]{1,0:T(8,128)S(1)} %bitcast.380), channel_id=1, source_target_pairs={{0,1},{1,0},{2,3},{3,2},{4,5},{5,4},{6,7},{7,6},{8,9},{9,8},{10,11... | collective-permute-start | bytes 1769480 | tf_op jit(solution)/shard_map/ppermute | solution.py:418
  570.1 9.6 %collective-permute-start.48 = (f32[2,48,768]{2,1,0:T(8,128)S(1)}, f32[2,48,768]{2,1,0:T(8,128)S(1)}, u32[]{:S(2)}, u32[]{:S(2)}) collective-permute-start(f32[2,48,768]{2,1,0:T(8,128)S(1)} %bitcast.402), channel_id=1, source_target_pairs={{0,8},{2,10},{4,12},{6,14},{8,0},{10,2},{12,4},{14,6},{16,24},{18,... | collective-permute-start | bytes 884744 | tf_op jit(solution)/shard_map/ppermute | solution.py:418
  570.3 17.4 %collective-permute-start.39 = (f32[192,768]{1,0:T(8,128)S(1)}, f32[192,768]{1,0:T(8,128)S(1)}, u32[]{:S(2)}, u32[]{:S(2)}) collective-permute-start(f32[192,768]{1,0:T(8,128)S(1)} %bitcast.410), channel_id=1, source_target_pairs={{0,4},{2,6},{4,0},{6,2},{8,12},{10,14},{12,8},{14,10},{16,20},{18,... | collective-permute-start | bytes 1769480 | tf_op jit(solution)/shard_map/ppermute | solution.py:418
  580.0 28.7 %collective-permute-start.57 = (f32[384,768]{1,0:T(8,128)S(1)}, f32[384,768]{1,0:T(8,128)S(1)}, u32[]{:S(2)}, u32[]{:S(2)}) collective-permute-start(f32[384,768]{1,0:T(8,128)S(1)} %bitcast.351), channel_id=1, source_target_pairs={{0,2},{2,0},{4,6},{6,4},{8,10},{10,8},{12,14},{14,12},{16,18},{18,... | collective-permute-start | bytes 3538952 | tf_op jit(solution)/shard_map/ppermute | solution.py:418
  580.1 9.9 %collective-permute-start.49 = (f32[96,768]{1,0:T(8,128)S(1)}, f32[96,768]{1,0:T(8,128)S(1)}, u32[]{:S(2)}, u32[]{:S(2)}) collective-permute-start(f32[96,768]{1,0:T(8,128)S(1)} %bitcast.405), channel_id=1, source_target_pairs={{0,4},{2,6},{4,0},{6,2},{8,12},{10,14},{12,8},{14,10},{16,20},{18,... | collective-permute-start | bytes 884744 | tf_op jit(solution)/shard_map/ppermute | solution.py:418
  586.6 21.8 %collective-permute-start.53 = (f32[192,768]{1,0:T(8,128)S(1)}, f32[192,768]{1,0:T(8,128)S(1)}, u32[]{:S(2)}, u32[]{:S(2)}) collective-permute-start(f32[192,768]{1,0:T(8,128)S(1)} %bitcast.411), channel_id=1, source_target_pairs={{0,4},{2,6},{4,0},{6,2},{8,12},{10,14},{12,8},{14,10},{16,20},{18,... | collective-permute-start | bytes 1769480 | tf_op jit(solution)/shard_map/ppermute | solution.py:418
  587.9 24.7 %collective-permute-start.40 = (f32[384,768]{1,0:T(8,128)S(1)}, f32[384,768]{1,0:T(8,128)S(1)}, u32[]{:S(2)}, u32[]{:S(2)}) collective-permute-start(f32[384,768]{1,0:T(8,128)S(1)} %bitcast.352), channel_id=1, source_target_pairs={{0,2},{2,0},{4,6},{6,4},{8,10},{10,8},{12,14},{14,12},{16,18},{18,... | collective-permute-start | bytes 3538952 | tf_op jit(solution)/shard_map/ppermute | solution.py:418
  590.1 20.7 %collective-permute-start.50 = (f32[192,768]{1,0:T(8,128)S(1)}, f32[192,768]{1,0:T(8,128)S(1)}, u32[]{:S(2)}, u32[]{:S(2)}) collective-permute-start(f32[192,768]{1,0:T(8,128)S(1)} %bitcast.383), channel_id=1, source_target_pairs={{0,1},{1,0},{2,3},{3,2},{4,5},{5,4},{6,7},{7,6},{8,9},{9,8},{10,11... | collective-permute-start | bytes 1769480 | tf_op jit(solution)/shard_map/ppermute | solution.py:418
  (62 other events, 400.7 us)
Sparse Core Ops, SparseCore 0:
  305.1 105.0 all-gather.2
  444.0 222.5 all-reduce.1

commit v3 on v2

--- a/solution.py
+++ b/solution.py
@@ -102,8 +102,7 @@
         minus = jnp.full((size, feats), -1.0, BF16)
         for head in range(heads):
             pair, e = divmod(head, 2)
-            turned = jnp.transpose(turns_ref[head].astype(F32)).astype(BF16)
-            dirs_ref[pair, pl.ds(e * size, size), pl.ds(e * feats, feats)] = turned
+            dirs_ref[pair, pl.ds(e * size, size), pl.ds(e * feats, feats)] = turns_ref[head]
             dirs_ref[pair, pl.ds(lanes + e * size, size), pl.ds(e * feats, feats)] = minus
 
     tile = x_ref.shape[0]
@@ -562,9 +561,9 @@
     unit = 8 << len(bits_of("seq"))
     sum_rows = -(-(width + heads) // unit) * unit
 
-    params = jnp.concatenate(
-        [b_query, b_key, b_value, b_out, b_down, norm1_gain, norm1_shift, norm2_gain, norm2_shift, b_up]
-    ).astype(F32).reshape(-1, width)
+    vectors = [b_query, b_key, b_value, b_out, b_down, norm1_gain, norm1_shift, norm2_gain, norm2_shift, b_up]
+    params = jnp.concatenate([vector.astype(F32).reshape(-1, width) for vector in vectors])
+    turns = head_feature_directions.transpose(0, 2, 1)
     x, ct = inputs[0], cotangent[0]
     order = Order()
 
@@ -588,9 +587,9 @@
     feat_rows, ff_rows = shape_of((tokens, all_feats), BF16), shape_of((tokens, ff), BF16)
     keys, values, key_feat, key_sum, dirs = order.call(
         functools.partial(key_kernel, consts), (steps,),
-        [starts, lengths, x, w_key, w_value, params, head_feature_directions],
+        [starts, lengths, x, w_key, w_value, params, turns],
         [bf16_rows, bf16_rows, feat_rows, shape_of(sums_shape, F32), shape_of(dirs_shape, BF16)],
-        [narrow, square, square, param_spec, whole(head_feature_directions.shape)],
+        [narrow, square, square, param_spec, whole(turns.shape)],
         [narrow, narrow, broad, summed(sums_shape), summed(dirs_shape)],
         scratch=[pltpu.VMEM((heads * (size + 16), tile), BF16)], prefetch=2,
     )
@@ -688,10 +687,12 @@
     first = gather_pair(order, finish(first))
     last = scatter_pair(order, last_sent, last_kept)
     step(last)
+    step(first, last)
+    step(first, last)
     input_grad = order.call(
         input_kernel, (steps,), [partial_input, key_grad, w_key, value_grad, w_value], f32_rows,
         [narrow, narrow, square, narrow, square], narrow,
-        deps=step(first) + step(last) + step(late),
+        deps=step(first) + step(last) + step(late) + [whole_up],
     )
     last = gather_pair(order, finish(last))
     first, last, late = [finish(part) for part in (first, last, late)]

time: 693 us -> 668 us (0.964)
  waiting for transfers between devices: 204 us -> 192 us
  local copies, waits for them, and re-layouts: 46.9 us -> 37.6 us
    psum x1, waiting for transfers between devices: 39.3 us -> 4.82 us  [on_device(): whole_up = lax.psum(grad_up, everyone)]
    ppermute x63, waiting for transfers between devices: 165 us -> 187 us  [exchange(): return lax.ppermute(sent, tag[0], pairs)]
    unnamed x101 -> x99, local copies, waits for them, and re-layouts: 24.2 us -> 10.3 us
  transfers between devices with their start and end apart: 65 -> 65, of which waited for: 30 -> 31; matrix products, arithmetic and copies ran while one was open for 9% -> 8% of each run, Pallas kernels for 26% -> 25%
where the time goes in v3:
time: 668 us; the launch traced here: 658 us
  Pallas kernels  269 us (40%)
  waiting for transfers between devices  192 us (29%)
  starting transfers between devices  59.7 us (9%)
  other arithmetic  55.9 us (8%)
  between operations  44.1 us (7%)
  local copies, waits for them, and re-layouts  37.6 us (6%)
    pallas_call x17, Pallas kernels, call(): pl.pallas_call(body, out_shape=[*outs, shape_of((1,), jnp.int32)], grid_s...  269 us
    ppermute x63, waiting for transfers between devices, exchange(): return lax.ppermute(sent, tag[0], pairs)  187 us
    ppermute x63, starting transfers between devices, exchange(): return lax.ppermute(sent, tag[0], pairs)  59.7 us
    add x18, other arithmetic, scatter_pair(): totals = [stay + came for stay, came in zip(kept, received)]  21 us
  transfers between devices with their start and end apart: 65, of which 31 were waited for; matrix products, arithmetic and copies ran while one was open for 8% of the time, Pallas kernels for 25%

profile of v3, /device:TPU:0, one launch (start us, length us, event | category | flops | bytes accessed | tf_op | source)
XLA Modules:
  0.0 658.2 jit_solution(4529598939190306944)
XLA Ops:
  14.8 19.8 %shard_map.349 = (bf16[2048,768]{1,0:T(8,128)(2,1)}, bf16[2048,768]{1,0:T(8,128)(2,1)}, bf16[2048,3072]{1,0:T(8,128)(2,1)}, f32[896,256]{1,0:T(8,128)}, bf16[6,256,512]{2,1,0:T(8,128)(2,1)}, /*index=5*/s32[1]{0:T(128)}) custom-call(s32[6]{0:T(128)} %bitcast.414, s32[6]{0:T(128)} %bitcast.416, bf16[2048,768]{1,0:T(8,128)(2,1)} %bitcast.331, ...), custom_call_target="tpu_custom_call" | custom-call | flops 1 | bytes 1 | tf_op jit(solution)/shard_map/pallas_call | solution.py:326
  41.1 3.0 collective-permute-start.1
  44.0 8.5 %shard_map.350 = (bf16[2048,768]{1,0:T(8,128)(2,1)}, bf16[2048,3072]{1,0:T(8,128)(2,1)}, s32[1]{0:T(128)}) custom-call(bf16[2048,768]{1,0:T(8,128)(2,1)} %bitcast.332, bf16[768,768]{1,0:T(8,128)(2,1)} %refs_2_.2, f32[13,768]{1,0:T(8,128)} %concatenate.12.refs_5_.refs_2_.refs_7_, bf16[6,256,512]{2,1,0:T(8,128)(2,1)} %get-tuple-element.77.refs_3_.refs_6_, ...), custom_call_target="tpu_custom_call" | custom-call | flops 1 | bytes 1 | tf_op jit(solution)/shard_map/pallas_call | solution.py:326
  57.5 4.7 collective-permute-done.2
  62.2 2.6 collective-permute-start.3
  64.8 4.6 collective-permute-done.3
  70.6 4.5 collective-permute-done.4
  75.2 3.3 collective-permute-start.5
  78.5 4.0 collective-permute-done.5
  84.2 8.5 %shard_map.351 = (bf16[2048,768]{1,0:T(8,128)(2,1)}, bf16[2048,3072]{1,0:T(8,128)(2,1)}, s32[1]{0:T(128)}) custom-call(bf16[2048,768]{1,0:T(8,128)(2,1)} %bitcast.333, bf16[768,768]{1,0:T(8,128)(2,1)} %refs_2_.2, f32[13,768]{1,0:T(8,128)} %concatenate.12.refs_5_.refs_2_.refs_7_, ...), custom_call_target="tpu_custom_call", output_to_operand_aliasing={{0}: (4, {}), {1}: (5, {})} | custom-call | flops 1 | bytes 1 | tf_op jit(solution)/shard_map/pallas_call | solution.py:326
  98.4 59.2 %shard_map.352 = (f32[2048,768]{1,0:T(8,128)}, bf16[2048,768]{1,0:T(8,128)(2,1)}, f32[2048,768]{1,0:T(8,128)}, f32[2048,768]{1,0:T(8,128)}, f32[2048,128]{1,0:T(...) custom-call(bf16[2048,768]{1,0:T(8,128)(2,1)} %bitcast.334, ...), custom_call_target="tpu_custom_call" | custom-call | flops 1 | bytes 1 | tf_op jit(solution)/shard_map/pallas_call | solution.py:326
  157.7 11.2 %shard_map.353 = (f32[2,768,768]{2,1,0:T(8,128)}, s32[1]{0:T(128)}) custom-call(s32[1]{0:T(128)} %bitcast.28.refs_0_, bf16[2048,3072]{1,0:T(8,128)(2,1)} %get-tuple-element.91.refs_1_, bf16[2048,768]{1,0:T(8,128)(2,1)} %get-tuple-element.86.refs_2_.refs_0_, s32[1]{0:T(128)} %get-tuple-element.92.refs_3_), custom_call_target="tpu_custom_call" | custom-call | flops 1 | bytes 1 | tf_op jit(solution)/shard_map/pallas_call | solution.py:326
  169.0 11.2 %shard_map.354 = (f32[2,768,768]{2,1,0:T(8,128)}, s32[1]{0:T(128)}) custom-call(s32[1]{0:T(128)} %bitcast.27.refs_0_, bf16[2048,3072]{1,0:T(8,128)(2,1)} %get-tuple-element.91.refs_1_, bf16[2048,768]{1,0:T(8,128)(2,1)} %get-tuple-element.86.refs_2_.refs_0_, s32[1]{0:T(128)} %get-tuple-element.93.refs_3_), custom_call_target="tpu_custom_call" | custom-call | flops 1 | bytes 1 | tf_op jit(solution)/shard_map/pallas_call | solution.py:326
  180.8 4.4 add.524
  192.4 32.3 %shard_map.355 = (bf16[2048,3072]{1,0:T(8,128)(2,1)}, f32[2048,768]{1,0:T(8,128)}, bf16[2048,768]{1,0:T(8,128)(2,1)}, f32[3,768]{1,0:T(4,128)}, f32[1,3072]{1,0:T(1,128)}, /*index=5*/s32[1]{0:T(128)}) custom-call(bf16[2048,768]{1,0:T(8,128)(2,1)} %get-tuple-element.86.refs_2_.refs_0_, bf16[2048,3072]{1,0:T(8,128)(2,1)} %get-tuple-element.87.refs_1_, ...), custom_call_target="tpu_custom_call" | custom-call | flops 1 | bytes 1 | tf_op jit(solution)/shard_map/pallas_call | solution.py:326
  232.1 21.4 %shard_map.356 = (bf16[2048,768]{1,0:T(8,128)(2,1)}, f32[896,256]{1,0:T(8,128)}, f32[1,768]{1,0:T(1,128)}, s32[1]{0:T(128)}) custom-call(bf16[2048,768]{1,0:T(8,128)(2,1)} %get-tuple-element.98.refs_0_.refs_2_, bf16[2048,768]{1,0:T(8,128)(2,1)} %get-tuple-element.99.refs_1_, f32[2048,768]{1,0:T(8,128)} %get-tuple-element.100.refs_2_, ...), custom_call_target="tpu_custom_call" | custom-call | flops 1 | bytes 1 | tf_op jit(solution)/shard_map/pallas_call | solution.py:326
  268.7 11.0 %shard_map.357 = (f32[768,3072]{1,0:T(8,128)}, s32[1]{0:T(128)}) custom-call(bf16[2048,768]{1,0:T(8,128)(2,1)} %get-tuple-element.107.refs_0_, bf16[2048,3072]{1,0:T(8,128)(2,1)} %get-tuple-element.108.refs_1_, f32[2,2,2,56,256]{4,3,2,1,0:T(8,128)} %copy-done.20, f32[2,96,768]{2,1,0:T(8,128)} %fusion.6.refs_3_, f32[11,768]{1,0:T(8,128)} %copy-done.34, ...), custom_call_target="tpu_custom_call" | custom-call | flops 1 | bytes 1 | tf_op jit(solution)/shard_map/pallas_call | solution.py:326
  287.0 11.0 %shard_map.358 = (f32[768,3072]{1,0:T(8,128)}, s32[1]{0:T(128)}) custom-call(bf16[2048,768]{1,0:T(8,128)(2,1)} %get-tuple-element.107.refs_0_, bf16[2048,3072]{1,0:T(8,128)(2,1)} %get-tuple-element.108.refs_1_, f32[768,3072]{1,0:T(8,128)} %get-tuple-element.114.refs_2_, ...), custom_call_target="tpu_custom_call", output_to_operand_aliasing={{0}: (2, {})} | custom-call | flops 1 | bytes 1 | tf_op jit(solution)/shard_map/pallas_call | solution.py:326
  306.2 14.4 %collective-permute-done.58 = f32[2,48,768]{2,1,0:T(8,128)S(1)} collective-permute-done((f32[2,48,768]{2,1,0:T(8,128)S(1)}, f32[2,48,768]{2,1,0:T(8,128)S(1)}, u32[]{:S(2)}, u32[]{:S(2)}) %collective-permute-start.58) | collective-permute-done | bytes 294944 | tf_op jit(solution)/shard_map/ppermute | solution.py:417
  323.3 9.2 %shard_map.359 = (f32[2,384,768]{2,1,0:T(8,128)}, s32[1]{0:T(128)}) custom-call(s32[1]{0:T(128)} %bitcast.28.refs_0_, bf16[2048,768]{1,0:T(8,128)(2,1)} %get-tuple-element.99.refs_1_, bf16[2048,768]{1,0:T(8,128)(2,1)} %get-tuple-element.98.refs_0_.refs_2_, bf16[2048,768]{1,0:T(8,128)(2,1)} %bitcast.335, ...), custom_call_target="tpu_custom_call" | custom-call | flops 1 | bytes 1 | tf_op jit(solution)/shard_map/pallas_call | solution.py:326
  334.4 9.9 %collective-permute-done.18 = f32[2,56,256]{2,1,0:T(8,128)S(1)} collective-permute-done((f32[2,56,256]{2,1,0:T(8,128)S(1)}, f32[2,56,256]{2,1,0:T(8,128)S(1)}, u32[]{:S(2)}, u32[]{:S(2)}) %collective-permute-start.18) | collective-permute-done | bytes 114720 | tf_op jit(solution)/shard_map/ppermute | solution.py:417
  345.0 8.9 %shard_map.360 = (f32[2,384,768]{2,1,0:T(8,128)}, s32[1]{0:T(128)}) custom-call(s32[1]{0:T(128)} %bitcast.27.refs_0_, bf16[2048,768]{1,0:T(8,128)(2,1)} %get-tuple-element.99.refs_1_, bf16[2048,768]{1,0:T(8,128)(2,1)} %get-tuple-element.98.refs_0_.refs_2_, bf16[2048,768]{1,0:T(8,128)(2,1)} %bitcast.336, ...), custom_call_target="tpu_custom_call" | custom-call | flops 1 | bytes 1 | tf_op jit(solution)/shard_map/pallas_call | solution.py:326
  360.1 9.4 %collective-permute-done.22 = f32[2,2,56,256]{3,2,1,0:T(8,128)S(1)} collective-permute-done((f32[2,2,56,256]{3,2,1,0:T(8,128)S(1)}, f32[2,2,56,256]{3,2,1,0:T(8,128)S(1)}, u32[]{:S(2)}, u32[]{:S(2)}) %collective-permute-start.22) | collective-permute-done | bytes 229408 | tf_op jit(solution)/shard_map/ppermute | solution.py:417
  377.8 9.5 %shard_map.361 = (f32[2048,768]{1,0:T(8,128)}, s32[1]{0:T(128)}) custom-call(f32[2048,768]{1,0:T(8,128)} %get-tuple-element.97.refs_0_, bf16[2048,768]{1,0:T(8,128)(2,1)} %get-tuple-element.104.refs_4_.refs_1_, bf16[768,768]{1,0:T(8,128)(2,1)} %refs_2_.2, f32[2,2,2,56,256]{4,3,2,1,0:T(8,128)} %copy-done.19, f32[192,768]{1,0:T(8,128)} %copy-done.11, ...), custom_call_target="tpu_custom_call" | custom-call | flops 1 | bytes 1 | tf_op jit(solution)/shard_map/pallas_call | solution.py:326
  390.9 8.5 %collective-permute-done.28 = f32[192,768]{1,0:T(8,128)} collective-permute-done((f32[192,768]{1,0:T(8,128)S(1)}, f32[192,768]{1,0:T(8,128)}, u32[]{:S(2)}, u32[]{:S(2)}) %collective-permute-start.28) | collective-permute-done | bytes 589856 | tf_op jit(solution)/shard_map/ppermute | solution.py:417
  404.9 3.5 collective-permute-done.30
  409.5 4.4 collective-permute-done.29
  418.5 17.0 %shard_map.362 = (bf16[2048,768]{1,0:T(8,128)(2,1)}, bf16[2048,768]{1,0:T(8,128)(2,1)}, f32[2,768]{1,0:T(2,128)}, s32[1]{0:T(128)}) custom-call(s32[6]{0:T(128)} %bitcast.415, s32[6]{0:T(128)} %bitcast.417, bf16[2048,768]{1,0:T(8,128)(2,1)} %get-tuple-element.121.refs_2_, bf16[2048,768]{1,0:T(8,128)(2,1)} %get-tuple-element.122.refs_3_, ...), custom_call_target="tpu_custom_call" | custom-call | flops 1 | bytes 1 | tf_op jit(solution)/shard_map/pallas_call | solution.py:326
  436.9 8.9 %shard_map.363 = (f32[2,384,768]{2,1,0:T(8,128)}, s32[1]{0:T(128)}) custom-call(s32[1]{0:T(128)} %bitcast.28.refs_0_, bf16[2048,768]{1,0:T(8,128)(2,1)} %bitcast.337, bf16[2048,768]{1,0:T(8,128)(2,1)} %get-tuple-element.125.refs_2_.refs_1_, bf16[2048,768]{1,0:T(8,128)(2,1)} %bitcast.338, bf16[2048,768]{1,0:T(8,128)(2,1)} %get-tuple-element.126.refs_4_.refs_3_, ...), custom_call_target="tpu_custom_call" | custom-call | flops 1 | bytes 1 | tf_op jit(solution)/shard_map/pallas_call | solution.py:326
  449.6 16.0 %collective-permute-done.31 = f32[2,48,768]{2,1,0:T(8,128)} collective-permute-done((f32[2,48,768]{2,1,0:T(8,128)S(1)}, f32[2,48,768]{2,1,0:T(8,128)}, u32[]{:S(2)}, u32[]{:S(2)}) %collective-permute-start.31) | collective-permute-done | bytes 294944 | tf_op jit(solution)/shard_map/ppermute | solution.py:417
  467.3 9.9 %shard_map.364 = (f32[2,384,768]{2,1,0:T(8,128)}, s32[1]{0:T(128)}) custom-call(s32[1]{0:T(128)} %bitcast.27.refs_0_, bf16[2048,768]{1,0:T(8,128)(2,1)} %bitcast.339, bf16[2048,768]{1,0:T(8,128)(2,1)} %get-tuple-element.125.refs_2_.refs_1_, bf16[2048,768]{1,0:T(8,128)(2,1)} %bitcast.340, bf16[2048,768]{1,0:T(8,128)(2,1)} %get-tuple-element.126.refs_4_.refs_3_, ...), custom_call_target="tpu_custom_call" | custom-call | flops 1 | bytes 1 | tf_op jit(solution)/shard_map/pallas_call | solution.py:326
  477.9 3.0 collective-permute-start.34
  485.9 4.8 collective-permute-done.34
  498.1 8.2 %collective-permute-done.35 = f32[2,48,768]{2,1,0:T(8,128)S(1)} collective-permute-done((f32[2,48,768]{2,1,0:T(8,128)S(1)}, f32[2,48,768]{2,1,0:T(8,128)S(1)}, u32[]{:S(2)}, u32[]{:S(2)}) %collective-permute-start.35) | collective-permute-done | bytes 294944 | tf_op jit(solution)/shard_map/ppermute | solution.py:417
  506.3 6.4 collective-permute-done.39
  517.8 4.9 collective-permute-done.40
  525.5 4.8 all-reduce.2.cloned.1.call-done.refs_9_
  530.3 11.6 %shard_map.365 = (f32[2048,768]{1,0:T(8,128)}, s32[1]{0:T(128)}) custom-call(f32[2048,768]{1,0:T(8,128)} %get-tuple-element.120.refs_0_, bf16[2048,768]{1,0:T(8,128)(2,1)} %get-tuple-element.125.refs_2_.refs_1_, bf16[768,768]{1,0:T(8,128)(2,1)} %refs_2_.3, bf16[2048,768]{1,0:T(8,128)(2,1)} %get-tuple-element.126.refs_4_.refs_3_, bf16[768,768]{1,0:T(8,128)(2,1)} %refs_4_.5, ...), custom_call_target="tpu_custom_call" | custom-call | flops 1 | bytes 1 | tf_op jit(solution)/shard_map/pallas_call | solution.py:326
  545.3 2.1 collective-permute-start.61
  549.9 7.8 %collective-permute-done.45 = f32[2,48,768]{2,1,0:T(8,128)S(1)} collective-permute-done((f32[2,48,768]{2,1,0:T(8,128)S(1)}, f32[2,48,768]{2,1,0:T(8,128)S(1)}, u32[]{:S(2)}, u32[]{:S(2)}) %collective-permute-start.45) | collective-permute-done | bytes 294944 | tf_op jit(solution)/shard_map/ppermute | solution.py:417
  562.2 13.1 %collective-permute-done.46 = f32[2,24,768]{2,1,0:T(8,128)S(1)} collective-permute-done((f32[2,24,768]{2,1,0:T(8,128)S(1)}, f32[2,24,768]{2,1,0:T(8,128)S(1)}, u32[]{:S(2)}, u32[]{:S(2)}) %collective-permute-start.46) | collective-permute-done | bytes 147488 | tf_op jit(solution)/shard_map/ppermute | solution.py:417
  575.4 3.0 collective-permute-start.62
  578.4 7.7 %collective-permute-done.47 = f32[2,24,768]{2,1,0:T(8,128)S(1)} collective-permute-done((f32[2,24,768]{2,1,0:T(8,128)S(1)}, f32[2,24,768]{2,1,0:T(8,128)S(1)}, u32[]{:S(2)}, u32[]{:S(2)}) %collective-permute-start.47) | collective-permute-done | bytes 147488 | tf_op jit(solution)/shard_map/ppermute | solution.py:417
  586.9 18.5 %collective-permute-done.48 = f32[2,48,768]{2,1,0:T(8,128)S(1)} collective-permute-done((f32[2,48,768]{2,1,0:T(8,128)S(1)}, f32[2,48,768]{2,1,0:T(8,128)S(1)}, u32[]{:S(2)}, u32[]{:S(2)}) %collective-permute-start.48) | collective-permute-done | bytes 294944 | tf_op jit(solution)/shard_map/ppermute | solution.py:417
  606.9 8.4 %collective-permute-done.52 = f32[96,768]{1,0:T(8,128)S(1)} collective-permute-done((f32[96,768]{1,0:T(8,128)S(1)}, f32[96,768]{1,0:T(8,128)S(1)}, u32[]{:S(2)}, u32[]{:S(2)}) %collective-permute-start.52) | collective-permute-done | bytes 294944 | tf_op jit(solution)/shard_map/ppermute | solution.py:417
  618.2 10.6 %collective-permute-done.53 = f32[192,768]{1,0:T(8,128)S(1)} collective-permute-done((f32[192,768]{1,0:T(8,128)S(1)}, f32[192,768]{1,0:T(8,128)S(1)}, u32[]{:S(2)}, u32[]{:S(2)}) %collective-permute-start.53) | collective-permute-done | bytes 589856 | tf_op jit(solution)/shard_map/ppermute | solution.py:417
  638.4 8.7 %copy.94 = f32[2,2,2,2,2,2,48,768]{7,6,5,4,3,2,1,0:T(8,128)} copy(f32[2,2,2,2,2,2,48,768]{7,6,1,2,0,3,4,5:T(8,128)} %bitcast.343) | data formatting | bytes 18874368 | tf_op jit(solution)/shard_map/transpose;transpose | solution.py:703
  647.1 3.7 copy.107
  (347 shorter events, 132.2 us)
Async XLA Ops:
  7.2 523.1 %all-reduce.2.cloned.1.call-start = ((), (), s32[]{:S(2)}) async-start(), calls=%async_computation | async-start | bytes 18874368 | tf_op jit(solution)/shard_map/psum | solution.py:657
  41.1 13.8 %collective-permute-start.1 = (f32[2,2,2,56,256]{4,3,2,1,0:T(8,128)S(1)}, f32[2,2,2,56,256]{4,3,2,1,0:T(8,128)S(1)}, u32[]{:S(2)}, u32[]{:S(2)}) collective-permute-start(f32[2,2,2,56,256]{4,3,2,1,0:T(8,128)S(1)} %dynamic-slice_bitcast_fusion.8.refs_4_), channel_id=1, source_target_pairs={{0,4},{2,6},{4,0},{6,2},{8,12},{10,14},{12,8},{14,10},{16,20},{18,... | collective-permute-start | bytes 1376264 | tf_op jit(solution)/shard_map/ppermute | solution.py:417
  168.8 12.0 %collective-permute-start.8 = (f32[2,768,768]{2,1,0:T(8,128)}, f32[2,768,768]{2,1,0:T(8,128)}, u32[]{:S(2)}, u32[]{:S(2)}) collective-permute-start(f32[2,768,768]{2,1,0:T(8,128)} %get-tuple-element.95), channel_id=1, source_target_pairs={{0,2},{2,0},{4,6},{6,4},{8,10},{10,8},{12,14},{14,12},{16,18},{18,... | collective-permute-start | bytes 14155784 | tf_op jit(solution)/shard_map/ppermute | solution.py:417
  188.0 38.0 %collective-permute-start.9 = (f32[384,768]{1,0:T(8,128)}, f32[384,768]{1,0:T(8,128)}, u32[]{:S(2)}, u32[]{:S(2)}) collective-permute-start(f32[384,768]{1,0:T(8,128)} %dynamic-slice_bitcast_fusion.refs_8_), channel_id=1, source_target_pairs={{0,1},{1,0},{2,3},{3,2},{4,5},{5,4},{6,7},{7,6},{8,9},{9,8},{10,11... | collective-permute-start | bytes 3538952 | tf_op jit(solution)/shard_map/ppermute | solution.py:417
  191.4 36.1 %collective-permute-start.10 = (f32[384,768]{1,0:T(8,128)S(1)}, f32[384,768]{1,0:T(8,128)}, u32[]{:S(2)}, u32[]{:S(2)}) collective-permute-start(f32[384,768]{1,0:T(8,128)S(1)} %bitcast.352), channel_id=1, source_target_pairs={{0,4},{2,6},{4,0},{6,2},{8,12},{10,14},{12,8},{14,10},{16,20},{18,... | collective-permute-start | bytes 3538952 | tf_op jit(solution)/shard_map/ppermute | solution.py:417
  230.5 29.4 %collective-permute-start.14 = (f32[192,768]{1,0:T(8,128)S(1)}, f32[192,768]{1,0:T(8,128)}, u32[]{:S(2)}, u32[]{:S(2)}) collective-permute-start(f32[192,768]{1,0:T(8,128)S(1)} %get-tuple-element.209.refs_9_), channel_id=1, source_target_pairs={{0,1},{1,0},{2,3},{3,2},{4,5},{5,4},{6,7},{7,6},{8,9},{9,8},{10,11... | collective-permute-start | bytes 1769480 | tf_op jit(solution)/shard_map/ppermute | solution.py:417
  231.1 30.1 %collective-permute-start.13 = (f32[192,768]{1,0:T(8,128)S(1)}, f32[192,768]{1,0:T(8,128)}, u32[]{:S(2)}, u32[]{:S(2)}) collective-permute-start(f32[192,768]{1,0:T(8,128)S(1)} %get-tuple-element.210.refs_8_), channel_id=1, source_target_pairs={{0,4},{2,6},{4,0},{6,2},{8,12},{10,14},{12,8},{14,10},{16,20},{18,... | collective-permute-start | bytes 1769480 | tf_op jit(solution)/shard_map/ppermute | solution.py:417
  259.3 21.2 %collective-permute-start.17 = (f32[11,768]{1,0:T(8,128)S(1)}, f32[11,768]{1,0:T(8,128)}, u32[]{:S(2)}, u32[]{:S(2)}) collective-permute-start(f32[11,768]{1,0:T(8,128)S(1)} %pad_maximum_fusion.22.refs_4_), channel_id=1, source_target_pairs={{0,2},{2,0},{4,6},{6,4},{8,10},{10,8},{12,14},{14,12},{16,18},{18,... | collective-permute-start | bytes 101384 | tf_op jit(solution)/shard_map/ppermute | solution.py:417
  263.4 19.9 %collective-permute-start.16 = (f32[2,96,768]{2,1,0:T(8,128)}, f32[2,96,768]{2,1,0:T(8,128)}, u32[]{:S(2)}, u32[]{:S(2)}) collective-permute-start(f32[2,96,768]{2,1,0:T(8,128)} %fusion.6.refs_3_), channel_id=1, source_target_pairs={{0,8},{2,10},{4,12},{6,14},{8,0},{10,2},{12,4},{14,6},{16,24},{18,... | collective-permute-start | bytes 1769480 | tf_op jit(solution)/shard_map/ppermute | solution.py:417
  267.7 17.5 %collective-permute-start.12 = (f32[2,2,2,56,256]{4,3,2,1,0:T(8,128)S(1)}, f32[2,2,2,56,256]{4,3,2,1,0:T(8,128)}, u32[]{:S(2)}, u32[]{:S(2)}) collective-permute-start(f32[2,2,2,56,256]{4,3,2,1,0:T(8,128)S(1)} %dynamic-slice_bitcast_fusion.7.refs_2_), channel_id=1, source_target_pairs={{0,4},{2,6},{4,0},{6,2},{8,12},{10,14},{12,8},{14,10},{16,20},{18,... | collective-permute-start | bytes 1376264 | tf_op jit(solution)/shard_map/ppermute | solution.py:417
  298.1 340.4 %all-gather.3.cloned.1.call-start = ((), (), s32[]{:S(2)}) async-start(), calls=%async_computation.1 | async-start | bytes 9732096 | tf_op jit(solution)/shard_map/all_gather | solution.py:513
  299.0 21.7 %collective-permute-start.58 = (f32[2,48,768]{2,1,0:T(8,128)S(1)}, f32[2,48,768]{2,1,0:T(8,128)S(1)}, u32[]{:S(2)}, u32[]{:S(2)}) collective-permute-start(f32[2,48,768]{2,1,0:T(8,128)S(1)} %copy-done.24), channel_id=1, source_target_pairs={{0,16},{2,18},{4,20},{6,22},{8,24},{10,26},{12,28},{14,30},{16,0},... | collective-permute-start | bytes 884744 | tf_op jit(solution)/shard_map/ppermute | solution.py:417
  303.8 18.7 %collective-permute-start.15 = (f32[2,2,56,256]{3,2,1,0:T(8,128)S(1)}, f32[2,2,56,256]{3,2,1,0:T(8,128)S(1)}, u32[]{:S(2)}, u32[]{:S(2)}) collective-permute-start(f32[2,2,56,256]{3,2,1,0:T(8,128)S(1)} %copy-done.27), channel_id=1, source_target_pairs={{0,8},{2,10},{4,12},{6,14},{8,0},{10,2},{12,4},{14,6},{16,24},{18,... | collective-permute-start | bytes 688136 | tf_op jit(solution)/shard_map/ppermute | solution.py:417
  332.5 38.1 %collective-permute-start.23 = (f32[2,384,768]{2,1,0:T(8,128)}, f32[2,384,768]{2,1,0:T(8,128)S(1)}, u32[]{:S(2)}, u32[]{:S(2)}) collective-permute-start(f32[2,384,768]{2,1,0:T(8,128)} %get-tuple-element.119), channel_id=1, source_target_pairs={{0,2},{2,0},{4,6},{6,4},{8,10},{10,8},{12,14},{14,12},{16,18},{18,... | collective-permute-start | bytes 7077896 | tf_op jit(solution)/shard_map/ppermute | solution.py:417
  332.5 11.8 %collective-permute-start.18 = (f32[2,56,256]{2,1,0:T(8,128)S(1)}, f32[2,56,256]{2,1,0:T(8,128)S(1)}, u32[]{:S(2)}, u32[]{:S(2)}) collective-permute-start(f32[2,56,256]{2,1,0:T(8,128)S(1)} %copy-done.29), channel_id=1, source_target_pairs={{0,16},{2,18},{4,20},{6,22},{8,24},{10,26},{12,28},{14,30},{16,0},... | collective-permute-start | bytes 344072 | tf_op jit(solution)/shard_map/ppermute | solution.py:417
  332.6 11.8 %collective-permute-start.20 = (f32[11,768]{1,0:T(8,128)S(1)}, f32[11,768]{1,0:T(8,128)S(1)}, u32[]{:S(2)}, u32[]{:S(2)}) collective-permute-start(f32[11,768]{1,0:T(8,128)S(1)} %copy-done.33), channel_id=1, source_target_pairs={{0,4},{2,6},{4,0},{6,2},{8,12},{10,14},{12,8},{14,10},{16,20},{18,... | collective-permute-start | bytes 101384 | tf_op jit(solution)/shard_map/ppermute | solution.py:417
  344.3 10.8 %collective-permute-start.21 = (f32[2,56,256]{2,1,0:T(8,128)S(1)}, f32[2,56,256]{2,1,0:T(8,128)S(1)}, u32[]{:S(2)}, u32[]{:S(2)}) collective-permute-start(f32[2,56,256]{2,1,0:T(8,128)S(1)} %bitcast_add_fusion.23.refs_5_), channel_id=1, source_target_pairs={{0,16},{2,18},{4,20},{6,22},{8,24},{10,26},{12,28},{14,30},{16,0},... | collective-permute-start | bytes 344072 | tf_op jit(solution)/shard_map/ppermute | solution.py:417
  356.0 13.5 %collective-permute-start.22 = (f32[2,2,56,256]{3,2,1,0:T(8,128)S(1)}, f32[2,2,56,256]{3,2,1,0:T(8,128)S(1)}, u32[]{:S(2)}, u32[]{:S(2)}) collective-permute-start(f32[2,2,56,256]{3,2,1,0:T(8,128)S(1)} %pad_maximum_fusion.21), channel_id=1, source_target_pairs={{0,8},{2,10},{4,12},{6,14},{8,0},{10,2},{12,4},{14,6},{16,24},{18,... | collective-permute-start | bytes 688136 | tf_op jit(solution)/shard_map/ppermute | solution.py:417
  357.3 17.5 %collective-permute-start.24 = (f32[11,768]{1,0:T(8,128)S(1)}, f32[11,768]{1,0:T(8,128)S(1)}, u32[]{:S(2)}, u32[]{:S(2)}) collective-permute-start(f32[11,768]{1,0:T(8,128)S(1)} %copy-done.32), channel_id=1, source_target_pairs={{0,8},{2,10},{4,12},{6,14},{8,0},{10,2},{12,4},{14,6},{16,24},{18,... | collective-permute-start | bytes 101384 | tf_op jit(solution)/shard_map/ppermute | solution.py:417
  369.6 18.3 %collective-permute-start.25 = (f32[2,2,2,56,256]{4,3,2,1,0:T(8,128)S(1)}, f32[2,2,2,56,256]{4,3,2,1,0:T(8,128)}, u32[]{:S(2)}, u32[]{:S(2)}) collective-permute-start(f32[2,2,2,56,256]{4,3,2,1,0:T(8,128)S(1)} %pad_maximum_fusion.15.refs_3_), channel_id=1, source_target_pairs={{0,4},{2,6},{4,0},{6,2},{8,12},{10,14},{12,8},{14,10},{16,20},{18,... | collective-permute-start | bytes 1376264 | tf_op jit(solution)/shard_map/ppermute | solution.py:417
  373.6 25.8 %collective-permute-start.28 = (f32[192,768]{1,0:T(8,128)S(1)}, f32[192,768]{1,0:T(8,128)}, u32[]{:S(2)}, u32[]{:S(2)}) collective-permute-start(f32[192,768]{1,0:T(8,128)S(1)} %bitcast.381), channel_id=1, source_target_pairs={{0,4},{2,6},{4,0},{6,2},{8,12},{10,14},{12,8},{14,10},{16,20},{18,... | collective-permute-start | bytes 1769480 | tf_op jit(solution)/shard_map/ppermute | solution.py:417
  376.1 26.6 %collective-permute-start.27 = (f32[192,768]{1,0:T(8,128)S(1)}, f32[192,768]{1,0:T(8,128)}, u32[]{:S(2)}, u32[]{:S(2)}) collective-permute-start(f32[192,768]{1,0:T(8,128)S(1)} %dynamic-slice_bitcast_fusion.4.refs_4_), channel_id=1, source_target_pairs={{0,1},{1,0},{2,3},{3,2},{4,5},{5,4},{6,7},{7,6},{8,9},{9,8},{10,11... | collective-permute-start | bytes 1769480 | tf_op jit(solution)/shard_map/ppermute | solution.py:417
  390.9 24.0 %collective-permute-start.26 = (f32[2,2,2,2,56,256]{5,4,3,2,1,0:T(8,128)}, f32[2,2,2,2,56,256]{5,4,3,2,1,0:T(8,128)}, u32[]{:S(2)}, u32[]{:S(2)}) collective-permute-start(f32[2,2,2,2,56,256]{5,4,3,2,1,0:T(8,128)} %pad_maximum_fusion.9), channel_id=1, source_target_pairs={{0,2},{2,0},{4,6},{6,4},{8,10},{10,8},{12,14},{14,12},{16,18},{18,... | collective-permute-start | bytes 2752520 | tf_op jit(solution)/shard_map/ppermute | solution.py:417
  445.8 45.0 %collective-permute-start.36 = (f32[2,384,768]{2,1,0:T(8,128)}, f32[2,384,768]{2,1,0:T(8,128)S(1)}, u32[]{:S(2)}, u32[]{:S(2)}) collective-permute-start(f32[2,384,768]{2,1,0:T(8,128)} %get-tuple-element.132), channel_id=1, source_target_pairs={{0,2},{2,0},{4,6},{6,4},{8,10},{10,8},{12,14},{14,12},{16,18},{18,... | collective-permute-start | bytes 7077896 | tf_op jit(solution)/shard_map/ppermute | solution.py:417
  445.8 19.8 %collective-permute-start.31 = (f32[2,48,768]{2,1,0:T(8,128)S(1)}, f32[2,48,768]{2,1,0:T(8,128)}, u32[]{:S(2)}, u32[]{:S(2)}) collective-permute-start(f32[2,48,768]{2,1,0:T(8,128)S(1)} %copy-done.23), channel_id=1, source_target_pairs={{0,8},{2,10},{4,12},{6,14},{8,0},{10,2},{12,4},{14,6},{16,24},{18,... | collective-permute-start | bytes 884744 | tf_op jit(solution)/shard_map/ppermute | solution.py:417
  447.3 33.5 %collective-permute-start.59 = (f32[11,768]{1,0:T(8,128)S(1)}, f32[11,768]{1,0:T(8,128)S(1)}, u32[]{:S(2)}, u32[]{:S(2)}) collective-permute-start(f32[11,768]{1,0:T(8,128)S(1)} %copy-done.30), channel_id=1, source_target_pairs={{0,16},{2,18},{4,20},{6,22},{8,24},{10,26},{12,28},{14,30},{16,0},... | collective-permute-start | bytes 101384 | tf_op jit(solution)/shard_map/ppermute | solution.py:417
  448.0 18.7 %collective-permute-start.32 = (f32[2,768]{1,0:T(2,128)S(1)}, f32[2,768]{1,0:T(2,128)S(1)}, u32[]{:S(2)}, u32[]{:S(2)}) collective-permute-start(f32[2,768]{1,0:T(2,128)S(1)} %copy-done.41), channel_id=1, source_target_pairs={{0,2},{2,0},{4,6},{6,4},{8,10},{10,8},{12,14},{14,12},{16,18},{18,... | collective-permute-start | bytes 18440 | tf_op jit(solution)/shard_map/ppermute | solution.py:417
  466.6 11.2 %collective-permute-start.33 = (f32[2,24,768]{2,1,0:T(8,128)S(1)}, f32[2,24,768]{2,1,0:T(8,128)S(1)}, u32[]{:S(2)}, u32[]{:S(2)}) collective-permute-start(f32[2,24,768]{2,1,0:T(8,128)S(1)} %dynamic-slice_bitcast_fusion.17.refs_5_), channel_id=1, source_target_pairs={{0,16},{2,18},{4,20},{6,22},{8,24},{10,26},{12,28},{14,30},{16,0},... | collective-permute-start | bytes 442376 | tf_op jit(solution)/shard_map/ppermute | solution.py:417
  477.9 12.8 %collective-permute-start.34 = (f32[2,24,768]{2,1,0:T(8,128)S(1)}, f32[2,24,768]{2,1,0:T(8,128)S(1)}, u32[]{:S(2)}, u32[]{:S(2)}) collective-permute-start(f32[2,24,768]{2,1,0:T(8,128)S(1)} %fusion.20), channel_id=1, source_target_pairs={{0,16},{2,18},{4,20},{6,22},{8,24},{10,26},{12,28},{14,30},{16,0},... | collective-permute-start | bytes 442376 | tf_op jit(solution)/shard_map/ppermute | solution.py:417
  482.2 13.0 %collective-permute-start.41 = (f32[2,768]{1,0:T(2,128)S(1)}, f32[2,768]{1,0:T(2,128)}, u32[]{:S(2)}, u32[]{:S(2)}) collective-permute-start(f32[2,768]{1,0:T(2,128)S(1)} %copy-done.37), channel_id=1, source_target_pairs={{0,1},{1,0},{2,3},{3,2},{4,5},{5,4},{6,7},{7,6},{8,9},{9,8},{10,11... | collective-permute-start | bytes 18440 | tf_op jit(solution)/shard_map/ppermute | solution.py:417
  490.8 15.5 %collective-permute-start.35 = (f32[2,48,768]{2,1,0:T(8,128)S(1)}, f32[2,48,768]{2,1,0:T(8,128)S(1)}, u32[]{:S(2)}, u32[]{:S(2)}) collective-permute-start(f32[2,48,768]{2,1,0:T(8,128)S(1)} %bitcast.403), channel_id=1, source_target_pairs={{0,8},{2,10},{4,12},{6,14},{8,0},{10,2},{12,4},{14,6},{16,24},{18,... | collective-permute-start | bytes 884744 | tf_op jit(solution)/shard_map/ppermute | solution.py:417
  494.0 18.7 %collective-permute-start.39 = (f32[192,768]{1,0:T(8,128)}, f32[192,768]{1,0:T(8,128)S(1)}, u32[]{:S(2)}, u32[]{:S(2)}) collective-permute-start(f32[192,768]{1,0:T(8,128)} %bitcast.115), channel_id=1, source_target_pairs={{0,4},{2,6},{4,0},{6,2},{8,12},{10,14},{12,8},{14,10},{16,20},{18,... | collective-permute-start | bytes 1769480 | tf_op jit(solution)/shard_map/ppermute | solution.py:417
  495.8 49.5 %collective-permute-start.60 = (f32[2,768]{1,0:T(2,128)S(1)}, f32[2,768]{1,0:T(2,128)S(1)}, u32[]{:S(2)}, u32[]{:S(2)}) collective-permute-start(f32[2,768]{1,0:T(2,128)S(1)} %add_add_fusion.8.refs_8_), channel_id=1, source_target_pairs={{0,4},{2,6},{4,0},{6,2},{8,12},{10,14},{12,8},{14,10},{16,20},{18,... | collective-permute-start | bytes 18440 | tf_op jit(solution)/shard_map/ppermute | solution.py:417
  496.8 17.8 %collective-permute-start.37 = (f32[192,768]{1,0:T(8,128)S(1)}, f32[192,768]{1,0:T(8,128)S(1)}, u32[]{:S(2)}, u32[]{:S(2)}) collective-permute-start(f32[192,768]{1,0:T(8,128)S(1)} %dynamic-slice_bitcast_fusion.3), channel_id=1, source_target_pairs={{0,1},{1,0},{2,3},{3,2},{4,5},{5,4},{6,7},{7,6},{8,9},{9,8},{10,11... | collective-permute-start | bytes 1769480 | tf_op jit(solution)/shard_map/ppermute | solution.py:417
  516.1 31.4 %collective-permute-start.55 = (f32[96,768]{1,0:T(8,128)S(1)}, f32[96,768]{1,0:T(8,128)S(1)}, u32[]{:S(2)}, u32[]{:S(2)}) collective-permute-start(f32[96,768]{1,0:T(8,128)S(1)} %bitcast.379), channel_id=1, source_target_pairs={{0,4},{2,6},{4,0},{6,2},{8,12},{10,14},{12,8},{14,10},{16,20},{18,... | collective-permute-start | bytes 884744 | tf_op jit(solution)/shard_map/ppermute | solution.py:417
  517.5 41.4 %collective-permute-start.42 = (f32[96,768]{1,0:T(8,128)}, f32[96,768]{1,0:T(8,128)S(1)}, u32[]{:S(2)}, u32[]{:S(2)}) collective-permute-start(f32[96,768]{1,0:T(8,128)} %bitcast.105.refs_6_), channel_id=1, source_target_pairs={{0,1},{1,0},{2,3},{3,2},{4,5},{5,4},{6,7},{7,6},{8,9},{9,8},{10,11... | collective-permute-start | bytes 884744 | tf_op jit(solution)/shard_map/ppermute | solution.py:417
  544.6 13.2 %collective-permute-start.45 = (f32[2,48,768]{2,1,0:T(8,128)S(1)}, f32[2,48,768]{2,1,0:T(8,128)S(1)}, u32[]{:S(2)}, u32[]{:S(2)}) collective-permute-start(f32[2,48,768]{2,1,0:T(8,128)S(1)} %copy-done.22), channel_id=1, source_target_pairs={{0,8},{2,10},{4,12},{6,14},{8,0},{10,2},{12,4},{14,6},{16,24},{18,... | collective-permute-start | bytes 884744 | tf_op jit(solution)/shard_map/ppermute | solution.py:417
  545.3 30.1 %collective-permute-start.61 = (f32[2,768]{1,0:T(2,128)S(1)}, f32[2,768]{1,0:T(2,128)S(1)}, u32[]{:S(2)}, u32[]{:S(2)}) collective-permute-start(f32[2,768]{1,0:T(2,128)S(1)} %add_add_fusion.7), channel_id=1, source_target_pairs={{0,8},{2,10},{4,12},{6,14},{8,0},{10,2},{12,4},{14,6},{16,24},{18,... | collective-permute-start | bytes 18440 | tf_op jit(solution)/shard_map/ppermute | solution.py:417
  548.5 58.1 %collective-permute-start.56 = (f32[192,768]{1,0:T(8,128)S(1)}, f32[192,768]{1,0:T(8,128)S(1)}, u32[]{:S(2)}, u32[]{:S(2)}) collective-permute-start(f32[192,768]{1,0:T(8,128)S(1)} %bitcast.383), channel_id=1, source_target_pairs={{0,1},{1,0},{2,3},{3,2},{4,5},{5,4},{6,7},{7,6},{8,9},{9,8},{10,11... | collective-permute-start | bytes 1769480 | tf_op jit(solution)/shard_map/ppermute | solution.py:417
  557.8 17.5 %collective-permute-start.46 = (f32[2,24,768]{2,1,0:T(8,128)S(1)}, f32[2,24,768]{2,1,0:T(8,128)S(1)}, u32[]{:S(2)}, u32[]{:S(2)}) collective-permute-start(f32[2,24,768]{2,1,0:T(8,128)S(1)} %dynamic-slice_bitcast_fusion.16), channel_id=1, source_target_pairs={{0,16},{2,18},{4,20},{6,22},{8,24},{10,26},{12,28},{14,30},{16,0},... | collective-permute-start | bytes 442376 | tf_op jit(solution)/shard_map/ppermute | solution.py:417
  560.7 57.2 %collective-permute-start.43 = (f32[192,768]{1,0:T(8,128)S(1)}, f32[192,768]{1,0:T(8,128)S(1)}, u32[]{:S(2)}, u32[]{:S(2)}) collective-permute-start(f32[192,768]{1,0:T(8,128)S(1)} %bitcast.411), channel_id=1, source_target_pairs={{0,4},{2,6},{4,0},{6,2},{8,12},{10,14},{12,8},{14,10},{16,20},{18,... | collective-permute-start | bytes 1769480 | tf_op jit(solution)/shard_map/ppermute | solution.py:417
  575.3 10.8 %collective-permute-start.47 = (f32[2,24,768]{2,1,0:T(8,128)S(1)}, f32[2,24,768]{2,1,0:T(8,128)S(1)}, u32[]{:S(2)}, u32[]{:S(2)}) collective-permute-start(f32[2,24,768]{2,1,0:T(8,128)S(1)} %fusion.21), channel_id=1, source_target_pairs={{0,16},{2,18},{4,20},{6,22},{8,24},{10,26},{12,28},{14,30},{16,0},... | collective-permute-start | bytes 442376 | tf_op jit(solution)/shard_map/ppermute | solution.py:417
  575.4 10.8 %collective-permute-start.62 = (f32[2,768]{1,0:T(2,128)S(1)}, f32[2,768]{1,0:T(2,128)S(1)}, u32[]{:S(2)}, u32[]{:S(2)}) collective-permute-start(f32[2,768]{1,0:T(2,128)S(1)} %add_add_fusion.6), channel_id=1, source_target_pairs={{0,16},{2,18},{4,20},{6,22},{8,24},{10,26},{12,28},{14,30},{16,0},... | collective-permute-start | bytes 18440 | tf_op jit(solution)/shard_map/ppermute | solution.py:417
  586.2 19.2 %collective-permute-start.48 = (f32[2,48,768]{2,1,0:T(8,128)S(1)}, f32[2,48,768]{2,1,0:T(8,128)S(1)}, u32[]{:S(2)}, u32[]{:S(2)}) collective-permute-start(f32[2,48,768]{2,1,0:T(8,128)S(1)} %bitcast.405), channel_id=1, source_target_pairs={{0,8},{2,10},{4,12},{6,14},{8,0},{10,2},{12,4},{14,6},{16,24},{18,... | collective-permute-start | bytes 884744 | tf_op jit(solution)/shard_map/ppermute | solution.py:417
  606.7 24.8 %collective-permute-start.57 = (f32[384,768]{1,0:T(8,128)S(1)}, f32[384,768]{1,0:T(8,128)S(1)}, u32[]{:S(2)}, u32[]{:S(2)}) collective-permute-start(f32[384,768]{1,0:T(8,128)S(1)} %bitcast.354), channel_id=1, source_target_pairs={{0,2},{2,0},{4,6},{6,4},{8,10},{10,8},{12,14},{14,12},{16,18},{18,... | collective-permute-start | bytes 3538952 | tf_op jit(solution)/shard_map/ppermute | solution.py:417
  615.3 13.5 %collective-permute-start.53 = (f32[192,768]{1,0:T(8,128)S(1)}, f32[192,768]{1,0:T(8,128)S(1)}, u32[]{:S(2)}, u32[]{:S(2)}) collective-permute-start(f32[192,768]{1,0:T(8,128)S(1)} %bitcast.412), channel_id=1, source_target_pairs={{0,4},{2,6},{4,0},{6,2},{8,12},{10,14},{12,8},{14,10},{16,20},{18,... | collective-permute-start | bytes 1769480 | tf_op jit(solution)/shard_map/ppermute | solution.py:417
  616.8 14.5 %collective-permute-start.50 = (f32[192,768]{1,0:T(8,128)S(1)}, f32[192,768]{1,0:T(8,128)S(1)}, u32[]{:S(2)}, u32[]{:S(2)}) collective-permute-start(f32[192,768]{1,0:T(8,128)S(1)} %bitcast.384), channel_id=1, source_target_pairs={{0,1},{1,0},{2,3},{3,2},{4,5},{5,4},{6,7},{7,6},{8,9},{9,8},{10,11... | collective-permute-start | bytes 1769480 | tf_op jit(solution)/shard_map/ppermute | solution.py:417
  618.1 15.1 %collective-permute-start.44 = (f32[384,768]{1,0:T(8,128)S(1)}, f32[384,768]{1,0:T(8,128)S(1)}, u32[]{:S(2)}, u32[]{:S(2)}) collective-permute-start(f32[384,768]{1,0:T(8,128)S(1)} %bitcast.355), channel_id=1, source_target_pairs={{0,2},{2,0},{4,6},{6,4},{8,10},{10,8},{12,14},{14,12},{16,18},{18,... | collective-permute-start | bytes 3538952 | tf_op jit(solution)/shard_map/ppermute | solution.py:417
  (66 other events, 449.0 us)
Sparse Core Ops, SparseCore 0:
  298.2 232.0 all-reduce.1
  533.6 99.8 all-gather.2
